TPU v7x, 256 devices: a whole 4x4x8 slice. The times are simulated.
256 devices in a mesh: rep: 2 (over z_hi), ctx: 128 (over x, y, z_lo, core).
Axes of the slice: x: 4, y: 4, z: 8 (z_hi: 2, z_lo: 4; z = z_hi * 4 + z_lo), core: 2. Of those that a mesh axis runs over, the one named last changes fastest.
Arguments:
- inputs: bfloat16 [2, 16384, 4096], P('rep', 'ctx'), may hold values from -6 to 6
- gate_li: bfloat16 [2, 16384, 4096], P('rep', 'ctx'), may hold values from -6 to 6
- gate_mr: bfloat16 [2, 16384, 4096], P('rep', 'ctx'), may hold values from -6 to 6
- cotangent: bfloat16 [2, 16384, 4096], P('rep', 'ctx'), may hold values from -6 to 6
- residues: float32 [128, 16], replicated, may hold values from -1.5 to 1.5
- rates: float32 [128, 16], replicated, may hold values from 1.2207031e-05 to 0.05
- taps: float32 [128, 128], replicated, may hold values from -0.5 to 0.5
Outputs:
- grad_inputs: bfloat16 [2, 16384, 4096], P('rep', 'ctx')
- grad_gate_li: bfloat16 [2, 16384, 4096], P('rep', 'ctx')
- grad_gate_mr: bfloat16 [2, 16384, 4096], P('rep', 'ctx')
- grad_residues: float32 [128, 16], replicated
- grad_taps: float32 [128, 128], replicated
All inputs are finite; a program needn't handle non-finite values.
Results may differ from a plain program's by a relative error of at most 0.0049.
Values may be sent and summed in bfloat16 or wider, within the bound.
No kernel may reach another device: no remote copies, remote signals or barrier semaphores. Data moves between devices by JAX's collectives and lax.ppermute only.
A program may use at most 320 MiB of HBM per device.

v0:
```python
import math

import jax
import jax.numpy as jnp
from jax import lax
from jax.sharding import PartitionSpec as P


def from_behind(block, axis, distance):
    devices = range(lax.axis_size(axis))
    route = [(i - distance, i) for i in devices if i - distance in devices]
    return lax.ppermute(block, axis, route)


def contract(form, left_op, right_op):
    return jnp.einsum(form, left_op, right_op, precision=lax.Precision.HIGHEST)


def diagonal_matrix(diag_vals, rows, cols):
    lead = diag_vals.shape[:-1]
    period = rows + cols
    reverse_vals = jnp.flip(diag_vals, -1)
    padded = jnp.concatenate([reverse_vals, jnp.zeros(lead + (1,), reverse_vals.dtype)], axis=-1)
    tiled = jnp.tile(padded, (1,) * len(lead) + (rows + 1,))
    window = tiled[..., rows - 1 : rows - 1 + rows * (period - 1)]
    return window.reshape(lead + (rows, period - 1))[..., :cols]


def li_matrix(kernel):
    block_len = kernel.shape[-1]
    lead = kernel.shape[:-1]
    diag_vals = jnp.concatenate([jnp.zeros(lead + (block_len - 1,), kernel.dtype), kernel], axis=-1)
    return diagonal_matrix(diag_vals, block_len, block_len)


def mr_matrix(tap_rows):
    block_len = tap_rows.shape[-1]
    lead = tap_rows.shape[:-1]
    diag_vals = jnp.concatenate(
        [
            jnp.zeros(lead + (block_len - 1,), tap_rows.dtype),
            tap_rows,
            jnp.zeros(lead + (block_len,), tap_rows.dtype),
        ],
        axis=-1,
    )
    return diagonal_matrix(diag_vals, block_len, 2 * block_len)


def mode_tables(rates_part, residues_part, block_len):
    steps_up = jnp.arange(block_len).astype(jnp.float32)
    lam_rows = jnp.exp(-rates_part[:, :, None] * steps_up)
    norm_factor = jnp.sqrt(-jnp.expm1(-2.0 * rates_part))
    weight = residues_part * norm_factor
    kernel = contract("gm,gmk->gk", weight, lam_rows)
    toeplitz = li_matrix(kernel)
    end_powers = jnp.exp(-rates_part[:, :, None] * (block_len - 1.0 - steps_up))
    starts = jnp.exp(-rates_part[:, :, None] * (steps_up + 1.0))
    decay_rate = jnp.exp(-rates_part * block_len)
    return (toeplitz, lam_rows, end_powers, starts, decay_rate, norm_factor, weight, kernel)


def link_states(earlier, later_one):
    return (earlier[0] * later_one[0], later_one[0] * earlier[1] + later_one[1])


def nothing_before(total_a, total_b):
    return jnp.zeros_like(total_b)


def chain_states(decay_rate, block_ends, outside):
    nblocks = block_ends.shape[0]
    factor = jnp.broadcast_to(
        decay_rate.T[None, :, :, None], (nblocks,) + decay_rate.T.shape + (1,)
    )
    inc_a, inc_b = lax.associative_scan(link_states, (factor, block_ends), axis=0)
    before_a = jnp.concatenate([jnp.ones_like(inc_a[:1]), inc_a[:-1]], axis=0)
    before_b = jnp.concatenate([jnp.zeros_like(inc_b[:1]), inc_b[:-1]], axis=0)
    from_device = outside(inc_a[-1], inc_b[-1])
    return before_b + before_a * from_device[None]


def long_filter(seq_blocks, tables, outside):
    toeplitz, lam_rows, end_powers, starts, decay_rate, norm_factor, weight, kernel = tables
    local_part = contract("gtu,nugc->ntgc", toeplitz, seq_blocks)
    block_ends = contract("gmu,nugc->nmgc", end_powers, seq_blocks)
    entering = chain_states(decay_rate, block_ends, outside)
    carried = contract("gmt,nmgc->ntgc", starts * weight[:, :, None], entering)
    return (local_part + carried, entering)


def residue_grad(cot_blocks, seq_blocks, entering, tables):
    toeplitz, lam_rows, end_powers, starts, decay_rate, norm_factor, weight, kernel = tables
    cross_terms = contract("ntgc,nugc->gtu", cot_blocks, seq_blocks)
    unused_value, pull_back = jax.vjp(li_matrix, kernel)
    lag_totals = pull_back(cross_terms)[0]
    from_before = contract("gmt,ntgc->nmgc", starts, cot_blocks)
    first_part = jnp.sum(from_before * entering, axis=(0, 3)).T
    return norm_factor * (first_part + contract("gk,gmk->gm", lag_totals, lam_rows))


def make_pairs(extended, block_len):
    nblocks = extended.shape[0] // block_len - 1
    split_rows = extended.reshape((nblocks + 1, block_len) + extended.shape[1:])
    return jnp.concatenate([split_rows[:-1], split_rows[1:]], axis=1)


def on_device(inputs, gate_li, gate_mr, cotangent, residues, rates, taps):
    row_count = inputs.shape[1]
    width_all = inputs.shape[2]
    block_len = taps.shape[1]
    groups_all = residues.shape[0]
    group_size = width_all // groups_all
    blocks_dev = row_count // block_len
    gate_one = gate_li[0].astype(jnp.float32)
    gate_two = gate_mr[0].astype(jnp.float32)
    cot_out = cotangent[0].astype(jnp.float32)
    ctx_count = lax.axis_size("ctx")
    local_width = width_all // ctx_count
    members = min(group_size, local_width)
    owned_groups = local_width // members
    first_group = lax.axis_index("ctx") * local_width // group_size
    rates_part = lax.dynamic_slice_in_dim(rates, first_group, owned_groups, 0)
    residues_part = lax.dynamic_slice_in_dim(residues, first_group, owned_groups, 0)
    tables = mode_tables(rates_part, residues_part, block_len)
    spread = lax.all_to_all(inputs, "ctx", split_axis=2, concat_axis=1, tiled=True)
    seq_rows = spread.shape[1]
    seq_blocks = (
        spread[0]
        .astype(jnp.float32)
        .reshape(seq_rows // block_len, block_len, owned_groups, members)
    )
    values_ch, entering = long_filter(seq_blocks, tables, nothing_before)
    values = lax.all_to_all(
        values_ch.reshape(1, seq_rows, local_width), "ctx", split_axis=1, concat_axis=2, tiled=True
    )[0]
    mixer_in = (gate_one * values).astype(jnp.bfloat16)
    before = from_behind(mixer_in, "ctx", 1)
    extended = jnp.concatenate([before, mixer_in], axis=0)
    extended = extended.astype(jnp.float32).reshape(row_count + block_len, groups_all, group_size)
    in_pairs = make_pairs(extended, block_len)
    forward_taps = mr_matrix(taps)
    mixed_out = contract("gts,nsgc->ntgc", forward_taps, in_pairs).reshape(row_count, width_all)
    grad_gate_mr = (cot_out * mixed_out).astype(jnp.bfloat16)
    scaled = (cot_out * gate_two).astype(jnp.bfloat16)
    rows_after = from_behind(scaled, "ctx", -1)
    ext_cot = jnp.concatenate([scaled, rows_after], axis=0)
    ext_cot = ext_cot.astype(jnp.float32).reshape(row_count + block_len, groups_all, group_size)
    cot_pairs = jnp.flip(make_pairs(ext_cot, block_len), 1)
    grad_mixer = jnp.flip(contract("gts,nsgc->ntgc", forward_taps, cot_pairs), 1).reshape(
        row_count, width_all
    )
    scaled_blocks = scaled.astype(jnp.float32).reshape(
        blocks_dev, block_len, groups_all, group_size
    )
    cross_taps = contract("ntgc,nsgc->gts", scaled_blocks, in_pairs)
    unused_matrix, tap_pull = jax.vjp(mr_matrix, taps)
    grad_taps = tap_pull(cross_taps)[0]
    grad_gate_li = (grad_mixer * values).astype(jnp.bfloat16)
    cot_li = grad_mixer * gate_one
    cot_spread = lax.all_to_all(cot_li[None], "ctx", split_axis=2, concat_axis=1, tiled=True)[0]
    cot_blocks = cot_spread.reshape(seq_rows // block_len, block_len, owned_groups, members)
    flipped = jnp.flip(cot_blocks, (0, 1))
    back_blk, unused_states = long_filter(flipped, tables, nothing_before)
    back_ch = jnp.flip(back_blk, (0, 1)).reshape(1, seq_rows, local_width)
    grad_inputs = lax.all_to_all(
        back_ch.astype(jnp.bfloat16), "ctx", split_axis=1, concat_axis=2, tiled=True
    ).astype(back_ch.dtype)[0]
    part_res = residue_grad(cot_blocks, seq_blocks, entering, tables)
    grad_res = lax.dynamic_update_slice_in_dim(jnp.zeros_like(residues), part_res, first_group, 0)
    summed = lax.psum((grad_res, grad_taps), ("rep", "ctx"))
    grad_scale = 1.0 / math.sqrt(lax.axis_size("rep") * seq_rows)
    return (
        grad_inputs.astype(jnp.bfloat16)[None],
        grad_gate_li[None],
        grad_gate_mr[None],
        summed[0] * grad_scale,
        summed[1] * grad_scale,
    )


def solution(mesh):
    in_specs = (
        P("rep", "ctx", None),
        P("rep", "ctx", None),
        P("rep", "ctx", None),
        P("rep", "ctx", None),
        P(),
        P(),
        P(),
    )
    out_specs = (P("rep", "ctx", None), P("rep", "ctx", None), P("rep", "ctx", None), P(), P())
    return jax.shard_map(
        on_device, mesh=mesh, in_specs=in_specs, out_specs=out_specs, check_vma=False
    )
```

profile of v0, /device:TPU:1, one launch (start us, length us, event | category | flops | bytes accessed | tf_op | source)
XLA Modules:
  0.0 1296.1 jit_solution(12394947973667064074)
XLA Ops:
  7.2 5.0 copy.187
  12.7 22.3 %reduce.7 = bf16[4096,128]{1,0:T(8,128)(2,1)S(1)} reduce(bf16[4096,1,128]{2,1,0:T(2,128)(2,1)S(1)} %bitcast.245, bf16[]{:T(256)} %broadcast.484), dimensions={1}, to_apply=%bitcast.210.reduce_sub_computation | reduce | bytes 2097154
  36.2 14.1 %all-to-all-start.2 = ((bf16[128,2,2048]{2,1,0:T(2,128)(2,1)}), bf16[128,2,2048]{2,1,0:T(2,128)(2,1)S(1)}, u32[]{:S(2)}, u32[]{:S(2)}) async-start(bf16[128,2,2048]{2,1,0:T(2,128)(2,1)} %reshape.684), calls=%async_computation.2 | async-start | bytes 2097152 | tf_op jit(solution)/shard_map/all_to_all | solution.py:126
  56.7 23.0 %all-to-all-done.2 = bf16[128,2,2048]{2,1,0:T(2,128)(2,1)S(1)} async-done(((bf16[128,2,2048]{2,1,0:T(2,128)(2,1)}), bf16[128,2,2048]{2,1,0:T(2,128)(2,1)S(1)}, u32[]{:S(2)}, u32[]{:S(2)}) %all-to-all-start.2) | async-done | bytes 1048608 | tf_op jit(solution)/shard_map/all_to_all | solution.py:126
  88.0 22.4 %pad.354 = f32[128,16,1,32]{3,1,0,2:T(8,128)S(1)} pad(f32[64,16,1,32]{3,1,0,2:T(8,128)} %add.351, f32[]{:T(128)} %constant.15.clone.1), padding=1_0_1x0_0_0x0_0_0x0_0_0 | pad | bytes 393220
  114.4 2.4 fusion.9
  116.8 1.9 copy.192
  118.7 13.9 %copy.193 = f32[1,16384,32]{2,0,1:T(1,128)} copy(f32[1,16384,32]{1,0,2:T(1,128)S(1)} %bitcast.242) | data formatting | bytes 4194304 | tf_op jit(solution)/shard_map/reshape | solution.py:135
  133.1 74.7 %reduce.8 = f32[16384,32]{1,0:T(8,128)} reduce(f32[16384,1,32]{2,1,0:T(1,128)} %bitcast.224, f32[]{:T(128)} %broadcast.485), dimensions={1}, to_apply=%bitcast.212.reduce_sub_computation | reduce | bytes 4194308
  207.8 7.8 reshape.686
  215.6 8.0 all-to-all-start.3
  224.3 50.9 %all-to-all-done.3 = f32[128,1,4096]{2,1,0:T(1,128)} async-done(((f32[128,1,4096]{2,1,0:T(1,128)}), f32[128,1,4096]{2,1,0:T(1,128)}, u32[]{:S(2)}, u32[]{:S(2)}) %all-to-all-start.3) | async-done | bytes 2097184 | tf_op jit(solution)/shard_map/all_to_all | solution.py:134
  275.1 7.3 reduce.9
  282.5 15.5 %reshape.687 = f32[16384,1,32]{2,1,0:T(1,128)} reshape(f32[128,4096]{1,0:T(8,128)S(1)} %reduce.9) | data formatting | bytes 4194304
  297.9 19.4 %copy.194 = f32[1,16384,32]{1,0,2:T(1,128)} copy(f32[1,16384,32]{2,0,1:T(1,128)} %bitcast.225) | data formatting | bytes 4194304 | tf_op jit(solution)/shard_map/all_to_all | solution.py:134
  317.4 2.8 copy.195
  321.4 1.9 collective-permute-start.1
  324.5 11.5 tile.20
  336.0 17.0 %slice.430 = f32[128,49024]{0,1:T(8,128)} slice(f32[128,49536]{0,1:T(8,128)} %bitcast.223), slice={[0:128], [127:49151]} | slice | bytes 50200576 | tf_op jit(solution)/shard_map/slice | solution.py:25
  353.0 22.3 %reshape.679 = f32[128,128,383]{0,2,1:T(8,128)} reshape(f32[128,49024]{0,1:T(8,128)} %slice.430) | data formatting | bytes 50200576 | tf_op jit(solution)/shard_map/reshape | solution.py:26
  375.3 11.6 slice.431
  387.0 17.7 %copy.208 = f32[128,128,256]{2,1,0:T(8,128)} copy(f32[128,128,256]{0,2,1:T(8,128)} %slice.431) | data formatting | bytes 33554432
  404.7 2.3 copy.174
  406.9 2.3 copy.175
  411.3 21.5 %fusion.3 = f32[128,32,128]{2,1,0:T(8,128)S(1)} fusion(f32[128,128,256]{2,1,0:T(8,128)} %copy.208, f32[1,128,128,32]{1,3,2,0:T(8,128)S(1)} %bitcast.234, f32[1,128,128,32]{1,3,2,0:T(8,128)S(1)} %bitcast.232), kind=kOutput, calls=%fused_computation.5 | convolution fusion | flops 1611661312 | bytes 23068672 | tf_op jit(solution)/shard_map/gts,nsgc->ntgc/dot_general | solution.py:16
  434.2 3.4 collective-permute-start
  437.6 12.7 collective-permute-done
  450.9 2.5 pad_maximum_fusion
  453.4 7.4 rev.27
  460.8 22.1 %fusion.12 = f32[1,128,128,32]{1,3,2,0:T(8,128)} fusion(f32[128,128,256]{2,1,0:T(8,128)} %copy.208, f32[1,256,128,32]{1,3,2,0:T(8,128)} %rev.27), kind=kOutput, calls=%fused_computation.23 | convolution fusion | flops 1610612736 | bytes 23068672 | tf_op jit(solution)/shard_map/gts,nsgc->ntgc/dot_general | solution.py:16
  482.9 4.2 rev.29
  487.1 3.1 fusion.8
  490.2 67.2 %all_to_all.63 = f32[1,128,4096]{1,0,2:T(1,128)S(1)} all-to-all(f32[1,128,4096]{1,0,2:T(1,128)S(1)} %bitcast.246), channel_id=1, replica_groups=mesh['rep'=2,'ctx'=128] {'ctx'}, dimensions={2} | all-to-all | bytes 4194304 | tf_op jit(solution)/shard_map/all_to_all | solution.py:161
  557.3 2.3 rev.30
  559.7 9.8 convolution_bitcast_fusion.1
  579.0 3.2 pad.165
  582.2 3.2 pad.166
  588.5 2.8 pad.168
  592.8 4.7 pad.167
  600.2 8.5 pad.170
  612.2 15.1 %pad.172 = f32[64,16,1,32]{3,1,0,2:T(8,128)} pad(f32[32,16,1,32]{3,1,0,2:T(8,128)} %add.316, f32[]{:T(128)} %constant.15.clone.1), padding=1_0_1x0_0_0x0_0_0x0_0_0 | pad | bytes 196612 | tf_op jit(solution)/shard_map/pad | solution.py:76
  628.3 10.3 pad.171
  641.0 20.1 %pad.258 = f32[127,16,1,32]{3,1,0,2:T(8,128)} pad(f32[64,16,1,32]{3,1,0,2:T(8,128)S(1)} %pad_maximum_fusion.1, f32[]{:T(128)} %constant.15.clone.1), padding=0_0_1x0_0_0x0_0_0x0_0_0 | pad | bytes 391172 | tf_op jit(solution)/shard_map/slice | solution.py:78
  661.1 22.4 %pad.352 = f32[128,16,1,32]{3,1,0,2:T(8,128)S(1)} pad(f32[64,16,1,32]{3,1,0,2:T(8,128)} %add.318, f32[]{:T(128)} %constant.15.clone.1), padding=1_0_1x0_0_0x0_0_0x0_0_0 | pad | bytes 393220
  685.8 3.5 fusion.47
  689.2 3.3 add_bitcast_fusion
  692.6 11.4 rev.32
  705.5 12.8 copy.184
  718.3 91.1 %reduce.10 = bf16[16384,32]{1,0:T(8,128)(2,1)} reduce(bf16[16384,1,32]{2,1,0:T(2,128)(2,1)} %bitcast.226, bf16[]{:T(256)} %broadcast.484), dimensions={1}, to_apply=%bitcast.208.reduce_sub_computation | reduce | bytes 2097154
  809.4 7.3 reshape.682
  816.7 7.5 all-to-all-start.1
  824.3 8.8 fusion.2
  833.2 9.1 pad.205
  842.3 26.8 %reshape.667 = f32[128,49024]{1,0:T(8,128)} reshape(f32[128,128,383]{2,1,0:T(8,128)} %pad.205) | data formatting | bytes 50200576 | tf_op jit(solution)/shard_map/transpose(jvp())/reshape | solution.py:26
  869.1 24.7 %copy.212 = f32[128,49024]{0,1:T(8,128)} copy(f32[128,49024]{1,0:T(8,128)} %reshape.667) | data formatting | bytes 50200576
  893.8 19.2 %pad.206.clone = f32[128,49536]{0,1:T(8,128)} pad(f32[128,49024]{0,1:T(8,128)} %copy.212, f32[]{:T(128)} %constant.15.clone.1), padding=0_0x127_385 | pad | bytes 50462724 | tf_op jit(solution)/shard_map/transpose(jvp())/pad | solution.py:25
  913.0 9.3 reduce_sum.32
  922.9 2.4 copy.202
  925.3 236.1 %all-reduce.53.cloned.1.call-done = f32[128,128]{0,1:T(8,128)} async-done(((f32[128,128]{0,1:T(8,128)}), f32[128,128]{0,1:T(8,128)}) %all-reduce.53.cloned.1.call-update) | async-done | bytes 65552 | tf_op jit(solution)/shard_map/psum | solution.py:171
  1163.0 2.4 copy.201
  1168.3 9.6 fusion.18
  1178.3 74.4 %psum.14 = f32[128,16]{0,1:T(8,128)S(1)} all-reduce(f32[128,16]{0,1:T(8,128)S(1)} %dynamic_update_slice.3), channel_id=1, replica_groups=mesh['rep'=2,'ctx'=128] {'rep','ctx'}, use_global_device_ids=true, to_apply=%region_2.3 | all-reduce | flops 2048 | bytes 16384 | tf_op jit(solution)/shard_map/psum | solution.py:171
  1253.3 18.4 %reshape.683 = bf16[16384,1,32]{2,1,0:T(2,128)(2,1)} reshape(bf16[128,2,2048]{2,1,0:T(2,128)(2,1)} %all-to-all-done.1) | data formatting | bytes 2097152
  1271.7 15.1 %copy.185 = bf16[1,16384,32]{1,2,0:T(8,128)(2,1)S(1)} copy(bf16[1,16384,32]{2,0,1:T(2,128)(2,1)} %bitcast.227) | data formatting | bytes 2097152 | tf_op jit(solution)/shard_map/all_to_all | solution.py:166
  (273 shorter events, 62.9 us)
Async XLA Ops:
  35.0 15.3 %copy-start.32 = (f32[128,16]{0,1:T(8,128)S(1)}, f32[128,16]{0,1:T(8,128)}, u32[]{:S(2)}) copy-start(f32[128,16]{0,1:T(8,128)} %param.12) | copy-start | bytes 24580
  35.0 15.3 %copy-start.33 = (f32[128,16]{0,1:T(8,128)S(1)}, f32[128,16]{0,1:T(8,128)}, u32[]{:S(2)}) copy-start(f32[128,16]{0,1:T(8,128)} %param.11) | copy-start | bytes 24580
  36.2 43.5 %all-to-all-start.2 = ((bf16[128,2,2048]{2,1,0:T(2,128)(2,1)}), bf16[128,2,2048]{2,1,0:T(2,128)(2,1)S(1)}, u32[]{:S(2)}, u32[]{:S(2)}) async-start(bf16[128,2,2048]{2,1,0:T(2,128)(2,1)} %reshape.684), calls=%async_computation.2 | async-start | bytes 2097152 | tf_op jit(solution)/shard_map/all_to_all | solution.py:126
  50.5 4.1 copy-start.42
  50.5 519.0 %copy-start.20 = (f32[1,16]{1,0:T(1,128)}, f32[1,16]{1,0:T(1,128)S(1)}, u32[]{:S(2)}) copy-start(f32[1,16]{1,0:T(1,128)S(1)} %get-tuple-element.31) | copy-start | bytes 196
  50.5 32.5 %copy-start.36 = (f32[16]{0:T(128)}, f32[16]{0:T(128)S(1)}, u32[]{:S(2)}) copy-start(f32[16]{0:T(128)S(1)} %get-tuple-element.57) | copy-start | bytes 196
  50.5 32.6 %copy-start.30 = (f32[16]{0:T(128)}, f32[16]{0:T(128)S(1)}, u32[]{:S(2)}) copy-start(f32[16]{0:T(128)S(1)} %get-tuple-element.60) | copy-start | bytes 196
  50.5 32.7 %copy-start.28 = (f32[16]{0:T(128)}, f32[16]{0:T(128)S(1)}, u32[]{:S(2)}) copy-start(f32[16]{0:T(128)S(1)} %get-tuple-element.59) | copy-start | bytes 196
  50.6 32.9 %copy-start.26 = (f32[16]{0:T(128)}, f32[16]{0:T(128)S(1)}, u32[]{:S(2)}) copy-start(f32[16]{0:T(128)S(1)} %get-tuple-element.58) | copy-start | bytes 196
  50.6 519.1 %copy-start.22 = (f32[16]{0:T(128)}, f32[16]{0:T(128)S(1)}, u32[]{:S(2)}) copy-start(f32[16]{0:T(128)S(1)} %get-tuple-element.62) | copy-start | bytes 196
  50.6 520.0 %copy-start.25 = (f32[16]{0:T(128)}, f32[16]{0:T(128)S(1)}, u32[]{:S(2)}) copy-start(f32[16]{0:T(128)S(1)} %get-tuple-element.61) | copy-start | bytes 196
  54.3 26.5 %copy-start.44 = (f32[128]{0:T(128)}, f32[128]{0:T(128)S(1)}, u32[]{:S(2)}) copy-start(f32[128]{0:T(128)S(1)} %iota_convert_fusion) | copy-start | bytes 1540
  54.3 58.1 %copy-start.38 = (f32[16]{0:T(128)}, f32[16]{0:T(128)S(1)}, u32[]{:S(2)}) copy-start(f32[16]{0:T(128)S(1)} %get-tuple-element.48) | copy-start | bytes 196
  54.3 505.4 %copy-start.23 = (f32[16]{0:T(128)}, f32[16]{0:T(128)S(1)}, u32[]{:S(2)}) copy-start(f32[16]{0:T(128)S(1)} %get-tuple-element.49) | copy-start | bytes 196
  56.5 24.4 %copy-start.40 = (f32[128]{0:T(128)}, f32[128]{0:T(128)S(1)}, u32[]{:S(2)}) copy-start(f32[128]{0:T(128)S(1)} %broadcast_subtract_fusion) | copy-start | bytes 1540
  56.5 55.9 %copy-start.34 = (f32[128]{0:T(128)}, f32[128]{0:T(128)S(1)}, u32[]{:S(2)}) copy-start(f32[128]{0:T(128)S(1)} %broadcast_add_fusion) | copy-start | bytes 1540
  56.7 53.9 %copy-start.13 = (f32[128,16,1,1]{1,3,2,0:T(1,128)}, f32[128,16,1,1]{1,3,2,0:T(1,128)S(1)}, u32[]{:S(2)}) copy-start(f32[128,16,1,1]{1,3,2,0:T(1,128)S(1)} %pad_multiply_fusion) | copy-start | bytes 24580
  80.9 33.4 %copy-start.3 = (bf16[1,128,4096]{1,2,0:T(8,128)(2,1)}, bf16[1,128,4096]{1,2,0:T(8,128)(2,1)S(1)}, u32[]{:S(2)}) copy-start(bf16[1,128,4096]{1,2,0:T(8,128)(2,1)S(1)} %copy.207) | copy-start | bytes 3145732
  110.6 1.0 copy-start.7
  111.9 2.4 copy-start.16
  215.6 8.0 copy-start.15
  215.6 59.5 %all-to-all-start.3 = ((f32[128,1,4096]{2,1,0:T(1,128)}), f32[128,1,4096]{2,1,0:T(1,128)}, u32[]{:S(2)}, u32[]{:S(2)}) async-start(f32[128,1,4096]{2,1,0:T(1,128)} %reshape.686), calls=%async_computation.3 | async-start | bytes 4194304 | tf_op jit(solution)/shard_map/all_to_all | solution.py:134
  320.2 3.2 copy-start.19
  321.4 87.8 %collective-permute-start.1 = (bf16[128,4096]{0,1:T(8,128)(2,1)}, bf16[128,4096]{0,1:T(8,128)(2,1)}, u32[]{:S(2)}, u32[]{:S(2)}) collective-permute-start(bf16[128,4096]{0,1:T(8,128)(2,1)} %fusion.7), channel_id=1, source_target_pairs={{0,1},{1,2},{2,3},{3,4},{4,5},{5,6},{6,7},{7,8},{8,9},{9,10},{10,1... | collective-permute-start | bytes 3145736 | tf_op jit(solution)/shard_map/ppermute | solution.py:12
  411.3 21.5 %copy-start.1 = (f32[128,4096]{0,1:T(8,128)}, f32[128,4096]{0,1:T(8,128)S(1)}, u32[]{:S(2)}) copy-start(f32[128,4096]{0,1:T(8,128)S(1)} %get-tuple-element.32) | copy-start | bytes 6291460
  411.3 21.5 %copy-start.2 = (f32[128,4096]{0,1:T(8,128)}, f32[128,4096]{0,1:T(8,128)S(1)}, u32[]{:S(2)}) copy-start(f32[128,4096]{0,1:T(8,128)S(1)} %get-tuple-element.33) | copy-start | bytes 6291460
  411.3 21.5 %copy-start.10 = (bf16[1,128,4096]{1,2,0:T(8,128)(2,1)S(1)}, bf16[1,128,4096]{1,2,0:T(8,128)(2,1)}, u32[]{:S(2)}) copy-start(bf16[1,128,4096]{1,2,0:T(8,128)(2,1)} %copy.174) | copy-start | bytes 3145732
  411.3 21.5 %copy-start.11 = (bf16[1,128,4096]{1,2,0:T(8,128)(2,1)S(1)}, bf16[1,128,4096]{1,2,0:T(8,128)(2,1)}, u32[]{:S(2)}) copy-start(bf16[1,128,4096]{1,2,0:T(8,128)(2,1)} %copy.175) | copy-start | bytes 3145732
  434.2 16.1 %copy-start.5 = (bf16[1,128,4096]{1,2,0:T(8,128)(2,1)}, bf16[1,128,4096]{1,2,0:T(8,128)(2,1)S(1)}, u32[]{:S(2)}) copy-start(bf16[1,128,4096]{1,2,0:T(8,128)(2,1)S(1)} %get-tuple-element.39) | copy-start | bytes 3145732
  434.2 16.1 %collective-permute-start = (bf16[128,4096]{0,1:T(8,128)(2,1)S(1)}, bf16[128,4096]{0,1:T(8,128)(2,1)S(1)}, u32[]{:S(2)}, u32[]{:S(2)}) collective-permute-start(bf16[128,4096]{0,1:T(8,128)(2,1)S(1)} %bitcast.239), channel_id=1, source_target_pairs={{1,0},{2,1},{3,2},{4,3},{5,4},{6,5},{7,6},{8,7},{9,8},{10,9},{11,1... | collective-permute-start | bytes 3145736 | tf_op jit(solution)/shard_map/ppermute | solution.py:12
  557.3 2.4 copy-start.41
  569.5 1.2 copy-start.27
  569.5 1.2 copy-start.29
  569.5 1.3 copy-start.31
  569.6 1.4 copy-start.37
  569.7 0.8 copy-start.12
  570.8 0.9 copy-start.18
  598.4 28.9 %slice-start = ((f32[64,16,1,32]{3,1,0,2:T(8,128)}), f32[1,16,1,32]{3,1,0,2:T(8,128)S(1)}, s32[]{:S(2)}) async-start(f32[64,16,1,32]{3,1,0,2:T(8,128)} %copy-done.12), calls=%async_computation.5 | async-start | bytes 16384 | tf_op jit(solution)/shard_map/slice | solution.py:76
  600.1 38.5 %copy-start.21 = (f32[1,16]{1,0:T(1,128)S(1)}, f32[1,16]{1,0:T(1,128)}, u32[]{:S(2)}) copy-start(f32[1,16]{1,0:T(1,128)} %copy-done.20) | copy-start | bytes 196
  638.6 1.4 copy-start.8
  638.6 1.5 copy-start.9
  661.1 23.7 %copy-start.14 = (f32[128,16,1,1]{1,3,2,0:T(1,128)S(1)}, f32[128,16,1,1]{1,3,2,0:T(1,128)}, u32[]{:S(2)}) copy-start(f32[128,16,1,1]{1,3,2,0:T(1,128)} %copy-done.13) | copy-start | bytes 24580
  684.9 0.9 copy-start.24
  684.9 0.9 copy-start.35
  684.9 0.9 copy-start.39
  685.7 3.5 copy-start
  685.7 3.5 copy-start.17
  816.7 7.6 copy-start.6
  816.7 436.6 %all-to-all-start.1 = ((bf16[128,2,2048]{2,1,0:T(2,128)(2,1)}), bf16[128,2,2048]{2,1,0:T(2,128)(2,1)}, u32[]{:S(2)}, u32[]{:S(2)}) async-start(bf16[128,2,2048]{2,1,0:T(2,128)(2,1)} %reshape.682), calls=%async_computation.1 | async-start | bytes 2097152 | tf_op jit(solution)/shard_map/all_to_all | solution.py:166
  824.2 337.1 %all-reduce.53.cloned.1.call-start = ((), (), s32[]{:S(2)}) async-start(), calls=%async_computation.4 | async-start | bytes 131072 | tf_op jit(solution)/shard_map/psum | solution.py:171
  922.9 242.5 %copy-start.4 = (bf16[1,128,4096]{1,2,0:T(8,128)(2,1)S(1)}, bf16[1,128,4096]{1,2,0:T(8,128)(2,1)}, u32[]{:S(2)}) copy-start(bf16[1,128,4096]{1,2,0:T(8,128)(2,1)} %copy-done.3) | copy-start | bytes 3145732
  1167.3 10.6 copy-start.43
  1167.3 10.6 copy-start.45
Sparse Core Ops, SparseCore 0:
  923.1 238.2 all-reduce.52
where the time goes:
time: 1310 us; the launch traced here: 1300 us
  local copies, waits for them, and re-layouts  453 us (35%)
  waiting for transfers between devices  323 us (25%)
  other arithmetic  243 us (19%)
  blocking collectives  142 us (11%)
  matrix products  86.1 us (7%)
  starting transfers between devices  35 us (3%)
  between operations  15.5 us (1%)
    psum x1, waiting for transfers between devices, on_device(): summed = lax.psum((grad_res, grad_taps), ('rep', 'ctx'))  236 us
    unnamed x3, other arithmetic  188 us
    unnamed x124, local copies, waits for them, and re-layouts  161 us
    dot_general x13, matrix products, contract(): return jnp.einsum(form, left_op, right_op, precision=lax.Precision.HIGHEST)  86.1 us
    psum x1, blocking collectives, on_device(): summed = lax.psum((grad_res, grad_taps), ('rep', 'ctx'))  74.4 us
    all_to_all x1, blocking collectives, on_device(): lax.all_to_all(cot_li[None], 'ctx', split_axis=2, concat_axis=1, tiled=True)  67.2 us
    pad x30, local copies, waits for them, and re-layouts, chain_states(): lax.associative_scan(link_states, (factor, block_ends), axis=0)  53 us
    all_to_all x1, waiting for transfers between devices, on_device(): lax.all_to_all(values_ch.reshape(1, seq_rows, local_width), 'ctx', split_...  50.9 us
  transfers between devices with their start and end apart: 6, of which 4 were waited for; matrix products, arithmetic and copies ran while one was open for 16% of the time, Pallas kernels for 0%

commit v1 on v0

v1 whole, which is shorter than its diff:
```python
import functools
import math

import jax
import jax.numpy as jnp
from jax import lax
from jax.experimental import pallas as pl
from jax.experimental.pallas import tpu as pltpu
from jax.sharding import PartitionSpec as P

F32 = jnp.float32
BF16 = jnp.bfloat16
LANES = 128
NN = (((1,), (0,)), ((), ()))
NT = (((1,), (1,)), ((), ()))
TN = (((0,), (0,)), ((), ()))
VMEM_LIMIT = 48 * 1024 * 1024


def dot(left, right, dims=NN):
    return lax.dot_general(left, right, dims, preferred_element_type=F32)


def split(x):
    high = x.astype(BF16)
    return high, (x - high.astype(F32)).astype(BF16)


def iota(shape, dim):
    return lax.broadcasted_iota(jnp.int32, shape, dim)


def roll_left(x, amount):
    return pltpu.roll(x, x.shape[1] - amount, 1)


def pick_groups(stacked, rows, size):
    lane_group = iota((rows, LANES), 1) // size
    out = stacked[:rows]
    for g in range(1, LANES // size):
        out = jnp.where(lane_group == g, stacked[g * rows : (g + 1) * rows], out)
    return out


def spread_groups(x, size):
    lane_group = iota(x.shape, 1) // size
    zero = jnp.zeros_like(x)
    return jnp.concatenate(
        [jnp.where(lane_group == g, x, zero) for g in range(LANES // size)], axis=0
    )


def circulant(row):
    return pltpu.roll(jnp.broadcast_to(row, (LANES, LANES)), 0, 1, stride=1, stride_axis=0)


def lag_sum(z):
    rows = LANES
    while rows > 8:
        rows //= 2
        z = z[:rows] + roll_left(z[rows:], rows)
    sub = iota((8, LANES), 0)
    for bit in (4, 2, 1):
        z = jnp.where((sub & bit) != 0, roll_left(z, bit), z)
    return jnp.sum(z, axis=0, keepdims=True)


def carried_part(table, entering, size):
    t_high, t_low = split(table)
    e_high, e_low = split(entering)
    e_high, e_low = spread_groups(e_high, size), spread_groups(e_low, size)
    return dot(
        jnp.concatenate([t_high, t_high, t_low], axis=0),
        jnp.concatenate([e_high, e_low, e_high], axis=0),
        TN,
    )


def states_kernel(size, modes, x_ref, table_ref, out_ref):
    per = LANES // size
    for i in range(x_ref.shape[1] // LANES):
        lanes = slice(i * LANES, (i + 1) * LANES)
        high, low = split(table_ref[i * per * modes : (i + 1) * per * modes, :])
        prod = dot(jnp.concatenate([high, low], axis=0), x_ref[:, lanes])
        prod = prod[: per * modes] + prod[per * modes :]
        out_ref[i * modes : (i + 1) * modes, :] = pick_groups(prod, modes, size)


def mixer_back_kernel(
    size, modes, own_ref, next_ref, gate_ref, x_ref, taps_ref, table_ref, gm_ref, out_ref, lag_ref
):
    per = LANES // size
    row, col = iota((LANES, LANES), 0), iota((LANES, LANES), 1)
    for i in range(x_ref.shape[1] // LANES):
        lanes = slice(i * LANES, (i + 1) * LANES)
        mats = []
        for g in range(per):
            full = circulant(taps_ref[i * per + g : i * per + g + 1, :])
            high, low = split(full)
            zero = jnp.zeros_like(high)
            mats.append(
                jnp.concatenate(
                    [jnp.where(col >= row, high, zero), jnp.where(col < row, high, zero),
                     jnp.where(col >= row, low, zero), jnp.where(col < row, low, zero)],
                    axis=1,
                )
            )
        own, after = own_ref[:, lanes], next_ref[:, lanes]
        prod = dot(jnp.concatenate(mats, axis=0), jnp.concatenate([own, after, own, after], axis=0))
        grad_mixer = pick_groups(prod, LANES, size)
        gm_ref[:, lanes] = grad_mixer
        cot = grad_mixer * gate_ref[:, lanes].astype(F32)
        high, low = split(cot)
        t_high, t_low = split(table_ref[i * per * modes : (i + 1) * per * modes, :])
        left = jnp.concatenate(
            [jnp.concatenate([t_high, t_high], axis=1), jnp.concatenate([t_low, t_low], axis=1)], axis=0
        )
        prod = dot(left, jnp.concatenate([high, low], axis=0))
        prod = prod[: per * modes] + prod[per * modes :]
        out_ref[i * modes : (i + 1) * modes, :] = pick_groups(prod, modes, size)
        pairs = dot(spread_groups(x_ref[:, lanes], size), high, NT)
        for g in range(per):
            z = jnp.where(col >= row, pairs[g * LANES : (g + 1) * LANES], 0.0)
            lag_ref[i * per + g : i * per + g + 1, :] = lag_sum(z)


def values_kernel(
    size, modes, x_ref, gate_ref, gm_ref, own_ref, next_ref, filt_ref, table_ref, enter_ref,
    mix_ref, ggl_ref, lag_ref,
):
    per = LANES // size
    row, col = iota((LANES, LANES), 0), iota((LANES, LANES), 1)
    for i in range(x_ref.shape[1] // LANES):
        lanes = slice(i * LANES, (i + 1) * LANES)
        mats = []
        for g in range(per):
            full = circulant(filt_ref[i * per + g : i * per + g + 1, :])
            high, low = split(jnp.where(col <= row, full, 0.0))
            mats.append(jnp.concatenate([high, low], axis=1))
        x = x_ref[:, lanes]
        prod = dot(jnp.concatenate(mats, axis=0), jnp.concatenate([x, x], axis=0))
        values = pick_groups(prod, LANES, size) + carried_part(
            table_ref[i * per * modes : (i + 1) * per * modes, :],
            enter_ref[i * modes : (i + 1) * modes, :],
            size,
        )
        ggl_ref[:, lanes] = (gm_ref[:, lanes] * values).astype(BF16)
        mix = (gate_ref[:, lanes].astype(F32) * values).astype(BF16)
        mix_ref[:, lanes] = mix
        both = jnp.concatenate([own_ref[:, lanes], next_ref[:, lanes]], axis=0)
        pairs = dot(spread_groups(mix, size), both, NT)
        for g in range(per):
            z = pairs[g * LANES : (g + 1) * LANES]
            lag_ref[i * per + g : i * per + g + 1, :] = lag_sum(
                jnp.where(col >= row, z[:, :LANES], z[:, LANES:])
            )


def input_grad_kernel(size, modes, gm_ref, gate_ref, filt_ref, table_ref, enter_ref, out_ref):
    per = LANES // size
    row, col = iota((LANES, LANES), 0), iota((LANES, LANES), 1)
    for i in range(gm_ref.shape[1] // LANES):
        lanes = slice(i * LANES, (i + 1) * LANES)
        mats = []
        for g in range(per):
            full = circulant(filt_ref[i * per + g : i * per + g + 1, :])
            high, low = split(jnp.where(col >= row, full, 0.0))
            mats.append(jnp.concatenate([high, low, high], axis=1))
        high, low = split(gm_ref[:, lanes] * gate_ref[:, lanes].astype(F32))
        prod = dot(jnp.concatenate(mats, axis=0), jnp.concatenate([high, high, low], axis=0))
        out_ref[:, lanes] = (
            pick_groups(prod, LANES, size)
            + carried_part(
                table_ref[i * per * modes : (i + 1) * per * modes, :],
                enter_ref[i * modes : (i + 1) * modes, :],
                size,
            )
        ).astype(BF16)


def mixer_kernel(size, own_ref, before_ref, taps_ref, cot_ref, out_ref):
    per = LANES // size
    row, col = iota((LANES, LANES), 0), iota((LANES, LANES), 1)
    for i in range(own_ref.shape[1] // LANES):
        lanes = slice(i * LANES, (i + 1) * LANES)
        mats = []
        for g in range(per):
            high, low = split(circulant(taps_ref[i * per + g : i * per + g + 1, :]))
            zero = jnp.zeros_like(high)
            mats.append(
                jnp.concatenate(
                    [jnp.where(col <= row, high, zero), jnp.where(col > row, high, zero),
                     jnp.where(col <= row, low, zero), jnp.where(col > row, low, zero)],
                    axis=1,
                )
            )
        own, before = own_ref[:, lanes], before_ref[:, lanes]
        prod = dot(jnp.concatenate(mats, axis=0), jnp.concatenate([own, before, own, before], axis=0))
        mixed = pick_groups(prod, LANES, size)
        out_ref[:, lanes] = (cot_ref[:, lanes].astype(F32) * mixed).astype(BF16)


def scan_kernel(x_ref, decay_ref, out_ref):
    decay = decay_ref[...]
    state = jnp.zeros_like(decay)
    for d in range(x_ref.shape[0]):
        out_ref[d] = state
        state = decay * state + x_ref[d]


def back_scan_kernel(rows, x_ref, decay_ref, front_ref, out_ref, sum_ref):
    decay = decay_ref[...]
    state = jnp.zeros_like(decay)
    total = jnp.zeros_like(decay)
    for d in reversed(range(x_ref.shape[0])):
        x = x_ref[d, rows:, :]
        out_ref[d] = state
        state = decay * state + x
        total = total + x * front_ref[d]
    sum_ref[...] = total


def call(body, width, step, specs, outs, args, flops):
    def block(rows):
        if rows is None:
            return pl.BlockSpec((LANES, step), lambda i: (0, i))
        return pl.BlockSpec((rows, LANES), lambda i: (i, 0))

    def shape(rows, kind):
        if rows is None:
            return jax.ShapeDtypeStruct((LANES, width), kind)
        return jax.ShapeDtypeStruct((rows * (width // step), LANES), kind)

    nbytes = sum(a.size * a.dtype.itemsize for a in args)
    return pl.pallas_call(
        body,
        grid=(width // step,),
        in_specs=[block(rows) for rows in specs],
        out_specs=[block(rows) for rows, kind in outs],
        out_shape=[shape(rows, kind) for rows, kind in outs],
        compiler_params=pltpu.CompilerParams(vmem_limit_bytes=VMEM_LIMIT),
        cost_estimate=pl.CostEstimate(flops=flops, bytes_accessed=nbytes, transcendentals=0),
    )(*args)


def whole(body, outs, args):
    return pl.pallas_call(
        body,
        out_shape=[jax.ShapeDtypeStruct(s, F32) for s in outs],
        compiler_params=pltpu.CompilerParams(vmem_limit_bytes=VMEM_LIMIT),
    )(*args)


def shifted(x, by):
    count = lax.axis_size("ctx")
    return lax.ppermute(x, "ctx", [(i, i + by) for i in range(count) if 0 <= i + by < count])


def exchange(x, axes="ctx"):
    return lax.all_to_all(x, axes, split_axis=0, concat_axis=0, tiled=True)


def on_device(inputs, gate_li, gate_mr, cotangent, residues, rates, taps):
    seq, gate, cot = inputs[0], gate_li[0], cotangent[0]
    width = seq.shape[1]
    groups, modes = rates.shape
    size = width // groups
    per = LANES // size
    tiles = width // LANES
    reps, count = lax.axis_size("rep"), lax.axis_size("ctx")
    me = lax.axis_index("ctx")
    own_rows = tiles * modes // count
    step = min(512, width)
    state_rows = step // LANES * modes
    table_rows = per * state_rows
    group_rows = step // size

    scaled = (cot.astype(F32) * gate_mr[0].astype(F32)).astype(BF16)
    after = shifted(scaled, -1)

    lags = jnp.arange(LANES).astype(F32)
    norm = jnp.sqrt(-jnp.expm1(-2.0 * rates))
    weight = residues * norm
    rate3, weight3 = rates[:, :, None], weight[:, :, None]
    lam = jnp.exp(-rate3 * lags)
    filt = jnp.sum(weight3 * lam, axis=1)
    filt_back = jnp.roll(jnp.flip(filt, 1), 1, axis=1)
    taps_back = jnp.roll(jnp.flip(taps, 1), 1, axis=1)
    to_end = jnp.exp(-rate3 * (LANES - 1.0 - lags))
    from_start = jnp.exp(-rate3 * (lags + 1.0))
    flat = (groups * modes, LANES)
    end_table = to_end.reshape(flat)
    start_table = from_start.reshape(flat)
    front_table = (weight3 * from_start).reshape(flat)
    back_table = (weight3 * to_end).reshape(flat)
    decay = jnp.exp(-rates * LANES).reshape(tiles, per, modes)
    decay = jnp.repeat(jnp.swapaxes(decay, 1, 2).reshape(tiles * modes, per), size, axis=1)
    decay = lax.dynamic_slice_in_dim(decay, me * own_rows, own_rows, 0)

    bind = functools.partial
    states = call(
        bind(states_kernel, size, modes), width, step, [None, table_rows], [(state_rows, F32)],
        [seq, end_table], 2 * LANES * width * 64,
    )[0]
    ends = exchange(states.reshape(count, own_rows, LANES))
    entering = whole(scan_kernel, [ends.shape], [ends, decay])[0]

    grad_mixer, back_states, lag_cot = call(
        bind(mixer_back_kernel, size, modes), width, step,
        [None, None, None, None, group_rows, table_rows],
        [(None, F32), (state_rows, F32), (group_rows, F32)],
        [scaled, after, gate, seq, taps, start_table], 2 * LANES * width * 1024,
    )
    second = exchange(
        jnp.concatenate([entering, back_states.reshape(count, own_rows, LANES)], axis=1)
    )
    back_entering, state_sums = whole(
        bind(back_scan_kernel, own_rows), [ends.shape, decay.shape], [second, decay, entering]
    )

    mixer_in, grad_gate_li, lag_taps = call(
        bind(values_kernel, size, modes), width, step,
        [None, None, None, None, None, group_rows, table_rows, state_rows],
        [(None, BF16), (None, BF16), (group_rows, F32)],
        [seq, gate, grad_mixer, scaled, after, filt_back, front_table,
         second[:, :own_rows].reshape(tiles * modes, LANES)], 2 * LANES * width * 1024,
    )
    before = shifted(mixer_in, 1)
    third = exchange(
        jnp.concatenate(
            [back_entering, lag_taps.reshape(count, -1, LANES), lag_cot.reshape(count, -1, LANES)], axis=1
        )
    )
    own_groups = groups // count
    grad_inputs = call(
        bind(input_grad_kernel, size, modes), width, step,
        [None, None, group_rows, table_rows, state_rows], [(None, BF16)],
        [grad_mixer, gate, filt, back_table, third[:, :own_rows].reshape(tiles * modes, LANES)],
        2 * LANES * width * 1024,
    )[0]
    lag_sums = jnp.sum(third[:, own_rows:], axis=0)
    tap_part, cot_part = lag_sums[:own_groups], lag_sums[own_groups:]
    lam_own = lax.dynamic_slice_in_dim(lam, me * own_groups, own_groups, 0)
    local_part = jnp.sum(lam_own * cot_part[:, None, :], axis=2)
    first_part = jnp.sum(state_sums.reshape(own_rows, per, size), axis=2)
    message = jnp.concatenate(
        [tap_part.reshape(-1), local_part.reshape(-1), first_part.reshape(-1)]
    )
    pad = -message.size % LANES
    message = jnp.concatenate([message, jnp.zeros((pad,), F32)]).reshape(-1, LANES)
    got = exchange(
        jnp.broadcast_to(message[None], (reps * count,) + message.shape), ("rep", "ctx")
    )
    got = jnp.sum(got.reshape(reps, count, -1), axis=0)
    n_tap, n_loc = own_groups * LANES, own_groups * modes
    grad_taps = got[:, :n_tap].reshape(groups, LANES)
    local_all = got[:, n_tap : n_tap + n_loc].reshape(groups, modes)
    first_all = got[:, n_tap + n_loc : n_tap + n_loc + own_rows * per].reshape(tiles, modes, per)
    first_all = jnp.swapaxes(first_all, 1, 2).reshape(groups, modes)

    grad_gate_mr = call(
        bind(mixer_kernel, size), width, step, [None, None, group_rows, None], [(None, BF16)],
        [mixer_in, before, taps_back, cot], 2 * LANES * width * 1024,
    )[0]
    scale = 1.0 / math.sqrt(reps * count * LANES)
    return (
        grad_inputs[None],
        grad_gate_li[None],
        grad_gate_mr[None],
        norm * (first_all + local_all) * scale,
        grad_taps * scale,
    )


def solution(mesh):
    big = P("rep", "ctx", None)
    return jax.shard_map(
        on_device,
        mesh=mesh,
        in_specs=(big, big, big, big, P(), P(), P()),
        out_specs=(big, big, big, P(), P()),
        check_vma=False,
    )
```

time: 1310 us -> 181 us (0.14)
  local copies, waits for them, and re-layouts: 453 us -> 16 us
  waiting for transfers between devices: 323 us -> 48 us
  other arithmetic: 243 us -> 13.3 us
  blocking collectives: 142 us -> 0 us
  matrix products: 86.1 us -> 0 us
  Pallas kernels: 0 us -> 57.9 us
  between operations: 15.5 us -> 0.9 us
    psum x1 -> x0, waiting for transfers between devices: 236 us -> none  [on_device(): summed = lax.psum((grad_res, grad_taps), ('rep', 'ctx'))]
    unnamed x3 -> x0, other arithmetic: 188 us -> none
    unnamed x124 -> x38, local copies, waits for them, and re-layouts: 161 us -> 6.59 us
    dot_general x13 -> x0, matrix products: 86.1 us -> none  [contract(): return jnp.einsum(form, left_op, right_op, precision=lax.Precision.HIGHEST)]
    pad x34 -> x0, local copies, waits for them, and re-layouts: 81.7 us -> none  [the longest x30 53 us: chain_states(): lax.associative_scan(link_states, (factor, block_ends), axis=0)]
    psum x1 -> x0, blocking collectives: 74.4 us -> none  [on_device(): summed = lax.psum((grad_res, grad_taps), ('rep', 'ctx'))]
    all_to_all x1 -> x0, blocking collectives: 67.2 us -> none  [on_device(): lax.all_to_all(cot_li[None], 'ctx', split_axis=2, concat_axis=1, tiled=True)]
    reshape x6 -> x7, local copies, waits for them, and re-layouts: 64.5 us -> 2.47 us  [the longest x1 1.16 us: on_device(): got = jnp.sum(got.reshape(reps, count, -1), axis=0)]
  transfers between devices with their start and end apart: 6 -> 6, of which waited for: 4 -> 3; matrix products, arithmetic and copies ran while one was open for 16% -> 8% of each run, Pallas kernels for 0% -> 10%
where the time goes in v1:
time: 181 us; the launch traced here: 180 us
  Pallas kernels  57.9 us (32%)
  waiting for transfers between devices  48 us (27%)
  starting transfers between devices  44.2 us (24%)
  local copies, waits for them, and re-layouts  16 us (9%)
  other arithmetic  13.3 us (7%)
    pallas_call x5, Pallas kernels, call(): pl.pallas_call(body, grid=(width // step,), in_specs=[block(rows) for row...  56.3 us
    all_to_all x4, waiting for transfers between devices, exchange(): return lax.all_to_all(x, axes, split_axis=0, concat_axis=0, tiled=True)  48 us
    all_to_all x4, starting transfers between devices, exchange(): return lax.all_to_all(x, axes, split_axis=0, concat_axis=0, tiled=True)  35.3 us
    ppermute x2, starting transfers between devices, shifted(): lax.ppermute(x, 'ctx', [(i, i + by) for i in range(count) if 0 <= i + by...  8.88 us
    unnamed x38, local copies, waits for them, and re-layouts  6.59 us
  transfers between devices with their start and end apart: 6, of which 3 were waited for; matrix products, arithmetic and copies ran while one was open for 8% of the time, Pallas kernels for 10%

profile of v1, /device:TPU:1, one launch (start us, length us, event | category | flops | bytes accessed | tf_op | source)
XLA Modules:
  0.0 180.2 jit_solution(13827835108904505137)
XLA Ops:
  0.7 1.8 fusion.own_ref
  2.5 5.2 %collective-permute-start = (bf16[128,4096]{1,0:T(8,128)(2,1)S(1)}, bf16[128,4096]{1,0:T(8,128)(2,1)}, u32[]{:S(2)}, u32[]{:S(2)}) collective-permute-start(bf16[128,4096]{1,0:T(8,128)(2,1)S(1)} %fusion.own_ref), channel_id=1, source_target_pairs={{1,0},{2,1},{3,2},{4,3},{5,4},{6,5},{7,6},{8,7},{9,8},{10,9},{11,1... | collective-permute-start | bytes 3145736 | tf_op jit(solution)/shard_map/ppermute | solution.py:256
  7.7 0.1 copy.52
  7.8 0.1 mul.128
  7.9 0.1 copy.51
  8.0 0.1 mul.116
  8.1 0.4 copy-done.14
  8.4 0.2 copy-done.15
  8.6 2.0 %broadcast_multiply_fusion = (f32[2048,128]{1,0:T(8,128)}, f32[2048,128]{1,0:T(8,128)}, f32[2048,128]{1,0:T(8,128)S(1)}, f32[2048,128]{1,0:T(8,128)}) fusion(f32[2048]{0:T(1024)S(1)} %mul.128, f32[128]{0:T(128)S(1)} %get-tuple-element.55, f32[2048]{0:T(1024)S(1)} %mul.116, f32[128]{0:T(128)S(1)} %get-tuple-element.54), kind=kLoop, calls=%fused_computation.8 | loop fusion | flops 1048576 | bytes 4211712 | tf_op jit(solution)/shard_map/mul | solution.py:294
  10.6 3.4 %shard_map.111 = f32[512,128]{1,0:T(8,128)} custom-call(bf16[128,4096]{1,0:T(8,128)(2,1)S(1)} %bitcast.34, f32[2048,128]{1,0:T(8,128)S(1)} %get-tuple-element.47.table_ref), custom_call_target="tpu_custom_call" | custom-call | flops 67108864 | bytes 2097152 | tf_op jit(solution)/shard_map/pallas_call | solution.py:235
  14.0 11.2 %all-to-all-start = ((f32[128,4,128]{2,1,0:T(4,128)}), f32[128,4,128]{2,1,0:T(4,128)S(1)}, u32[]{:S(2)}, u32[]{:S(2)}) async-start(f32[128,4,128]{2,1,0:T(4,128)} %bitcast.4), calls=%async_computation | async-start | bytes 524288 | tf_op jit(solution)/shard_map/all_to_all | solution.py:260
  25.2 0.1 copy.55
  25.3 0.6 copy.56
  26.0 0.9 reshape.90
  26.9 0.1 constant_dynamic-slice_fusion
  27.0 0.1 copy.62.decay_ref
  27.1 11.4 %all-to-all-done.x_ref = f32[128,4,128]{2,1,0:T(4,128)S(1)} async-done(((f32[128,4,128]{2,1,0:T(4,128)}), f32[128,4,128]{2,1,0:T(4,128)S(1)}, u32[]{:S(2)}, u32[]{:S(2)}) %all-to-all-start) | async-done | bytes 262176 | tf_op jit(solution)/shard_map/all_to_all | solution.py:260
  38.5 0.7 copy-done.6
  39.2 0.9 copy-done.7
  40.1 0.3 shard_map.112.front_ref
  40.4 0.0 copy-start.5
  40.4 1.2 copy-done.5
  41.6 20.8 %shard_map.110 = (f32[128,4096]{1,0:T(8,128)}, f32[512,128]{1,0:T(8,128)S(1)}, f32[128,128]{1,0:T(8,128)S(1)}) custom-call(bf16[128,4096]{1,0:T(8,128)(2,1)S(1)} %fusion.own_ref, bf16[128,4096]{1,0:T(8,128)(2,1)} %collective-permute-done.next_ref, bf16[128,4096]{1,0:T(8,128)(2,1)S(1)} %bitcast.37, bf16[128,4096]{1,0:T(8,128)(2,1)S(1)} %bitcast.35, ...), custom_call_target="tpu_custom_call" | custom-call | flops 1073741824 | bytes 5308416 | tf_op jit(solution)/shard_map/pallas_call | solution.py:235
  62.4 0.9 pad_maximum_fusion
  63.3 6.8 %all-to-all-start.1 = ((f32[128,8,128]{2,1,0:T(8,128)}), f32[128,8,128]{2,1,0:T(8,128)}, u32[]{:S(2)}, u32[]{:S(2)}) async-start(f32[128,8,128]{2,1,0:T(8,128)} %pad_maximum_fusion), calls=%async_computation.1 | async-start | bytes 1048576 | tf_op jit(solution)/shard_map/all_to_all | solution.py:260
  70.2 2.5 %multiply_exponential_fusion.1 = (f32[128,16,128]{2,1,0:T(8,128)}, f32[128,128]{1,0:T(8,128)S(1)}) fusion(f32[128]{0:T(128)S(1)} %iota_convert_fusion, f32[128,16]{1,0:T(8,128)} %copy-done.15, f32[128,16]{1,0:T(8,128)} %copy-done.14), kind=kLoop, calls=%fused_computation.4 | loop fusion | flops 770048 | bytes 1131008 | tf_op jit(solution)/shard_map/exp | solution.py:285
  72.6 0.7 slice.61
  73.3 1.6 slice.48
  74.9 1.6 pad_maximum_fusion.2.filt_ref
  76.5 11.7 %all-to-all-done.1.x_ref = f32[128,8,128]{2,1,0:T(8,128)} async-done(((f32[128,8,128]{2,1,0:T(8,128)}), f32[128,8,128]{2,1,0:T(8,128)}, u32[]{:S(2)}, u32[]{:S(2)}) %all-to-all-start.1) | async-done | bytes 524320 | tf_op jit(solution)/shard_map/all_to_all | solution.py:260
  88.2 1.3 shard_map.113
  89.5 1.1 slice.62
  90.6 0.0 copy-start.11
  90.6 0.8 copy-done.11
  91.4 17.0 %shard_map.114 = (bf16[128,4096]{1,0:T(8,128)(2,1)S(1)}, bf16[128,4096]{1,0:T(8,128)(2,1)}, f32[128,128]{1,0:T(8,128)S(1)}) custom-call(bf16[128,4096]{1,0:T(8,128)(2,1)S(1)} %bitcast.36, bf16[128,4096]{1,0:T(8,128)(2,1)S(1)} %bitcast.38, f32[128,4096]{1,0:T(8,128)} %get-tuple-element.13.gm_ref, bf16[128,4096]{1,0:T(8,128)(2,1)S(1)} %fusion.own_ref, ...), custom_call_target="tpu_custom_call" | custom-call | flops 1073741824 | bytes 7667712 | tf_op jit(solution)/shard_map/pallas_call | solution.py:235
  108.4 1.0 copy-done.8
  109.4 1.0 pad_maximum_fusion.1
  110.4 7.4 %all-to-all-start.2 = ((f32[128,6,128]{2,1,0:T(8,128)}), f32[128,6,128]{2,1,0:T(8,128)}, u32[]{:S(2)}, u32[]{:S(2)}) async-start(f32[128,6,128]{2,1,0:T(8,128)} %pad_maximum_fusion.1), calls=%async_computation.2 | async-start | bytes 1048576 | tf_op jit(solution)/shard_map/all_to_all | solution.py:260
  117.7 3.7 %collective-permute-start.1 = (bf16[128,4096]{1,0:T(8,128)(2,1)}, bf16[128,4096]{1,0:T(8,128)(2,1)}, u32[]{:S(2)}, u32[]{:S(2)}) collective-permute-start(bf16[128,4096]{1,0:T(8,128)(2,1)} %copy-done.8), channel_id=1, source_target_pairs={{0,1},{1,2},{2,3},{3,4},{4,5},{5,6},{6,7},{7,8},{8,9},{9,10},{10,1... | collective-permute-start | bytes 3145736 | tf_op jit(solution)/shard_map/ppermute | solution.py:256
  121.5 0.1 reshape.98
  121.6 0.1 reduce_sum.48
  121.6 0.1 reshape.99
  121.7 24.9 %all-to-all-done.2 = f32[128,6,128]{2,1,0:T(8,128)} async-done(((f32[128,6,128]{2,1,0:T(8,128)}), f32[128,6,128]{2,1,0:T(8,128)}, u32[]{:S(2)}, u32[]{:S(2)}) %all-to-all-start.2) | async-done | bytes 393248 | tf_op jit(solution)/shard_map/all_to_all | solution.py:260
  146.6 1.2 slice_reduce_fusion
  147.8 0.8 multiply_reduce_fusion.1
  148.6 0.1 maximum_bitcast_fusion
  148.7 0.8 broadcast_in_dim.34
  149.5 9.9 %all-to-all-start.3 = ((f32[256,2,128]{2,1,0:T(2,128)}), f32[256,2,128]{2,1,0:T(2,128)}, u32[]{:S(2)}, u32[]{:S(2)}) async-start(f32[256,2,128]{2,1,0:T(2,128)} %broadcast_in_dim.34), calls=%async_computation.3 | async-start | bytes 524288 | tf_op jit(solution)/shard_map/all_to_all | solution.py:260
  159.4 0.1 slice.52
  159.5 0.1 slice.53
  159.5 0.1 pad_maximum_fusion.3.taps_ref
  159.6 1.1 slice.63
  160.7 0.0 copy-start.4
  160.8 1.2 copy-done.4
  162.0 6.7 %shard_map.115 = bf16[128,4096]{1,0:T(8,128)(2,1)} custom-call(f32[128,4096]{1,0:T(8,128)S(1)} %copy-done.2, bf16[128,4096]{1,0:T(8,128)(2,1)S(1)} %bitcast.39, f32[128,128]{1,0:T(8,128)S(1)} %get-tuple-element.44.filt_ref, f32[2048,128]{1,0:T(8,128)S(1)} %copy-done.4, f32[512,128]{1,0:T(8,128)S(1)} %bitcast.42), custom_call_target="tpu_custom_call" | custom-call | flops 1073741824 | bytes 4521984 | tf_op jit(solution)/shard_map/pallas_call | solution.py:235
  168.7 8.4 %shard_map.116 = bf16[128,4096]{1,0:T(8,128)(2,1)} custom-call(bf16[128,4096]{1,0:T(8,128)(2,1)S(1)} %copy-done.9, bf16[128,4096]{1,0:T(8,128)(2,1)} %collective-permute-done.1.before_ref, f32[128,128]{1,0:T(8,128)S(1)} %pad_maximum_fusion.3.taps_ref, bf16[128,4096]{1,0:T(8,128)(2,1)S(1)} %bitcast.40), custom_call_target="tpu_custom_call" | custom-call | flops 1073741824 | bytes 3211264 | tf_op jit(solution)/shard_map/pallas_call | solution.py:235
  177.1 1.2 reshape.100
  178.3 0.6 slice_multiply_fusion
  178.9 0.1 fusion.2
  179.0 0.1 copy.63
  179.0 0.1 reshape.101
  179.2 0.2 copy.59
  179.4 0.1 copy.61
  179.5 0.7 multiply_multiply_fusion
  (35 shorter events, 0.1 us)
Async XLA Ops:
  0.6 7.0 %copy-start.16 = (f32[128,16]{0,1:T(8,128)S(1)}, f32[128,16]{0,1:T(8,128)}, u32[]{:S(2)}) copy-start(f32[128,16]{0,1:T(8,128)} %param.12) | copy-start | bytes 24580
  0.6 7.0 %copy-start.17 = (f32[128,16]{0,1:T(8,128)S(1)}, f32[128,16]{0,1:T(8,128)}, u32[]{:S(2)}) copy-start(f32[128,16]{0,1:T(8,128)} %param.11) | copy-start | bytes 24580
  2.5 37.9 %collective-permute-start = (bf16[128,4096]{1,0:T(8,128)(2,1)S(1)}, bf16[128,4096]{1,0:T(8,128)(2,1)}, u32[]{:S(2)}, u32[]{:S(2)}) collective-permute-start(bf16[128,4096]{1,0:T(8,128)(2,1)S(1)} %fusion.own_ref), channel_id=1, source_target_pairs={{1,0},{2,1},{3,2},{4,3},{5,4},{6,5},{7,6},{8,7},{9,8},{10,9},{11,1... | collective-permute-start | bytes 3145736 | tf_op jit(solution)/shard_map/ppermute | solution.py:256
  7.8 0.6 copy-start.14
  8.0 0.6 copy-start.15
  8.6 2.0 %copy-start = (bf16[1,128,4096]{2,1,0:T(8,128)(2,1)S(1)}, bf16[1,128,4096]{2,1,0:T(8,128)(2,1)}, u32[]{:S(2)}) copy-start(bf16[1,128,4096]{2,1,0:T(8,128)(2,1)} %param.7) | copy-start | bytes 3145732
  10.6 29.8 %copy-start.1 = (bf16[1,128,4096]{2,1,0:T(8,128)(2,1)S(1)}, bf16[1,128,4096]{2,1,0:T(8,128)(2,1)}, u32[]{:S(2)}) copy-start(bf16[1,128,4096]{2,1,0:T(8,128)(2,1)} %param.8) | copy-start | bytes 3145732
  10.6 29.8 %copy-start.10 = (f32[128,128]{1,0:T(8,128)S(1)}, f32[128,128]{1,0:T(8,128)}, u32[]{:S(2)}) copy-start(f32[128,128]{1,0:T(8,128)} %taps_ref.1) | copy-start | bytes 196612
  14.0 24.5 %all-to-all-start = ((f32[128,4,128]{2,1,0:T(4,128)}), f32[128,4,128]{2,1,0:T(4,128)S(1)}, u32[]{:S(2)}, u32[]{:S(2)}) async-start(f32[128,4,128]{2,1,0:T(4,128)} %bitcast.4), calls=%async_computation | async-start | bytes 524288 | tf_op jit(solution)/shard_map/all_to_all | solution.py:260
  38.5 0.7 copy-start.6
  39.2 0.9 copy-start.7
  40.4 1.2 copy-start.5
  62.4 7.7 %copy-start.12 = (f32[128,128]{1,0:T(8,128)}, f32[128,128]{1,0:T(8,128)S(1)}, u32[]{:S(2)}) copy-start(f32[128,128]{1,0:T(8,128)S(1)} %get-tuple-element.17) | copy-start | bytes 196612
  63.3 24.9 %all-to-all-start.1 = ((f32[128,8,128]{2,1,0:T(8,128)}), f32[128,8,128]{2,1,0:T(8,128)}, u32[]{:S(2)}, u32[]{:S(2)}) async-start(f32[128,8,128]{2,1,0:T(8,128)} %pad_maximum_fusion), calls=%async_computation.1 | async-start | bytes 1048576 | tf_op jit(solution)/shard_map/all_to_all | solution.py:260
  90.6 0.8 copy-start.11
  91.4 18.0 %copy-start.13 = (f32[128,128]{1,0:T(8,128)S(1)}, f32[128,128]{1,0:T(8,128)}, u32[]{:S(2)}) copy-start(f32[128,128]{1,0:T(8,128)} %copy-done.12) | copy-start | bytes 196612
  108.4 1.0 copy-start.8
  109.4 51.3 %copy-start.2 = (f32[128,4096]{1,0:T(8,128)S(1)}, f32[128,4096]{1,0:T(8,128)}, u32[]{:S(2)}) copy-start(f32[128,4096]{1,0:T(8,128)} %get-tuple-element.13.gm_ref) | copy-start | bytes 6291460
  110.4 36.3 %all-to-all-start.2 = ((f32[128,6,128]{2,1,0:T(8,128)}), f32[128,6,128]{2,1,0:T(8,128)}, u32[]{:S(2)}, u32[]{:S(2)}) async-start(f32[128,6,128]{2,1,0:T(8,128)} %pad_maximum_fusion.1), calls=%async_computation.2 | async-start | bytes 1048576 | tf_op jit(solution)/shard_map/all_to_all | solution.py:260
  117.7 50.9 %collective-permute-start.1 = (bf16[128,4096]{1,0:T(8,128)(2,1)}, bf16[128,4096]{1,0:T(8,128)(2,1)}, u32[]{:S(2)}, u32[]{:S(2)}) collective-permute-start(bf16[128,4096]{1,0:T(8,128)(2,1)} %copy-done.8), channel_id=1, source_target_pairs={{0,1},{1,2},{2,3},{3,4},{4,5},{5,6},{6,7},{7,8},{8,9},{9,10},{10,1... | collective-permute-start | bytes 3145736 | tf_op jit(solution)/shard_map/ppermute | solution.py:256
  149.5 27.6 %all-to-all-start.3 = ((f32[256,2,128]{2,1,0:T(2,128)}), f32[256,2,128]{2,1,0:T(2,128)}, u32[]{:S(2)}, u32[]{:S(2)}) async-start(f32[256,2,128]{2,1,0:T(2,128)} %broadcast_in_dim.34), calls=%async_computation.3 | async-start | bytes 524288 | tf_op jit(solution)/shard_map/all_to_all | solution.py:260
  160.7 1.2 copy-start.4
  162.0 6.7 %copy-start.3 = (bf16[1,128,4096]{2,1,0:T(8,128)(2,1)S(1)}, bf16[1,128,4096]{2,1,0:T(8,128)(2,1)}, u32[]{:S(2)}) copy-start(bf16[1,128,4096]{2,1,0:T(8,128)(2,1)} %param.10) | copy-start | bytes 3145732
  162.0 6.7 %copy-start.9 = (bf16[128,4096]{1,0:T(8,128)(2,1)S(1)}, bf16[128,4096]{1,0:T(8,128)(2,1)}, u32[]{:S(2)}) copy-start(bf16[128,4096]{1,0:T(8,128)(2,1)} %copy-done.8) | copy-start | bytes 3145732

commit v2 on v1

v2 whole, which is shorter than its diff:
```python
import functools
import math

import jax
import jax.numpy as jnp
from jax import lax
from jax.experimental import pallas as pl
from jax.experimental.pallas import tpu as pltpu
from jax.sharding import PartitionSpec as P

F32 = jnp.float32
BF16 = jnp.bfloat16
LANES = 128
NN = (((1,), (0,)), ((), ()))
NT = (((1,), (1,)), ((), ()))
TN = (((0,), (0,)), ((), ()))
VMEM_LIMIT = 60 * 1024 * 1024


def dot(left, right, dims=NN):
    return lax.dot_general(left, right, dims, preferred_element_type=F32)


def split(x):
    high = x.astype(BF16)
    return high, (x - high.astype(F32)).astype(BF16)


def iota(shape, dim):
    return lax.broadcasted_iota(jnp.int32, shape, dim)


def roll_left(x, amount):
    return pltpu.roll(x, x.shape[1] - amount, 1)


def pick_groups(stacked, rows, size):
    lane_group = iota((rows, LANES), 1) // size
    out = stacked[:rows]
    for g in range(1, LANES // size):
        out = jnp.where(lane_group == g, stacked[g * rows : (g + 1) * rows], out)
    return out


def spread_groups(x, size):
    lane_group = iota(x.shape, 1) // size
    zero = jnp.zeros_like(x)
    return jnp.concatenate(
        [jnp.where(lane_group == g, x, zero) for g in range(LANES // size)], axis=0
    )


def circulant(row):
    return split(pltpu.roll(jnp.broadcast_to(row, (LANES, LANES)), 0, 1, stride=1, stride_axis=0))


def masked(row, keeps):
    parts = circulant(row)
    zero = jnp.zeros_like(parts[0])
    return jnp.concatenate([jnp.where(keep, part, zero) for part in parts for keep in keeps], axis=1)


def toeplitz(rows_ref, i, per, keeps):
    return jnp.concatenate(
        [masked(rows_ref[i * per + g : i * per + g + 1, :], keeps) for g in range(per)], axis=0
    )


def lag_rows(z):
    sums = [None] * 4
    for k in range(LANES // 8):
        part = z[8 * k : 8 * k + 8]
        part = roll_left(part, 8 * k) if k else part
        sums[k % 4] = part if sums[k % 4] is None else sums[k % 4] + part
    return (sums[0] + sums[1]) + (sums[2] + sums[3])


def lag_sums(rows):
    rows = jnp.concatenate(rows, axis=0)
    sub = iota(rows.shape, 0)
    for bit in (4, 2, 1):
        rows = jnp.where((sub & bit) != 0, roll_left(rows, bit), rows)
    return jnp.sum(rows.reshape(-1, 8, LANES), axis=1)


def carried_part(table, entering, size):
    high, low = (spread_groups(part, size) for part in split(entering))
    return dot(
        jnp.concatenate([table, table], axis=1), jnp.concatenate([high, high, low, low], axis=0)
    )


def states_of(ref, i, modes):
    return jnp.concatenate(
        [ref[i * 2 * modes + k : i * 2 * modes + k + 4, :] for k in range(0, 2 * modes, 8)], axis=0
    )


def mode_sums(table, x, size, modes):
    high, low = split(table)
    if x.dtype == BF16:
        prod = dot(jnp.concatenate([high, low], axis=0), x)
    else:
        left = jnp.concatenate(
            [jnp.concatenate([high, high], axis=1), jnp.concatenate([low, low], axis=1)], axis=0
        )
        prod = dot(left, jnp.concatenate(split(x), axis=0))
    half = prod.shape[0] // 2
    return pick_groups(prod[:half] + prod[half:], modes, size)


def tiles_of(ref):
    return [slice(i * LANES, (i + 1) * LANES) for i in range(ref.shape[1] // LANES)]


def states_kernel(size, modes, x_ref, table_ref, out_ref):
    rows = LANES // size * modes
    out = [
        mode_sums(table_ref[i * rows : (i + 1) * rows, :], x_ref[:, lanes], size, modes)
        for i, lanes in enumerate(tiles_of(x_ref))
    ]
    out_ref[...] = jnp.concatenate(out, axis=0)


def mixer_back_kernel(
    size, modes, own_ref, next_ref, gate_ref, x_ref, taps_ref, table_ref, gm_ref, out_ref, lag_ref
):
    per = LANES // size
    rows = per * modes
    row, col = iota((LANES, LANES), 0), iota((LANES, LANES), 1)
    tiles = tiles_of(x_ref)
    cots, out, lag_parts = [], [], []
    for i, lanes in enumerate(tiles):
        own, after = own_ref[:, lanes], next_ref[:, lanes]
        left = toeplitz(taps_ref, i, per, [col >= row, col < row])
        prod = dot(left, jnp.concatenate([own, after, own, after], axis=0))
        grad_mixer = pick_groups(prod, LANES, size)
        gm_ref[:, lanes] = grad_mixer
        cots.append(grad_mixer * gate_ref[:, lanes].astype(F32))
    for i, lanes in enumerate(tiles):
        out.append(mode_sums(table_ref[i * rows : (i + 1) * rows, :], cots[i], size, modes))
    for i, lanes in enumerate(tiles):
        pairs = dot(spread_groups(x_ref[:, lanes], size), cots[i].astype(BF16), NT)
        for g in range(per):
            lag_parts.append(lag_rows(jnp.where(col >= row, pairs[g * LANES : (g + 1) * LANES], 0.0)))
    out_ref[...] = jnp.concatenate(out, axis=0)
    lag_ref[...] = lag_sums(lag_parts)


def values_kernel(
    size, modes, x_ref, gate_ref, gm_ref, own_ref, next_ref, filt_ref, table_ref, enter_ref,
    mix_ref, ggl_ref, lag_ref,
):
    per = LANES // size
    row, col = iota((LANES, LANES), 0), iota((LANES, LANES), 1)
    tiles = tiles_of(x_ref)
    values, mixes, lag_parts = [], [], []
    for i, lanes in enumerate(tiles):
        values.append(
            carried_part(
                table_ref[i * LANES : (i + 1) * LANES, :], states_of(enter_ref, i, modes), size
            )
        )
    for i, lanes in enumerate(tiles):
        x = x_ref[:, lanes]
        prod = dot(toeplitz(filt_ref, i, per, [col <= row]), jnp.concatenate([x, x], axis=0))
        full = pick_groups(prod, LANES, size) + values[i]
        ggl_ref[:, lanes] = (gm_ref[:, lanes] * full).astype(BF16)
        mixes.append((gate_ref[:, lanes].astype(F32) * full).astype(BF16))
    for i, lanes in enumerate(tiles):
        mix_ref[:, lanes] = mixes[i]
        both = jnp.concatenate([own_ref[:, lanes], next_ref[:, lanes]], axis=0)
        pairs = dot(spread_groups(mixes[i], size), both, NT)
        for g in range(per):
            z = pairs[g * LANES : (g + 1) * LANES]
            lag_parts.append(lag_rows(jnp.where(col >= row, z[:, :LANES], z[:, LANES:])))
    lag_ref[...] = lag_sums(lag_parts)


def input_grad_kernel(size, modes, gm_ref, gate_ref, filt_ref, table_ref, enter_ref, out_ref):
    per = LANES // size
    row, col = iota((LANES, LANES), 0), iota((LANES, LANES), 1)
    for i, lanes in enumerate(tiles_of(gm_ref)):
        left = toeplitz(filt_ref, i, per, [col >= row])
        high, low = split(gm_ref[:, lanes] * gate_ref[:, lanes].astype(F32))
        prod = dot(
            jnp.concatenate([left, left[:, :LANES]], axis=1), jnp.concatenate([high, high, low], axis=0)
        )
        out_ref[:, lanes] = (
            pick_groups(prod, LANES, size)
            + carried_part(
                table_ref[i * LANES : (i + 1) * LANES, :], states_of(enter_ref, i, modes), size
            )
        ).astype(BF16)


def mixer_kernel(size, own_ref, before_ref, taps_ref, cot_ref, out_ref):
    per = LANES // size
    row, col = iota((LANES, LANES), 0), iota((LANES, LANES), 1)
    for i, lanes in enumerate(tiles_of(own_ref)):
        own, before = own_ref[:, lanes], before_ref[:, lanes]
        left = toeplitz(taps_ref, i, per, [col <= row, col > row])
        prod = dot(left, jnp.concatenate([own, before, own, before], axis=0))
        mixed = pick_groups(prod, LANES, size)
        out_ref[:, lanes] = (cot_ref[:, lanes].astype(F32) * mixed).astype(BF16)


def scan_kernel(x_ref, decay_ref, beside_ref, out_ref):
    decay = decay_ref[...]
    rows = decay.shape[0]
    state = jnp.zeros_like(decay)
    for d in range(x_ref.shape[0]):
        out_ref[d, :rows, :] = state
        out_ref[d, rows:, :] = beside_ref[d]
        state = decay * state + x_ref[d]


def back_scan_kernel(x_ref, decay_ref, front_ref, tap_ref, cot_ref, out_ref, sum_ref):
    decay = decay_ref[...]
    rows = decay.shape[0]
    per = tap_ref.shape[0] // x_ref.shape[0]
    state = jnp.zeros_like(decay)
    total = jnp.zeros_like(decay)
    rest = jnp.zeros((rows - 2 * per, LANES), F32)
    for d in reversed(range(x_ref.shape[0])):
        x = x_ref[d, rows:, :]
        out_ref[d, :rows, :] = state
        out_ref[d, rows:, :] = jnp.concatenate(
            [tap_ref[d * per : (d + 1) * per, :], cot_ref[d * per : (d + 1) * per, :], rest], axis=0
        )
        state = decay * state + x
        total = total + x * front_ref[d, :rows, :]
    sum_ref[...] = total


def collect_kernel(size, x_ref, sum_ref, lam_ref, out_ref):
    rows, modes = sum_ref.shape[0], lam_ref.shape[0]
    lags = jnp.sum(x_ref[:, rows:, :], axis=0)
    exact = functools.partial(
        lax.dot_general, precision=lax.Precision.HIGHEST, preferred_element_type=F32
    )
    lam = jnp.concatenate([lam_ref[...], jnp.zeros((LANES - modes, LANES), F32)], axis=0)
    second = exact(jnp.broadcast_to(lags[1:2], (8, LANES)), lam, NT)[:1]
    lane, place = iota((LANES, LANES), 0), iota((LANES, LANES), 1)
    per = LANES // size
    for q in range(rows):
        pick = (place == modes + q * per + lane // size).astype(F32)
        second = second + exact(jnp.broadcast_to(sum_ref[q : q + 1, :], (8, LANES)), pick, NN)[:1]
    message = jnp.concatenate([lags[:1], second], axis=0)
    out_ref[...] = jnp.broadcast_to(message[None], out_ref.shape)


def call(body, width, step, chunk, specs, outs, args, micros):
    kinds = list(specs) + [rows for rows, kind in outs]
    chunks = step // chunk

    def kernel(*refs):
        def part(c, carry):
            views = []
            for ref, rows in zip(refs, kinds):
                if rows is None:
                    views.append(ref.at[:, pl.ds(pl.multiple_of(c * chunk, chunk), chunk)])
                else:
                    views.append(ref.at[pl.ds(pl.multiple_of(c * rows, rows), rows), :])
            body(*views)
            return carry

        lax.fori_loop(0, chunks, part, 0)

    def block(rows):
        if rows is None:
            return pl.BlockSpec((LANES, step), lambda i: (0, i))
        return pl.BlockSpec((rows * chunks, LANES), lambda i: (i, 0))

    def shape(rows, kind):
        if rows is None:
            return jax.ShapeDtypeStruct((LANES, width), kind)
        return jax.ShapeDtypeStruct((rows * (width // chunk), LANES), kind)

    nbytes = sum(a.size * a.dtype.itemsize for a in args)
    return pl.pallas_call(
        kernel,
        grid=(width // step,),
        in_specs=[block(rows) for rows in specs],
        out_specs=[block(rows) for rows, kind in outs],
        out_shape=[shape(rows, kind) for rows, kind in outs],
        compiler_params=pltpu.CompilerParams(vmem_limit_bytes=VMEM_LIMIT),
        cost_estimate=pl.CostEstimate(flops=micros * 1_000_000_000, bytes_accessed=nbytes, transcendentals=0),
    )(*args)


def whole(body, outs, args):
    return pl.pallas_call(
        body,
        out_shape=[jax.ShapeDtypeStruct(s, F32) for s in outs],
        compiler_params=pltpu.CompilerParams(vmem_limit_bytes=VMEM_LIMIT),
    )(*args)


def shifted(x, by):
    count = lax.axis_size("ctx")
    return lax.ppermute(x, "ctx", [(i, i + by) for i in range(count) if 0 <= i + by < count])


def exchange(x, axes="ctx"):
    return lax.all_to_all(x, axes, split_axis=0, concat_axis=0, tiled=True)


def carry_table(x):
    return jnp.concatenate(split(x), axis=2).reshape(-1, 2 * x.shape[2])


def on_device(inputs, gate_li, gate_mr, cotangent, residues, rates, taps):
    seq, gate, cot = inputs[0], gate_li[0], cotangent[0]
    width = seq.shape[1]
    groups, modes = rates.shape
    size = width // groups
    per = LANES // size
    tiles = width // LANES
    reps, count = lax.axis_size("rep"), lax.axis_size("ctx")
    me = lax.axis_index("ctx")
    own_rows = tiles * modes // count
    step, chunk = min(2048, width), min(1024, width)
    state_rows = chunk // LANES * modes
    table_rows = per * state_rows
    group_rows = chunk // size
    carry_rows = chunk

    scaled = (cot.astype(F32) * gate_mr[0].astype(F32)).astype(BF16)
    after = shifted(scaled, -1)

    lags = jnp.arange(LANES).astype(F32)
    norm = jnp.sqrt(-jnp.expm1(-2.0 * rates))
    weight = residues * norm
    rate3, weight3 = rates[:, :, None], weight[:, :, None]
    lam = jnp.exp(-rate3 * lags)
    filt = jnp.sum(weight3 * lam, axis=1)
    filt_back = jnp.roll(jnp.flip(filt, 1), 1, axis=1)
    taps_back = jnp.roll(jnp.flip(taps, 1), 1, axis=1)
    to_end = jnp.exp(-rate3 * (LANES - 1.0 - lags))
    from_start = jnp.exp(-rate3 * (lags + 1.0))
    flat = (groups * modes, LANES)
    end_table = to_end.reshape(flat)
    start_table = from_start.reshape(flat)
    rate_row = rates.reshape(tiles, 1, per * modes)
    weight_row = weight.reshape(tiles, 1, per * modes)
    front_table = carry_table(weight_row * jnp.exp(-rate_row * (lags[:, None] + 1.0)))
    back_table = carry_table(weight_row * jnp.exp(-rate_row * (LANES - 1.0 - lags[:, None])))
    decay = jnp.exp(-rates * LANES).reshape(tiles, per, modes)
    decay = jnp.repeat(jnp.swapaxes(decay, 1, 2).reshape(tiles * modes, per), size, axis=1)
    decay = lax.dynamic_slice_in_dim(decay, me * own_rows, own_rows, 0)

    bind = functools.partial
    states = call(
        bind(states_kernel, size, modes), width, step, chunk, [None, table_rows], [(state_rows, F32)],
        [seq, end_table], 3,
    )[0]
    ends = exchange(states.reshape(count, own_rows, LANES))

    grad_mixer, back_states, lag_cot = call(
        bind(mixer_back_kernel, size, modes), width, step, chunk,
        [None, None, None, None, group_rows, table_rows],
        [(None, F32), (state_rows, F32), (group_rows, F32)],
        [scaled, after, gate, seq, taps, start_table], 11,
    )
    first = whole(
        scan_kernel, [(count, 2 * own_rows, LANES)],
        [ends, decay, back_states.reshape(count, own_rows, LANES)],
    )[0]
    second = exchange(first)
    mixer_in, grad_gate_li, lag_taps = call(
        bind(values_kernel, size, modes), width, step, chunk,
        [None, None, None, None, None, group_rows, carry_rows, 2 * state_rows],
        [(None, BF16), (None, BF16), (group_rows, F32)],
        [seq, gate, grad_mixer, scaled, after, filt_back, front_table, second.reshape(-1, LANES)], 10,
    )
    before = shifted(mixer_in, 1)
    message, state_sums = whole(
        back_scan_kernel, [first.shape, decay.shape], [second, decay, first, lag_taps, lag_cot]
    )
    third = exchange(message)
    own_groups = groups // count
    lam_own = lax.dynamic_slice_in_dim(lam, me * own_groups, own_groups, 0).reshape(modes, LANES)
    spread = whole(
        bind(collect_kernel, size), [(reps * count, 2, LANES)], [third, state_sums, lam_own]
    )[0]
    got = exchange(spread, ("rep", "ctx"))
    grad_inputs = call(
        bind(input_grad_kernel, size, modes), width, step, chunk,
        [None, None, group_rows, carry_rows, 2 * state_rows], [(None, BF16)],
        [grad_mixer, gate, filt, back_table, third.reshape(-1, LANES)], 6,
    )[0]
    grad_gate_mr = call(
        bind(mixer_kernel, size), width, step, chunk, [None, None, group_rows, None], [(None, BF16)],
        [mixer_in, before, taps_back, cot], 7,
    )[0]
    got = jnp.sum(got.reshape(reps, count, 2, LANES), axis=0)
    local_all = got[:, 1, :modes]
    first_all = got[:, 1, modes : modes + own_rows * per].reshape(tiles, modes, per)
    first_all = jnp.swapaxes(first_all, 1, 2).reshape(groups, modes)
    scale = 1.0 / math.sqrt(reps * count * LANES)
    return (
        grad_inputs[None],
        grad_gate_li[None],
        grad_gate_mr[None],
        norm * (first_all + local_all) * scale,
        got[:, 0] * scale,
    )


def solution(mesh):
    big = P("rep", "ctx", None)
    return jax.shard_map(
        on_device,
        mesh=mesh,
        in_specs=(big, big, big, big, P(), P(), P()),
        out_specs=(big, big, big, P(), P()),
        check_vma=False,
    )
```

time: 181 us -> 151 us (0.83)
  waiting for transfers between devices: 48 us -> 35 us
  Pallas kernels: 57.9 us -> 46.2 us
  local copies, waits for them, and re-layouts: 16 us -> 7.12 us
  starting transfers between devices: 44.2 us -> 49 us
    pallas_call x5, Pallas kernels: 56.3 us -> 39.4 us  [call(): pl.pallas_call(kernel, grid=(width // step,), in_specs=[block(rows) for r...]
    all_to_all x4, waiting for transfers between devices: 48 us -> 35 us  [exchange(): return lax.all_to_all(x, axes, split_axis=0, concat_axis=0, tiled=True)]
    pallas_call x2 -> x3, Pallas kernels: 1.58 us -> 6.83 us  [whole(): pl.pallas_call(body, out_shape=[jax.ShapeDtypeStruct(s, F32) for s in out...]
    all_to_all x4, starting transfers between devices: 35.3 us -> 40.4 us  [exchange(): return lax.all_to_all(x, axes, split_axis=0, concat_axis=0, tiled=True)]
    unnamed x38 -> x20, local copies, waits for them, and re-layouts: 6.59 us -> 3.99 us
    slice x2, local copies, waits for them, and re-layouts: 2.27 us -> 0.16 us  [on_device(): filt_back = jnp.roll(jnp.flip(filt, 1), 1, axis=1)]
    slice x3 -> x1, local copies, waits for them, and re-layouts: 2.24 us -> 0.3 us  [on_device(): local_all = got[:, 1, :modes]]
    reduce_sum x4 -> x1, other arithmetic: 2.1 us -> 0.18 us  [on_device(): got = jnp.sum(got.reshape(reps, count, 2, LANES), axis=0)]
  transfers between devices with their start and end apart: 6 -> 6, of which waited for: 3 -> 3; matrix products, arithmetic and copies ran while one was open for 8% -> 8% of each run, Pallas kernels for 10% -> 21%
where the time goes in v2:
time: 151 us
  starting transfers between devices  49 us (32%)
  Pallas kernels  46.2 us (31%)
  waiting for transfers between devices  35 us (23%)
  other arithmetic  12.6 us (8%)
  local copies, waits for them, and re-layouts  7.12 us (5%)
    all_to_all x4, starting transfers between devices, exchange(): return lax.all_to_all(x, axes, split_axis=0, concat_axis=0, tiled=True)  40.4 us
    pallas_call x5, Pallas kernels, call(): pl.pallas_call(kernel, grid=(width // step,), in_specs=[block(rows) for r...  39.4 us
    all_to_all x4, waiting for transfers between devices, exchange(): return lax.all_to_all(x, axes, split_axis=0, concat_axis=0, tiled=True)  35 us
    ppermute x2, starting transfers between devices, shifted(): lax.ppermute(x, 'ctx', [(i, i + by) for i in range(count) if 0 <= i + by...  8.68 us
    pallas_call x3, Pallas kernels, whole(): pl.pallas_call(body, out_shape=[jax.ShapeDtypeStruct(s, F32) for s in out...  6.83 us
    unnamed x20, local copies, waits for them, and re-layouts  3.99 us
    concatenate x2, other arithmetic, carry_table(): return jnp.concatenate(split(x), axis=2).reshape(-1, 2 * x.shape[2])  3.09 us
  transfers between devices with their start and end apart: 6, of which 3 were waited for; matrix products, arithmetic and copies ran while one was open for 8% of the time, Pallas kernels for 21%

profile of v2, /device:TPU:1, one launch (start us, length us, event | category | flops | bytes accessed | tf_op | source)
XLA Modules:
  0.0 150.9 jit_solution(2391090399644145815)
XLA Ops:
  0.6 0.0 copy-start.6
  0.6 0.0 copy-start.7
  0.7 1.8 %fusion.8.refs_0_.refs_3_ = bf16[128,4096]{1,0:T(8,128)(2,1)S(1)} fusion(bf16[1,128,4096]{2,1,0:T(8,128)(2,1)} %param.9, bf16[1,128,4096]{2,1,0:T(8,128)(2,1)} %param.10), kind=kLoop, calls=%fused_computation.13 | loop fusion | flops 2097152 | bytes 3145728 | tf_op jit(solution)/shard_map/convert_element_type | solution.py:329
  2.5 0.0 copy-start.2
  2.5 5.1 %collective-permute-start = (bf16[128,4096]{1,0:T(8,128)(2,1)S(1)}, bf16[128,4096]{1,0:T(8,128)(2,1)S(1)}, u32[]{:S(2)}, u32[]{:S(2)}) collective-permute-start(bf16[128,4096]{1,0:T(8,128)(2,1)S(1)} %fusion.8.refs_0_.refs_3_), channel_id=1, source_target_pairs={{1,0},{2,1},{3,2},{4,3},{5,4},{6,5},{7,6},{8,7},{9,8},{10,9},{11,1... | collective-permute-start | bytes 3145736 | tf_op jit(solution)/shard_map/ppermute | solution.py:302
  7.6 0.0 copy-done.6
  7.6 0.0 copy-done.7
  7.7 0.1 copy.50
  7.8 0.1 mul.149
  7.9 1.7 %multiply_exponential_fusion = (f32[2048,128]{1,0:T(8,128)}, f32[2048,128]{1,0:T(8,128)}) fusion(f32[128]{0:T(128)S(1)} %get-tuple-element.56, f32[2048]{0:T(1024)S(1)} %mul.149, f32[128]{0:T(128)S(1)} %get-tuple-element.57), kind=kLoop, calls=%fused_computation.16 | loop fusion | flops 524288 | bytes 2106368 | tf_op jit(solution)/shard_map/exp | solution.py:340
  9.5 2.8 %shard_map.111 = f32[512,128]{1,0:T(8,128)} custom-call(bf16[128,4096]{1,0:T(8,128)(2,1)} %bitcast.97, f32[2048,128]{1,0:T(8,128)} %get-tuple-element.54.refs_1_), custom_call_target="tpu_custom_call" | custom-call | flops 3000000000 | bytes 2097152 | tf_op jit(solution)/shard_map/pallas_call | solution.py:281
  12.3 0.0 copy-done.2
  12.3 10.7 %all-to-all-start = ((f32[128,4,128]{2,1,0:T(4,128)}), f32[128,4,128]{2,1,0:T(4,128)S(1)}, u32[]{:S(2)}, u32[]{:S(2)}) async-start(f32[128,4,128]{2,1,0:T(4,128)} %bitcast.93), calls=%async_computation | async-start | bytes 524288 | tf_op jit(solution)/shard_map/all_to_all | solution.py:306
  23.0 0.1 copy.55
  23.1 0.1 reshape.105
  23.2 0.1 copy.51
  23.3 0.1 constant_dynamic-slice_fusion
  23.4 0.7 copy.61.decay_ref
  24.1 0.0 collective-permute-done.refs_1_.refs_4_
  24.1 1.0 copy-done.8
  25.1 12.0 %shard_map.110 = (f32[128,4096]{1,0:T(8,128)}, f32[512,128]{1,0:T(8,128)}, f32[128,128]{1,0:T(8,128)}) custom-call(bf16[128,4096]{1,0:T(8,128)(2,1)} %copy-done.2, bf16[128,4096]{1,0:T(8,128)(2,1)} %copy-done.8, bf16[128,4096]{1,0:T(8,128)(2,1)} %bitcast.100, bf16[128,4096]{1,0:T(8,128)(2,1)} %bitcast.98, f32[128,128]{1,0:T(8,128)} %refs_4_.1, ...), custom_call_target="tpu_custom_call" | custom-call | flops 11000000512 | bytes 5308416 | tf_op jit(solution)/shard_map/pallas_call | solution.py:281
  37.0 0.0 all-to-all-done.x_ref
  37.1 0.0 copy-start.3
  37.1 0.7 copy-done.3
  37.8 2.1 %shard_map.112.front_ref = f32[128,8,128]{2,1,0:T(8,128)} custom-call(f32[128,4,128]{2,1,0:T(4,128)} %copy-done.3, f32[4,128]{1,0:T(4,128)} %copy.61.decay_ref, f32[128,4,128]{2,1,0:T(4,128)} %bitcast.95), custom_call_target="tpu_custom_call" | custom-call | tf_op jit(solution)/shard_map/pallas_call | solution.py:293
  39.9 14.0 %all-to-all-start.1 = ((f32[128,8,128]{2,1,0:T(8,128)}), f32[128,8,128]{2,1,0:T(8,128)S(1)}, u32[]{:S(2)}, u32[]{:S(2)}) async-start(f32[128,8,128]{2,1,0:T(8,128)} %shard_map.112.front_ref), calls=%async_computation.1 | async-start | bytes 1048576 | tf_op jit(solution)/shard_map/all_to_all | solution.py:306
  53.9 1.6 %multiply_exponential_fusion.1 = (f32[128,16,128]{2,1,0:T(8,128)}, f32[128,128]{1,0:T(8,128)S(1)}) fusion(f32[128]{0:T(128)S(1)} %iota_convert_fusion, f32[128,16]{1,0:T(8,128)S(1)} %copy.50, f32[128,16]{1,0:T(8,128)S(1)} %copy.51), kind=kLoop, calls=%fused_computation.18 | loop fusion | flops 770048 | bytes 1131008 | tf_op jit(solution)/shard_map/exp | solution.py:336
  55.5 0.1 neg.22
  55.6 0.1 mul.161
  55.7 0.1 slice.41
  55.8 0.1 slice.33
  55.9 1.4 fusion.6
  57.3 0.0 copy-done.4
  57.3 0.7 pad_maximum_fusion.2.refs_5_
  58.1 1.5 %pad_maximum_fusion.1.refs_6_ = bf16[4096,128]{1,0:T(8,128)(2,1)} fusion(bf16[4096,64]{1,0:T(8,128)(2,1)S(1)} %get-tuple-element.46, bf16[4096,64]{1,0:T(8,128)(2,1)S(1)} %get-tuple-element.45), kind=kLoop, calls=%fused_computation.15 | loop fusion | flops 2097152 | bytes 2097152 | tf_op jit(solution)/shard_map/concatenate | solution.py:310
  59.6 12.6 %all-to-all-done.1.x_ref = f32[128,8,128]{2,1,0:T(8,128)S(1)} async-done(((f32[128,8,128]{2,1,0:T(8,128)}), f32[128,8,128]{2,1,0:T(8,128)S(1)}, u32[]{:S(2)}, u32[]{:S(2)}) %all-to-all-start.1) | async-done | bytes 524320 | tf_op jit(solution)/shard_map/all_to_all | solution.py:306
  72.2 0.8 copy-done
  73.0 10.0 %shard_map.113 = (bf16[128,4096]{1,0:T(8,128)(2,1)}, bf16[128,4096]{1,0:T(8,128)(2,1)}, f32[128,128]{1,0:T(8,128)}) custom-call(bf16[128,4096]{1,0:T(8,128)(2,1)} %bitcast.99, bf16[128,4096]{1,0:T(8,128)(2,1)} %bitcast.101, f32[128,4096]{1,0:T(8,128)} %get-tuple-element.13.refs_2_.refs_0_, bf16[128,4096]{1,0:T(8,128)(2,1)} %copy-done.2, ...), custom_call_target="tpu_custom_call" | custom-call | flops 10000000000 | bytes 7929856 | tf_op jit(solution)/shard_map/pallas_call | solution.py:281
  83.0 0.0 copy-start.5
  83.0 2.4 %shard_map.114 = (f32[128,8,128]{2,1,0:T(8,128)}, f32[4,128]{1,0:T(4,128)}) custom-call(f32[128,8,128]{2,1,0:T(8,128)} %copy-done, f32[4,128]{1,0:T(4,128)} %copy.61.decay_ref, f32[128,8,128]{2,1,0:T(8,128)} %shard_map.112.front_ref, f32[128,128]{1,0:T(8,128)} %get-tuple-element.15.tap_ref, f32[128,128]{1,0:T(8,128)} %get-tuple-element.16.cot_ref), custom_call_target="tpu_custom_call" | custom-call | tf_op jit(solution)/shard_map/pallas_call | solution.py:293
  85.4 7.0 %all-to-all-start.2 = ((f32[128,8,128]{2,1,0:T(8,128)}), f32[128,8,128]{2,1,0:T(8,128)S(1)}, u32[]{:S(2)}, u32[]{:S(2)}) async-start(f32[128,8,128]{2,1,0:T(8,128)} %get-tuple-element.17), calls=%async_computation.2 | async-start | bytes 1048576 | tf_op jit(solution)/shard_map/all_to_all | solution.py:306
  92.4 0.0 copy-done.5
  92.4 0.1 slice.35
  92.5 0.1 slice.36
  92.6 0.7 pad_maximum_fusion.3.refs_2_
  93.3 3.5 %collective-permute-start.1 = (bf16[128,4096]{1,0:T(8,128)(2,1)}, bf16[128,4096]{1,0:T(8,128)(2,1)}, u32[]{:S(2)}, u32[]{:S(2)}) collective-permute-start(bf16[128,4096]{1,0:T(8,128)(2,1)} %get-tuple-element.19.refs_0_), channel_id=1, source_target_pairs={{0,1},{1,2},{2,3},{3,4},{4,5},{5,6},{6,7},{7,8},{8,9},{9,10},{10,1... | collective-permute-start | bytes 3145736 | tf_op jit(solution)/shard_map/ppermute | solution.py:302
  96.9 1.3 dynamic-slice_bitcast_fusion.lam_ref
  98.2 1.5 %pad_maximum_fusion.refs_3_ = bf16[4096,128]{1,0:T(8,128)(2,1)} fusion(bf16[4096,64]{1,0:T(8,128)(2,1)S(1)} %get-tuple-element.49, bf16[4096,64]{1,0:T(8,128)(2,1)S(1)} %get-tuple-element.50), kind=kLoop, calls=%fused_computation.14 | loop fusion | flops 2097152 | bytes 2097152 | tf_op jit(solution)/shard_map/concatenate | solution.py:310
  99.7 21.8 %all-to-all-done.2.x_ref = f32[128,8,128]{2,1,0:T(8,128)S(1)} async-done(((f32[128,8,128]{2,1,0:T(8,128)}), f32[128,8,128]{2,1,0:T(8,128)S(1)}, u32[]{:S(2)}, u32[]{:S(2)}) %all-to-all-start.2) | async-done | bytes 524320 | tf_op jit(solution)/shard_map/all_to_all | solution.py:306
  121.6 0.8 copy-done.1
  122.3 2.3 %shard_map.117 = f32[256,2,128]{2,1,0:T(2,128)} custom-call(f32[128,8,128]{2,1,0:T(8,128)} %copy-done.1, f32[4,128]{1,0:T(4,128)} %get-tuple-element.20.sum_ref, f32[16,128]{1,0:T(8,128)} %dynamic-slice_bitcast_fusion.lam_ref), custom_call_target="tpu_custom_call" | custom-call | tf_op jit(solution)/shard_map/pallas_call | solution.py:293
  124.7 8.6 %all-to-all-start.3 = ((f32[256,2,128]{2,1,0:T(2,128)}), f32[256,2,128]{2,1,0:T(2,128)S(1)}, u32[]{:S(2)}, u32[]{:S(2)}) async-start(f32[256,2,128]{2,1,0:T(2,128)} %shard_map.117), calls=%async_computation.3 | async-start | bytes 524288 | tf_op jit(solution)/shard_map/all_to_all | solution.py:306
  133.3 7.2 %shard_map.115 = bf16[128,4096]{1,0:T(8,128)(2,1)} custom-call(f32[128,4096]{1,0:T(8,128)} %get-tuple-element.13.refs_2_.refs_0_, bf16[128,4096]{1,0:T(8,128)(2,1)} %bitcast.102, f32[128,128]{1,0:T(8,128)} %copy-done.4, bf16[4096,128]{1,0:T(8,128)(2,1)} %pad_maximum_fusion.refs_3_, f32[1024,128]{1,0:T(8,128)} %bitcast.85), custom_call_target="tpu_custom_call" | custom-call | flops 6000000000 | bytes 4784128 | tf_op jit(solution)/shard_map/pallas_call | solution.py:281
  140.5 0.0 collective-permute-done.1.refs_1_
  140.5 7.5 %shard_map.116 = bf16[128,4096]{1,0:T(8,128)(2,1)} custom-call(bf16[128,4096]{1,0:T(8,128)(2,1)} %get-tuple-element.19.refs_0_, bf16[128,4096]{1,0:T(8,128)(2,1)} %collective-permute-done.1.refs_1_, f32[128,128]{1,0:T(8,128)} %pad_maximum_fusion.3.refs_2_, bf16[128,4096]{1,0:T(8,128)(2,1)} %bitcast.86), custom_call_target="tpu_custom_call" | custom-call | flops 7000000000 | bytes 3211264 | tf_op jit(solution)/shard_map/pallas_call | solution.py:281
  147.9 0.6 all-to-all-done.3
  148.5 0.2 reduce_sum.19
  148.7 0.7 slice_multiply_fusion
  149.4 0.3 fusion.12
  149.7 0.1 copy.62
  149.8 0.1 reshape_squeeze.3
  149.9 0.2 copy.58
  150.2 0.1 copy.60
  150.2 0.7 fusion.10
  (11 shorter events, 0.1 us)
Async XLA Ops:
  0.6 7.0 %copy-start.6 = (f32[128,16]{0,1:T(8,128)S(1)}, f32[128,16]{0,1:T(8,128)}, u32[]{:S(2)}) copy-start(f32[128,16]{0,1:T(8,128)} %param.12) | copy-start | bytes 24580
  0.6 7.0 %copy-start.7 = (f32[128,16]{0,1:T(8,128)S(1)}, f32[128,16]{0,1:T(8,128)}, u32[]{:S(2)}) copy-start(f32[128,16]{0,1:T(8,128)} %param.11) | copy-start | bytes 24580
  2.5 9.8 %copy-start.2 = (bf16[128,4096]{1,0:T(8,128)(2,1)}, bf16[128,4096]{1,0:T(8,128)(2,1)S(1)}, u32[]{:S(2)}) copy-start(bf16[128,4096]{1,0:T(8,128)(2,1)S(1)} %fusion.8.refs_0_.refs_3_) | copy-start | bytes 3145732
  2.5 21.6 %collective-permute-start = (bf16[128,4096]{1,0:T(8,128)(2,1)S(1)}, bf16[128,4096]{1,0:T(8,128)(2,1)S(1)}, u32[]{:S(2)}, u32[]{:S(2)}) collective-permute-start(bf16[128,4096]{1,0:T(8,128)(2,1)S(1)} %fusion.8.refs_0_.refs_3_), channel_id=1, source_target_pairs={{1,0},{2,1},{3,2},{4,3},{5,4},{6,5},{7,6},{8,7},{9,8},{10,9},{11,1... | collective-permute-start | bytes 3145736 | tf_op jit(solution)/shard_map/ppermute | solution.py:302
  12.3 24.8 %all-to-all-start = ((f32[128,4,128]{2,1,0:T(4,128)}), f32[128,4,128]{2,1,0:T(4,128)S(1)}, u32[]{:S(2)}, u32[]{:S(2)}) async-start(f32[128,4,128]{2,1,0:T(4,128)} %bitcast.93), calls=%async_computation | async-start | bytes 524288 | tf_op jit(solution)/shard_map/all_to_all | solution.py:306
  24.1 1.0 copy-start.8
  37.1 0.7 copy-start.3
  39.9 32.3 %all-to-all-start.1 = ((f32[128,8,128]{2,1,0:T(8,128)}), f32[128,8,128]{2,1,0:T(8,128)S(1)}, u32[]{:S(2)}, u32[]{:S(2)}) async-start(f32[128,8,128]{2,1,0:T(8,128)} %shard_map.112.front_ref), calls=%async_computation.1 | async-start | bytes 1048576 | tf_op jit(solution)/shard_map/all_to_all | solution.py:306
  55.5 1.8 %copy-start.4 = (f32[128,128]{1,0:T(8,128)}, f32[128,128]{1,0:T(8,128)S(1)}, u32[]{:S(2)}) copy-start(f32[128,128]{1,0:T(8,128)S(1)} %get-tuple-element.44.refs_2_) | copy-start | bytes 196612
  72.2 0.8 copy-start
  83.0 9.4 %copy-start.5 = (f32[128,128]{1,0:T(8,128)S(1)}, f32[128,128]{1,0:T(8,128)}, u32[]{:S(2)}) copy-start(f32[128,128]{1,0:T(8,128)} %refs_4_.1) | copy-start | bytes 196612
  85.4 36.1 %all-to-all-start.2 = ((f32[128,8,128]{2,1,0:T(8,128)}), f32[128,8,128]{2,1,0:T(8,128)S(1)}, u32[]{:S(2)}, u32[]{:S(2)}) async-start(f32[128,8,128]{2,1,0:T(8,128)} %get-tuple-element.17), calls=%async_computation.2 | async-start | bytes 1048576 | tf_op jit(solution)/shard_map/all_to_all | solution.py:306
  93.3 47.1 %collective-permute-start.1 = (bf16[128,4096]{1,0:T(8,128)(2,1)}, bf16[128,4096]{1,0:T(8,128)(2,1)}, u32[]{:S(2)}, u32[]{:S(2)}) collective-permute-start(bf16[128,4096]{1,0:T(8,128)(2,1)} %get-tuple-element.19.refs_0_), channel_id=1, source_target_pairs={{0,1},{1,2},{2,3},{3,4},{4,5},{5,6},{6,7},{7,8},{8,9},{9,10},{10,1... | collective-permute-start | bytes 3145736 | tf_op jit(solution)/shard_map/ppermute | solution.py:302
  121.5 0.8 copy-start.1
  124.7 23.9 %all-to-all-start.3 = ((f32[256,2,128]{2,1,0:T(2,128)}), f32[256,2,128]{2,1,0:T(2,128)S(1)}, u32[]{:S(2)}, u32[]{:S(2)}) async-start(f32[256,2,128]{2,1,0:T(2,128)} %shard_map.117), calls=%async_computation.3 | async-start | bytes 524288 | tf_op jit(solution)/shard_map/all_to_all | solution.py:306

commit v3 on v2

--- a/solution.py
+++ b/solution.py
@@ -14,7 +14,6 @@
 NN = (((1,), (0,)), ((), ()))
 NT = (((1,), (1,)), ((), ()))
 TN = (((0,), (0,)), ((), ()))
-VMEM_LIMIT = 60 * 1024 * 1024
 
 
 def dot(left, right, dims=NN):
@@ -83,17 +82,11 @@
     return jnp.sum(rows.reshape(-1, 8, LANES), axis=1)
 
 
-def carried_part(table, entering, size):
-    high, low = (spread_groups(part, size) for part in split(entering))
-    return dot(
-        jnp.concatenate([table, table], axis=1), jnp.concatenate([high, high, low, low], axis=0)
-    )
-
-
-def states_of(ref, i, modes):
-    return jnp.concatenate(
-        [ref[i * 2 * modes + k : i * 2 * modes + k + 4, :] for k in range(0, 2 * modes, 8)], axis=0
-    )
+def carried_part(table, ref, i, modes, size):
+    x = ref[i * 2 * modes : (i + 1) * 2 * modes, :].astype(F32)
+    x = jnp.concatenate([x[k : k + 4] for k in range(0, 2 * modes, 8)], axis=0)
+    x = spread_groups(x, size).astype(BF16)
+    return dot(table, jnp.concatenate([x, x], axis=0))
 
 
 def mode_sums(table, x, size, modes):
@@ -147,24 +140,32 @@
     lag_ref[...] = lag_sums(lag_parts)
 
 
+def local_kernel(size, x_ref, filt_ref, rate_ref, weight_ref, out_ref, front_ref, back_ref):
+    per = LANES // size
+    row, col = iota((LANES, LANES), 0), iota((LANES, LANES), 1)
+    up = row.astype(F32)
+    for i, lanes in enumerate(tiles_of(x_ref)):
+        x = x_ref[:, lanes]
+        prod = dot(toeplitz(filt_ref, i, per, [col <= row]), jnp.concatenate([x, x], axis=0))
+        out_ref[:, lanes] = pick_groups(prod, LANES, size)
+    for i in range(x_ref.shape[1] // LANES):
+        rate, weight = rate_ref[i : i + 1, :], weight_ref[i : i + 1, :]
+        for ref, steps in ((front_ref, up + 1.0), (back_ref, LANES - 1.0 - up)):
+            high, low = split(weight * jnp.exp(-rate * steps))
+            ref[i * LANES : (i + 1) * LANES, :] = jnp.where(col < LANES // 2, high, low)
+
+
 def values_kernel(
-    size, modes, x_ref, gate_ref, gm_ref, own_ref, next_ref, filt_ref, table_ref, enter_ref,
+    size, modes, local_ref, gate_ref, gm_ref, own_ref, next_ref, table_ref, enter_ref,
     mix_ref, ggl_ref, lag_ref,
 ):
     per = LANES // size
     row, col = iota((LANES, LANES), 0), iota((LANES, LANES), 1)
-    tiles = tiles_of(x_ref)
-    values, mixes, lag_parts = [], [], []
+    tiles = tiles_of(local_ref)
+    mixes, lag_parts = [], []
     for i, lanes in enumerate(tiles):
-        values.append(
-            carried_part(
-                table_ref[i * LANES : (i + 1) * LANES, :], states_of(enter_ref, i, modes), size
-            )
-        )
-    for i, lanes in enumerate(tiles):
-        x = x_ref[:, lanes]
-        prod = dot(toeplitz(filt_ref, i, per, [col <= row]), jnp.concatenate([x, x], axis=0))
-        full = pick_groups(prod, LANES, size) + values[i]
+        table = table_ref[i * LANES : (i + 1) * LANES, :]
+        full = local_ref[:, lanes] + carried_part(table, enter_ref, i, modes, size)
         ggl_ref[:, lanes] = (gm_ref[:, lanes] * full).astype(BF16)
         mixes.append((gate_ref[:, lanes].astype(F32) * full).astype(BF16))
     for i, lanes in enumerate(tiles):
@@ -186,12 +187,9 @@
         prod = dot(
             jnp.concatenate([left, left[:, :LANES]], axis=1), jnp.concatenate([high, high, low], axis=0)
         )
-        out_ref[:, lanes] = (
-            pick_groups(prod, LANES, size)
-            + carried_part(
-                table_ref[i * LANES : (i + 1) * LANES, :], states_of(enter_ref, i, modes), size
-            )
-        ).astype(BF16)
+        table = table_ref[i * LANES : (i + 1) * LANES, :]
+        carried = carried_part(table, enter_ref, i, modes, size)
+        out_ref[:, lanes] = (pick_groups(prod, LANES, size) + carried).astype(BF16)
 
 
 def mixer_kernel(size, own_ref, before_ref, taps_ref, cot_ref, out_ref):
@@ -205,13 +203,43 @@
         out_ref[:, lanes] = (cot_ref[:, lanes].astype(F32) * mixed).astype(BF16)
 
 
-def scan_kernel(x_ref, decay_ref, beside_ref, out_ref):
+def exact_dot(left, right, dims=NN):
+    return lax.dot_general(
+        left, right, dims, precision=lax.Precision.HIGHEST, preferred_element_type=F32
+    )
+
+
+def prepare_kernel(
+    size, own_rows, me_ref, rates_ref, weight_ref, taps_ref, filt_ref, filt_back_ref, taps_back_ref,
+    decay_ref, lam_ref,
+):
+    me = me_ref[0, 0]
+    rates, taps = rates_ref[...], taps_ref[...]
+    groups, modes = rates.shape
+    lag = iota((groups, LANES), 1).astype(F32)
+    filt = jnp.zeros((groups, LANES), F32)
+    for m in range(modes):
+        filt = filt + weight_ref[:, m : m + 1] * jnp.exp(-rates[:, m : m + 1] * lag)
+    row, col = iota((LANES, LANES), 0), iota((LANES, LANES), 1)
+    mirror = ((row + col) % LANES == 0).astype(F32)
+    filt_ref[...] = filt
+    filt_back_ref[...] = exact_dot(filt, mirror)
+    taps_back_ref[...] = exact_dot(taps, mirror)
+    per, parts = LANES // size, modes // own_rows
+    pick = iota((8, modes), 1) == me % parts * own_rows + iota((8, modes), 0)
+    chosen = exact_dot(pick.astype(F32), rates, NT)
+    spread = iota((groups, LANES), 0) == me // parts * per + iota((groups, LANES), 1) // size
+    decay_ref[...] = jnp.exp(-exact_dot(chosen, spread.astype(F32))[:own_rows] * LANES)
+    own = (iota((groups, LANES), 0) == me).astype(F32)
+    lam_ref[...] = jnp.exp(-exact_dot(rates, own, TN) * iota((modes, LANES), 1).astype(F32))
+
+
+def scan_kernel(x_ref, decay_ref, beside_ref, out_ref, state_ref):
     decay = decay_ref[...]
-    rows = decay.shape[0]
     state = jnp.zeros_like(decay)
     for d in range(x_ref.shape[0]):
-        out_ref[d, :rows, :] = state
-        out_ref[d, rows:, :] = beside_ref[d]
+        state_ref[d] = state
+        out_ref[d] = jnp.concatenate([state, beside_ref[d]], axis=0).astype(BF16)
         state = decay * state + x_ref[d]
 
 
@@ -221,36 +249,49 @@
     per = tap_ref.shape[0] // x_ref.shape[0]
     state = jnp.zeros_like(decay)
     total = jnp.zeros_like(decay)
-    rest = jnp.zeros((rows - 2 * per, LANES), F32)
     for d in reversed(range(x_ref.shape[0])):
-        x = x_ref[d, rows:, :]
-        out_ref[d, :rows, :] = state
-        out_ref[d, rows:, :] = jnp.concatenate(
-            [tap_ref[d * per : (d + 1) * per, :], cot_ref[d * per : (d + 1) * per, :], rest], axis=0
+        x = x_ref[d].astype(F32)[rows:]
+        lags = jnp.concatenate(
+            [tap_ref[d * per : (d + 1) * per, :], cot_ref[d * per : (d + 1) * per, :]], axis=0
         )
+        low = lags - lags.astype(BF16).astype(F32)
+        out_ref[d] = jnp.concatenate([state, lags, low], axis=0).astype(BF16)
         state = decay * state + x
-        total = total + x * front_ref[d, :rows, :]
+        total = total + x * front_ref[d]
     sum_ref[...] = total
 
 
 def collect_kernel(size, x_ref, sum_ref, lam_ref, out_ref):
     rows, modes = sum_ref.shape[0], lam_ref.shape[0]
-    lags = jnp.sum(x_ref[:, rows:, :], axis=0)
-    exact = functools.partial(
-        lax.dot_general, precision=lax.Precision.HIGHEST, preferred_element_type=F32
-    )
+    lags = jnp.sum(x_ref[...].astype(F32), axis=0)[rows:]
+    lags = lags[:2] + lags[2:]
     lam = jnp.concatenate([lam_ref[...], jnp.zeros((LANES - modes, LANES), F32)], axis=0)
-    second = exact(jnp.broadcast_to(lags[1:2], (8, LANES)), lam, NT)[:1]
+    second = exact_dot(jnp.broadcast_to(lags[1:2], (8, LANES)), lam, NT)[:1]
     lane, place = iota((LANES, LANES), 0), iota((LANES, LANES), 1)
-    per = LANES // size
     for q in range(rows):
-        pick = (place == modes + q * per + lane // size).astype(F32)
-        second = second + exact(jnp.broadcast_to(sum_ref[q : q + 1, :], (8, LANES)), pick, NN)[:1]
+        pick = (place == modes + lane // size * rows + q).astype(F32)
+        second = second + exact_dot(jnp.broadcast_to(sum_ref[q : q + 1, :], (8, LANES)), pick, NN)[:1]
     message = jnp.concatenate([lags[:1], second], axis=0)
     out_ref[...] = jnp.broadcast_to(message[None], out_ref.shape)
 
 
-def call(body, width, step, chunk, specs, outs, args, micros):
+def finish_kernel(scale, per, rows, x_ref, norm_ref, res_ref, tap_ref):
+    count, modes = norm_ref.shape
+    x = x_ref[0:count]
+    for k in range(count, x_ref.shape[0], count):
+        x = x + x_ref[k : k + count]
+    tap_ref[...] = x[:, 0, :] * scale
+    rest = x[:, 1, :]
+    total = rest
+    h, j = iota(rest.shape, 0) % per, iota(rest.shape, 1) // rows
+    for delta in range(1 - per, per):
+        moved = rest if delta == 0 else pltpu.roll(rest, delta % count, 0)
+        moved = pltpu.roll(moved, (-modes - rows * delta) % LANES, 1)
+        total = total + jnp.where(h - j == delta, moved, 0.0)
+    res_ref[...] = total[:, :modes] * norm_ref[...] * scale
+
+
+def call(body, width, step, chunk, specs, outs, args, micros, room=60):
     kinds = list(specs) + [rows for rows, kind in outs]
     chunks = step // chunk
 
@@ -284,7 +325,7 @@
         in_specs=[block(rows) for rows in specs],
         out_specs=[block(rows) for rows, kind in outs],
         out_shape=[shape(rows, kind) for rows, kind in outs],
-        compiler_params=pltpu.CompilerParams(vmem_limit_bytes=VMEM_LIMIT),
+        compiler_params=pltpu.CompilerParams(vmem_limit_bytes=room * 1024 * 1024),
         cost_estimate=pl.CostEstimate(flops=micros * 1_000_000_000, bytes_accessed=nbytes, transcendentals=0),
     )(*args)
 
@@ -292,8 +333,9 @@
 def whole(body, outs, args):
     return pl.pallas_call(
         body,
-        out_shape=[jax.ShapeDtypeStruct(s, F32) for s in outs],
-        compiler_params=pltpu.CompilerParams(vmem_limit_bytes=VMEM_LIMIT),
+        out_shape=[jax.ShapeDtypeStruct(shape, kind) for shape, kind in outs],
+        compiler_params=pltpu.CompilerParams(vmem_limit_bytes=8 * 1024 * 1024),
+        cost_estimate=pl.CostEstimate(flops=2_000_000_000, bytes_accessed=1 << 20, transcendentals=0),
     )(*args)
 
 
@@ -304,10 +346,6 @@
 
 def exchange(x, axes="ctx"):
     return lax.all_to_all(x, axes, split_axis=0, concat_axis=0, tiled=True)
-
-
-def carry_table(x):
-    return jnp.concatenate(split(x), axis=2).reshape(-1, 2 * x.shape[2])
 
 
 def on_device(inputs, gate_li, gate_mr, cotangent, residues, rates, taps):
@@ -324,7 +362,7 @@
     state_rows = chunk // LANES * modes
     table_rows = per * state_rows
     group_rows = chunk // size
-    carry_rows = chunk
+    carry_rows, tile_rows = chunk, chunk // LANES
 
     scaled = (cot.astype(F32) * gate_mr[0].astype(F32)).astype(BF16)
     after = shifted(scaled, -1)
@@ -333,22 +371,25 @@
     norm = jnp.sqrt(-jnp.expm1(-2.0 * rates))
     weight = residues * norm
     rate3, weight3 = rates[:, :, None], weight[:, :, None]
-    lam = jnp.exp(-rate3 * lags)
-    filt = jnp.sum(weight3 * lam, axis=1)
-    filt_back = jnp.roll(jnp.flip(filt, 1), 1, axis=1)
-    taps_back = jnp.roll(jnp.flip(taps, 1), 1, axis=1)
     to_end = jnp.exp(-rate3 * (LANES - 1.0 - lags))
     from_start = jnp.exp(-rate3 * (lags + 1.0))
     flat = (groups * modes, LANES)
     end_table = to_end.reshape(flat)
     start_table = from_start.reshape(flat)
-    rate_row = rates.reshape(tiles, 1, per * modes)
-    weight_row = weight.reshape(tiles, 1, per * modes)
-    front_table = carry_table(weight_row * jnp.exp(-rate_row * (lags[:, None] + 1.0)))
-    back_table = carry_table(weight_row * jnp.exp(-rate_row * (LANES - 1.0 - lags[:, None])))
-    decay = jnp.exp(-rates * LANES).reshape(tiles, per, modes)
-    decay = jnp.repeat(jnp.swapaxes(decay, 1, 2).reshape(tiles * modes, per), size, axis=1)
-    decay = lax.dynamic_slice_in_dim(decay, me * own_rows, own_rows, 0)
+    rate_row = rates.reshape(tiles, per * modes)
+    rate_row = jnp.concatenate([rate_row, rate_row], axis=1)
+    weight_row = weight.reshape(tiles, per * modes)
+    weight_row = jnp.concatenate([weight_row, weight_row], axis=1)
+    filt, filt_back, taps_back, decay, lam_own = pl.pallas_call(
+        functools.partial(prepare_kernel, size, own_rows),
+        in_specs=[pl.BlockSpec(memory_space=pltpu.SMEM)] + [pl.BlockSpec(memory_space=pltpu.VMEM)] * 3,
+        out_shape=[
+            jax.ShapeDtypeStruct(shape, F32)
+            for shape in (taps.shape, taps.shape, taps.shape, (own_rows, LANES), (modes, LANES))
+        ],
+        compiler_params=pltpu.CompilerParams(vmem_limit_bytes=8 * 1024 * 1024),
+        cost_estimate=pl.CostEstimate(flops=3_000_000_000, bytes_accessed=1 << 20, transcendentals=0),
+    )(me.astype(jnp.int32).reshape(1, 1), rates, weight, taps)
 
     bind = functools.partial
     states = call(
@@ -357,55 +398,56 @@
     )[0]
     ends = exchange(states.reshape(count, own_rows, LANES))
 
+    after, filt, filt_back, taps_back, decay, lam_own = lax.optimization_barrier(
+        (after, filt, filt_back, taps_back, decay, lam_own)
+    )
     grad_mixer, back_states, lag_cot = call(
         bind(mixer_back_kernel, size, modes), width, step, chunk,
         [None, None, None, None, group_rows, table_rows],
         [(None, F32), (state_rows, F32), (group_rows, F32)],
         [scaled, after, gate, seq, taps, start_table], 11,
     )
-    first = whole(
-        scan_kernel, [(count, 2 * own_rows, LANES)],
+    first, entering = whole(
+        scan_kernel, [((count, 2 * own_rows, LANES), BF16), (ends.shape, F32)],
         [ends, decay, back_states.reshape(count, own_rows, LANES)],
-    )[0]
+    )
     second = exchange(first)
+    local, front_table, back_table = call(
+        bind(local_kernel, size), width, step, chunk,
+        [None, group_rows, tile_rows, tile_rows], [(None, F32), (carry_rows, BF16), (carry_rows, BF16)],
+        [seq, filt_back, rate_row, weight_row], 7,
+    )
     mixer_in, grad_gate_li, lag_taps = call(
         bind(values_kernel, size, modes), width, step, chunk,
-        [None, None, None, None, None, group_rows, carry_rows, 2 * state_rows],
+        [None, None, None, None, None, carry_rows, 2 * state_rows],
         [(None, BF16), (None, BF16), (group_rows, F32)],
-        [seq, gate, grad_mixer, scaled, after, filt_back, front_table, second.reshape(-1, LANES)], 10,
+        [local, gate, grad_mixer, scaled, after, front_table, second.reshape(-1, LANES)], 6,
     )
     before = shifted(mixer_in, 1)
     message, state_sums = whole(
-        back_scan_kernel, [first.shape, decay.shape], [second, decay, first, lag_taps, lag_cot]
+        back_scan_kernel, [(first.shape, BF16), (decay.shape, F32)],
+        [second, decay, entering, lag_taps, lag_cot],
     )
     third = exchange(message)
-    own_groups = groups // count
-    lam_own = lax.dynamic_slice_in_dim(lam, me * own_groups, own_groups, 0).reshape(modes, LANES)
+    grad_gate_mr = call(
+        bind(mixer_kernel, size), width, step, chunk, [None, None, group_rows, None], [(None, BF16)],
+        [mixer_in, before, taps_back, cot], 7, 32,
+    )[0]
+    third, grad_gate_mr = lax.optimization_barrier((third, grad_gate_mr))
     spread = whole(
-        bind(collect_kernel, size), [(reps * count, 2, LANES)], [third, state_sums, lam_own]
+        bind(collect_kernel, size), [((reps * count, 2, LANES), F32)], [third, state_sums, lam_own]
     )[0]
     got = exchange(spread, ("rep", "ctx"))
     grad_inputs = call(
         bind(input_grad_kernel, size, modes), width, step, chunk,
         [None, None, group_rows, carry_rows, 2 * state_rows], [(None, BF16)],
-        [grad_mixer, gate, filt, back_table, third.reshape(-1, LANES)], 6,
+        [grad_mixer, gate, filt, back_table, third.reshape(-1, LANES)], 7,
     )[0]
-    grad_gate_mr = call(
-        bind(mixer_kernel, size), width, step, chunk, [None, None, group_rows, None], [(None, BF16)],
-        [mixer_in, before, taps_back, cot], 7,
-    )[0]
-    got = jnp.sum(got.reshape(reps, count, 2, LANES), axis=0)
-    local_all = got[:, 1, :modes]
-    first_all = got[:, 1, modes : modes + own_rows * per].reshape(tiles, modes, per)
-    first_all = jnp.swapaxes(first_all, 1, 2).reshape(groups, modes)
-    scale = 1.0 / math.sqrt(reps * count * LANES)
-    return (
-        grad_inputs[None],
-        grad_gate_li[None],
-        grad_gate_mr[None],
-        norm * (first_all + local_all) * scale,
-        got[:, 0] * scale,
-    )
+    grad_residues, grad_taps = whole(
+        bind(finish_kernel, 1.0 / math.sqrt(reps * count * LANES), per, own_rows),
+        [(rates.shape, F32), (taps.shape, F32)], [got, norm],
+    )
+    return grad_inputs[None], grad_gate_li[None], grad_gate_mr[None], grad_residues, grad_taps
 
 
 def solution(mesh):

time: 151 us -> 131 us (0.87)
  waiting for transfers between devices: 35 us -> 21.5 us
  other arithmetic: 12.6 us -> 4.2 us
  Pallas kernels: 46.2 us -> 48.3 us
    all_to_all x4, waiting for transfers between devices: 35 us -> 21.5 us  [exchange(): return lax.all_to_all(x, axes, split_axis=0, concat_axis=0, tiled=True)]
    concatenate x4 -> x1, other arithmetic: 4.53 us -> 0.7 us  [on_device(): rate_row = jnp.concatenate([rate_row, rate_row], axis=1)]
    pallas_call x5 -> x6, Pallas kernels: 39.4 us -> 42.8 us  [call(): pl.pallas_call(kernel, grid=(width // step,), in_specs=[block(rows) for r...]
    unnamed x20 -> x37, local copies, waits for them, and re-layouts: 3.99 us -> 7.33 us
    exp x2 -> x0, other arithmetic: 1.63 us -> none  [the longest x1 1.61 us: on_device(): lam = jnp.exp(-rate3 * lags)]
    pallas_call x3 -> x5, Pallas kernels: 6.83 us -> 5.54 us  [the longest x4 4 us: whole(): pl.pallas_call(body, out_shape=[jax.ShapeDtypeStruct(shape, kind) for sha...]
  transfers between devices with their start and end apart: 6 -> 6, of which waited for: 3 -> 3; matrix products, arithmetic and copies ran while one was open for 8% -> 2% of each run, Pallas kernels for 21% -> 29%
where the time goes in v3:
time: 131 us
  Pallas kernels  48.3 us (37%)
  starting transfers between devices  48 us (37%)
  waiting for transfers between devices  21.5 us (16%)
  local copies, waits for them, and re-layouts  7.77 us (6%)
  other arithmetic  4.2 us (3%)
    pallas_call x6, Pallas kernels, call(): pl.pallas_call(kernel, grid=(width // step,), in_specs=[block(rows) for r...  42.8 us
    all_to_all x4, starting transfers between devices, exchange(): return lax.all_to_all(x, axes, split_axis=0, concat_axis=0, tiled=True)  40.2 us
    all_to_all x4, waiting for transfers between devices, exchange(): return lax.all_to_all(x, axes, split_axis=0, concat_axis=0, tiled=True)  21.5 us
    ppermute x2, starting transfers between devices, shifted(): lax.ppermute(x, 'ctx', [(i, i + by) for i in range(count) if 0 <= i + by...  7.77 us
    unnamed x37, local copies, waits for them, and re-layouts  7.33 us
    pallas_call x4, Pallas kernels, whole(): pl.pallas_call(body, out_shape=[jax.ShapeDtypeStruct(shape, kind) for sha...  4 us
  transfers between devices with their start and end apart: 6, of which 3 were waited for; matrix products, arithmetic and copies ran while one was open for 2% of the time, Pallas kernels for 29%

profile of v3, /device:TPU:1, one launch (start us, length us, event | category | flops | bytes accessed | tf_op | source)
XLA Modules:
  0.0 130.6 jit_solution(3774403590130958410)
XLA Ops:
  0.6 0.0 copy-start.14
  0.6 1.8 %fusion.refs_0_.refs_3_ = bf16[128,4096]{1,0:T(8,128)(2,1)S(1)} fusion(bf16[1,128,4096]{2,1,0:T(8,128)(2,1)} %param.9, bf16[1,128,4096]{2,1,0:T(8,128)(2,1)} %param.10), kind=kLoop, calls=%fused_computation.1 | loop fusion | flops 2097152 | bytes 3145728 | tf_op jit(solution)/shard_map/convert_element_type | solution.py:367
  2.4 0.0 copy-start.13
  2.5 5.1 %collective-permute-start = (bf16[128,4096]{1,0:T(8,128)(2,1)S(1)}, bf16[128,4096]{1,0:T(8,128)(2,1)S(1)}, u32[]{:S(2)}, u32[]{:S(2)}) collective-permute-start(bf16[128,4096]{1,0:T(8,128)(2,1)S(1)} %fusion.refs_0_.refs_3_), channel_id=1, source_target_pairs={{1,0},{2,1},{3,2},{4,3},{5,4},{6,5},{7,6},{8,7},{9,8},{10,9},{11,1... | collective-permute-start | bytes 3145736 | tf_op jit(solution)/shard_map/ppermute | solution.py:344
  7.6 0.0 copy-done.14
  7.6 0.1 copy.28
  7.7 0.1 mul.44
  7.8 1.7 %multiply_exponential_fusion = (f32[2048,128]{1,0:T(8,128)}, f32[2048,128]{1,0:T(8,128)}) fusion(f32[128]{0:T(128)S(1)} %get-tuple-element.82, f32[2048]{0:T(1024)S(1)} %mul.44, f32[128]{0:T(128)S(1)} %get-tuple-element.83), kind=kLoop, calls=%fused_computation.2 | loop fusion | flops 524288 | bytes 2106368 | tf_op jit(solution)/shard_map/exp | solution.py:374
  9.5 0.0 copy-start.15
  9.5 0.0 copy-start.5
  9.5 2.8 %shard_map.113 = f32[512,128]{1,0:T(8,128)} custom-call(bf16[128,4096]{1,0:T(8,128)(2,1)} %bitcast.20, f32[2048,128]{1,0:T(8,128)} %get-tuple-element.78.refs_1_), custom_call_target="tpu_custom_call" | custom-call | flops 3000000000 | bytes 2097152 | tf_op jit(solution)/shard_map/pallas_call | solution.py:322
  12.3 0.0 copy-done.13
  12.3 10.7 %all-to-all-start = ((f32[128,4,128]{2,1,0:T(4,128)}), f32[128,4,128]{2,1,0:T(4,128)S(1)}, u32[]{:S(2)}, u32[]{:S(2)}) async-start(f32[128,4,128]{2,1,0:T(4,128)} %bitcast.19), calls=%async_computation | async-start | bytes 524288 | tf_op jit(solution)/shard_map/all_to_all | solution.py:348
  23.0 0.1 copy.27.rates_ref
  23.1 0.1 reshape.49
  23.2 0.1 copy.25
  23.3 0.0 copy-done.15
  23.3 0.1 copy.26
  23.4 0.1 reshape.50
  23.5 0.7 pad_maximum_fusion
  24.2 0.0 copy-done.5
  24.2 1.5 %shard_map.110 = (f32[128,128]{1,0:T(8,128)S(1)}, f32[128,128]{1,0:T(8,128)S(1)}, f32[128,128]{1,0:T(8,128)S(1)}, f32[4,128]{1,0:T(4,128)S(1)}, f32[16,128]{1,0:T(8,128)S(1)}) custom-call(s32[1,1]{1,0:T(1,128)} %bitcast.2.me_ref, f32[128,16]{1,0:T(8,128)S(1)} %copy.27.rates_ref, f32[128,16]{1,0:T(8,128)S(1)} %get-tuple-element.77.weight_ref, ...), custom_call_target="tpu_custom_call" | custom-call | flops 3000000000 | bytes 1048576 | tf_op jit(solution)/shard_map/pallas_call | solution.py:383
  25.8 0.0 copy-start.11
  25.8 0.7 copy-done.11
  26.4 0.0 copy-start.12
  26.4 0.6 copy-done.12
  27.0 0.0 collective-permute-done.refs_1_.refs_4_
  27.0 0.0 copy-start.16
  27.0 1.0 copy-done.16
  28.0 12.1 %shard_map.111 = (f32[128,4096]{1,0:T(8,128)}, f32[512,128]{1,0:T(8,128)}, f32[128,128]{1,0:T(8,128)}) custom-call(bf16[128,4096]{1,0:T(8,128)(2,1)} %copy-done.13, bf16[128,4096]{1,0:T(8,128)(2,1)} %copy-done.16, bf16[128,4096]{1,0:T(8,128)(2,1)} %bitcast.23, bf16[128,4096]{1,0:T(8,128)(2,1)} %bitcast.21, f32[128,128]{1,0:T(8,128)} %refs_4_.1, ...), custom_call_target="tpu_custom_call" | custom-call | flops 11000000512 | bytes 5308416 | tf_op jit(solution)/shard_map/pallas_call | solution.py:322
  40.1 0.0 all-to-all-done.x_ref
  40.1 0.0 copy-start.6
  40.1 0.9 copy-done.6
  41.1 1.0 shard_map.114
  42.0 0.0 copy-start.7
  42.0 0.7 copy-done.7
  42.7 11.7 %all-to-all-start.1 = ((bf16[128,8,128]{2,1,0:T(8,128)(2,1)}), bf16[128,8,128]{2,1,0:T(8,128)(2,1)S(1)}, u32[]{:S(2)}, u32[]{:S(2)}) async-start(bf16[128,8,128]{2,1,0:T(8,128)(2,1)} %get-tuple-element.45), calls=%async_computation.1 | async-start | bytes 524288 | tf_op jit(solution)/shard_map/all_to_all | solution.py:348
  54.5 6.7 %shard_map.112 = (f32[128,4096]{1,0:T(8,128)}, bf16[4096,128]{1,0:T(8,128)(2,1)}, bf16[4096,128]{1,0:T(8,128)(2,1)}) custom-call(bf16[128,4096]{1,0:T(8,128)(2,1)} %bitcast.22, f32[128,128]{1,0:T(8,128)} %copy-done.12, f32[32,128]{1,0:T(8,128)} %get-tuple-element.84.refs_2_, f32[32,128]{1,0:T(8,128)} %get-tuple-element.85.refs_3_), custom_call_target="tpu_custom_call" | custom-call | flops 7000000000 | bytes 1146880 | tf_op jit(solution)/shard_map/pallas_call | solution.py:322
  61.1 6.5 %all-to-all-done.1.x_ref = bf16[128,8,128]{2,1,0:T(8,128)(2,1)S(1)} async-done(((bf16[128,8,128]{2,1,0:T(8,128)(2,1)}), bf16[128,8,128]{2,1,0:T(8,128)(2,1)S(1)}, u32[]{:S(2)}, u32[]{:S(2)}) %all-to-all-start.1) | async-done | bytes 262176 | tf_op jit(solution)/shard_map/all_to_all | solution.py:348
  67.7 0.0 copy-start.1
  67.7 0.7 copy-done.1
  68.4 0.0 copy-start.8
  68.4 7.8 %shard_map.115 = (bf16[128,4096]{1,0:T(8,128)(2,1)}, bf16[128,4096]{1,0:T(8,128)(2,1)}, f32[128,128]{1,0:T(8,128)}) custom-call(f32[128,4096]{1,0:T(8,128)} %get-tuple-element.47.refs_0_, bf16[128,4096]{1,0:T(8,128)(2,1)} %bitcast.24, f32[128,4096]{1,0:T(8,128)} %get-tuple-element.39.refs_2_.refs_0_, bf16[128,4096]{1,0:T(8,128)(2,1)} %copy-done.13, ...), custom_call_target="tpu_custom_call" | custom-call | flops 6000000000 | bytes 8650752 | tf_op jit(solution)/shard_map/pallas_call | solution.py:322
  76.3 2.6 %collective-permute-start.1 = (bf16[128,4096]{1,0:T(8,128)(2,1)}, bf16[128,4096]{1,0:T(8,128)(2,1)S(1)}, u32[]{:S(2)}, u32[]{:S(2)}) collective-permute-start(bf16[128,4096]{1,0:T(8,128)(2,1)} %get-tuple-element.52.refs_0_), channel_id=1, source_target_pairs={{0,1},{1,2},{2,3},{3,4},{4,5},{5,6},{6,7},{7,8},{8,9},{9,10},{10,1... | collective-permute-start | bytes 3145736 | tf_op jit(solution)/shard_map/ppermute | solution.py:344
  78.9 0.0 copy-done.8
  78.9 0.0 copy-done.9
  78.9 0.0 copy-start.2
  79.0 0.9 copy-done.2
  79.9 0.0 copy-start.10
  79.9 0.8 copy-done.10
  80.7 1.0 shard_map.116
  81.7 9.4 %all-to-all-start.2 = ((bf16[128,8,128]{2,1,0:T(8,128)(2,1)}), bf16[128,8,128]{2,1,0:T(8,128)(2,1)S(1)}, u32[]{:S(2)}, u32[]{:S(2)}) async-start(bf16[128,8,128]{2,1,0:T(8,128)(2,1)} %get-tuple-element.51), calls=%async_computation.2 | async-start | bytes 524288 | tf_op jit(solution)/shard_map/all_to_all | solution.py:348
  91.2 0.0 collective-permute-done.1.refs_1_
  91.2 0.0 copy-done
  91.2 0.0 copy-done.4
  91.2 6.4 %shard_map.117 = bf16[128,4096]{1,0:T(8,128)(2,1)} custom-call(bf16[128,4096]{1,0:T(8,128)(2,1)S(1)} %copy-done.4, bf16[128,4096]{1,0:T(8,128)(2,1)S(1)} %collective-permute-done.1.refs_1_, f32[128,128]{1,0:T(8,128)S(1)} %get-tuple-element.53.refs_2_, bf16[128,4096]{1,0:T(8,128)(2,1)S(1)} %bitcast.15), custom_call_target="tpu_custom_call" | custom-call | flops 7000000000 | bytes 3211264 | tf_op jit(solution)/shard_map/pallas_call | solution.py:322
  97.6 6.8 %all-to-all-done.2.x_ref = bf16[128,8,128]{2,1,0:T(8,128)(2,1)S(1)} async-done(((bf16[128,8,128]{2,1,0:T(8,128)(2,1)}), bf16[128,8,128]{2,1,0:T(8,128)(2,1)S(1)}, u32[]{:S(2)}, u32[]{:S(2)}) %all-to-all-start.2) | async-done | bytes 262176 | tf_op jit(solution)/shard_map/all_to_all | solution.py:348
  104.4 1.3 shard_map.119
  105.7 0.0 copy-done.3
  105.7 8.3 %all-to-all-start.3 = ((f32[256,2,128]{2,1,0:T(2,128)}), f32[256,2,128]{2,1,0:T(2,128)S(1)}, u32[]{:S(2)}, u32[]{:S(2)}) async-start(f32[256,2,128]{2,1,0:T(2,128)} %shard_map.119), calls=%async_computation.3 | async-start | bytes 524288 | tf_op jit(solution)/shard_map/all_to_all | solution.py:348
  114.0 7.0 %shard_map.118 = bf16[128,4096]{1,0:T(8,128)(2,1)} custom-call(f32[128,4096]{1,0:T(8,128)} %get-tuple-element.39.refs_2_.refs_0_, bf16[128,4096]{1,0:T(8,128)(2,1)} %bitcast.25, f32[128,128]{1,0:T(8,128)} %copy-done.11, bf16[4096,128]{1,0:T(8,128)(2,1)} %get-tuple-element.42.refs_3_, bf16[1024,128]{1,0:T(8,128)(2,1)} %bitcast.17), custom_call_target="tpu_custom_call" | custom-call | flops 7000000000 | bytes 4521984 | tf_op jit(solution)/shard_map/pallas_call | solution.py:322
  121.1 8.1 %all-to-all-done.3.x_ref = f32[256,2,128]{2,1,0:T(2,128)S(1)} async-done(((f32[256,2,128]{2,1,0:T(2,128)}), f32[256,2,128]{2,1,0:T(2,128)S(1)}, u32[]{:S(2)}, u32[]{:S(2)}) %all-to-all-start.3) | async-done | bytes 262176 | tf_op jit(solution)/shard_map/all_to_all | solution.py:348
  129.2 0.7 shard_map.120
  130.0 0.7 copy.30
  (7 shorter events, 0.0 us)
Async XLA Ops:
  0.6 7.0 %copy-start.14 = (f32[128,16]{0,1:T(8,128)S(1)}, f32[128,16]{0,1:T(8,128)}, u32[]{:S(2)}) copy-start(f32[128,16]{0,1:T(8,128)} %param.12) | copy-start | bytes 24580
  2.4 9.9 %copy-start.13 = (bf16[128,4096]{1,0:T(8,128)(2,1)}, bf16[128,4096]{1,0:T(8,128)(2,1)S(1)}, u32[]{:S(2)}) copy-start(bf16[128,4096]{1,0:T(8,128)(2,1)S(1)} %fusion.refs_0_.refs_3_) | copy-start | bytes 3145732
  2.5 24.6 %collective-permute-start = (bf16[128,4096]{1,0:T(8,128)(2,1)S(1)}, bf16[128,4096]{1,0:T(8,128)(2,1)S(1)}, u32[]{:S(2)}, u32[]{:S(2)}) collective-permute-start(bf16[128,4096]{1,0:T(8,128)(2,1)S(1)} %fusion.refs_0_.refs_3_), channel_id=1, source_target_pairs={{1,0},{2,1},{3,2},{4,3},{5,4},{6,5},{7,6},{8,7},{9,8},{10,9},{11,1... | collective-permute-start | bytes 3145736 | tf_op jit(solution)/shard_map/ppermute | solution.py:344
  9.5 13.8 %copy-start.15 = (f32[128,16]{0,1:T(8,128)S(1)}, f32[128,16]{0,1:T(8,128)}, u32[]{:S(2)}) copy-start(f32[128,16]{0,1:T(8,128)} %param.11) | copy-start | bytes 24580
  9.5 14.7 %copy-start.5 = (f32[128,128]{1,0:T(8,128)S(1)}, f32[128,128]{1,0:T(8,128)}, u32[]{:S(2)}) copy-start(f32[128,128]{1,0:T(8,128)} %refs_4_.1) | copy-start | bytes 196612
  12.3 27.8 %all-to-all-start = ((f32[128,4,128]{2,1,0:T(4,128)}), f32[128,4,128]{2,1,0:T(4,128)S(1)}, u32[]{:S(2)}, u32[]{:S(2)}) async-start(f32[128,4,128]{2,1,0:T(4,128)} %bitcast.19), calls=%async_computation | async-start | bytes 524288 | tf_op jit(solution)/shard_map/all_to_all | solution.py:348
  25.8 0.7 copy-start.11
  26.4 0.6 copy-start.12
  27.0 1.0 copy-start.16
  40.1 1.0 copy-start.6
  42.0 0.7 copy-start.7
  42.7 25.0 %all-to-all-start.1 = ((bf16[128,8,128]{2,1,0:T(8,128)(2,1)}), bf16[128,8,128]{2,1,0:T(8,128)(2,1)S(1)}, u32[]{:S(2)}, u32[]{:S(2)}) async-start(bf16[128,8,128]{2,1,0:T(8,128)(2,1)} %get-tuple-element.45), calls=%async_computation.1 | async-start | bytes 524288 | tf_op jit(solution)/shard_map/all_to_all | solution.py:348
  67.7 0.8 copy-start.1
  68.4 10.5 %copy-start.8 = (f32[128,4,128]{2,1,0:T(4,128)S(1)}, f32[128,4,128]{2,1,0:T(4,128)}, u32[]{:S(2)}) copy-start(f32[128,4,128]{2,1,0:T(4,128)} %copy-done.7) | copy-start | bytes 786436
  68.4 10.5 %copy-start.9 = (f32[128,128]{1,0:T(8,128)S(1)}, f32[128,128]{1,0:T(8,128)}, u32[]{:S(2)}) copy-start(f32[128,128]{1,0:T(8,128)} %get-tuple-element.50.cot_ref) | copy-start | bytes 196612
  76.3 14.9 %collective-permute-start.1 = (bf16[128,4096]{1,0:T(8,128)(2,1)}, bf16[128,4096]{1,0:T(8,128)(2,1)S(1)}, u32[]{:S(2)}, u32[]{:S(2)}) collective-permute-start(bf16[128,4096]{1,0:T(8,128)(2,1)} %get-tuple-element.52.refs_0_), channel_id=1, source_target_pairs={{0,1},{1,2},{2,3},{3,4},{4,5},{5,6},{6,7},{7,8},{8,9},{9,10},{10,1... | collective-permute-start | bytes 3145736 | tf_op jit(solution)/shard_map/ppermute | solution.py:344
  78.9 1.0 copy-start.2
  79.9 0.8 copy-start.10
  80.7 10.4 %copy-start = (bf16[1,128,4096]{2,1,0:T(8,128)(2,1)S(1)}, bf16[1,128,4096]{2,1,0:T(8,128)(2,1)}, u32[]{:S(2)}) copy-start(bf16[1,128,4096]{2,1,0:T(8,128)(2,1)} %param.10) | copy-start | bytes 3145732
  80.7 10.4 %copy-start.4 = (bf16[128,4096]{1,0:T(8,128)(2,1)S(1)}, bf16[128,4096]{1,0:T(8,128)(2,1)}, u32[]{:S(2)}) copy-start(bf16[128,4096]{1,0:T(8,128)(2,1)} %get-tuple-element.52.refs_0_) | copy-start | bytes 3145732
  81.7 22.7 %all-to-all-start.2 = ((bf16[128,8,128]{2,1,0:T(8,128)(2,1)}), bf16[128,8,128]{2,1,0:T(8,128)(2,1)S(1)}, u32[]{:S(2)}, u32[]{:S(2)}) async-start(bf16[128,8,128]{2,1,0:T(8,128)(2,1)} %get-tuple-element.51), calls=%async_computation.2 | async-start | bytes 524288 | tf_op jit(solution)/shard_map/all_to_all | solution.py:348
  104.4 1.3 %copy-start.3 = (bf16[128,8,128]{2,1,0:T(8,128)(2,1)}, bf16[128,8,128]{2,1,0:T(8,128)(2,1)S(1)}, u32[]{:S(2)}) copy-start(bf16[128,8,128]{2,1,0:T(8,128)(2,1)S(1)} %all-to-all-done.2.x_ref) | copy-start | bytes 786436
  105.7 23.5 %all-to-all-start.3 = ((f32[256,2,128]{2,1,0:T(2,128)}), f32[256,2,128]{2,1,0:T(2,128)S(1)}, u32[]{:S(2)}, u32[]{:S(2)}) async-start(f32[256,2,128]{2,1,0:T(2,128)} %shard_map.119), calls=%async_computation.3 | async-start | bytes 524288 | tf_op jit(solution)/shard_map/all_to_all | solution.py:348

commit v4 on v3

--- a/solution.py
+++ b/solution.py
@@ -115,14 +115,12 @@
     out_ref[...] = jnp.concatenate(out, axis=0)
 
 
-def mixer_back_kernel(
-    size, modes, own_ref, next_ref, gate_ref, x_ref, taps_ref, table_ref, gm_ref, out_ref, lag_ref
-):
+def mixer_back_kernel(size, modes, own_ref, next_ref, gate_ref, taps_ref, table_ref, gm_ref, out_ref):
     per = LANES // size
     rows = per * modes
     row, col = iota((LANES, LANES), 0), iota((LANES, LANES), 1)
-    tiles = tiles_of(x_ref)
-    cots, out, lag_parts = [], [], []
+    tiles = tiles_of(own_ref)
+    cots, out = [], []
     for i, lanes in enumerate(tiles):
         own, after = own_ref[:, lanes], next_ref[:, lanes]
         left = toeplitz(taps_ref, i, per, [col >= row, col < row])
@@ -132,27 +130,33 @@
         cots.append(grad_mixer * gate_ref[:, lanes].astype(F32))
     for i, lanes in enumerate(tiles):
         out.append(mode_sums(table_ref[i * rows : (i + 1) * rows, :], cots[i], size, modes))
-    for i, lanes in enumerate(tiles):
-        pairs = dot(spread_groups(x_ref[:, lanes], size), cots[i].astype(BF16), NT)
-        for g in range(per):
-            lag_parts.append(lag_rows(jnp.where(col >= row, pairs[g * LANES : (g + 1) * LANES], 0.0)))
     out_ref[...] = jnp.concatenate(out, axis=0)
-    lag_ref[...] = lag_sums(lag_parts)
-
-
-def local_kernel(size, x_ref, filt_ref, rate_ref, weight_ref, out_ref, front_ref, back_ref):
+
+
+def local_kernel(
+    size, x_ref, gate_ref, gm_ref, filt_ref, rate_ref, weight_ref,
+    out_ref, front_ref, back_ref, lag_ref,
+):
     per = LANES // size
     row, col = iota((LANES, LANES), 0), iota((LANES, LANES), 1)
     up = row.astype(F32)
-    for i, lanes in enumerate(tiles_of(x_ref)):
+    tiles = tiles_of(x_ref)
+    lag_parts = []
+    for i, lanes in enumerate(tiles):
         x = x_ref[:, lanes]
         prod = dot(toeplitz(filt_ref, i, per, [col <= row]), jnp.concatenate([x, x], axis=0))
         out_ref[:, lanes] = pick_groups(prod, LANES, size)
-    for i in range(x_ref.shape[1] // LANES):
+    for i in range(len(tiles)):
         rate, weight = rate_ref[i : i + 1, :], weight_ref[i : i + 1, :]
         for ref, steps in ((front_ref, up + 1.0), (back_ref, LANES - 1.0 - up)):
             high, low = split(weight * jnp.exp(-rate * steps))
             ref[i * LANES : (i + 1) * LANES, :] = jnp.where(col < LANES // 2, high, low)
+    for i, lanes in enumerate(tiles):
+        cot = (gm_ref[:, lanes] * gate_ref[:, lanes].astype(F32)).astype(BF16)
+        pairs = dot(spread_groups(x_ref[:, lanes], size), cot, NT)
+        for g in range(per):
+            lag_parts.append(lag_rows(jnp.where(col >= row, pairs[g * LANES : (g + 1) * LANES], 0.0)))
+    lag_ref[...] = lag_sums(lag_parts)
 
 
 def values_kernel(
@@ -234,11 +238,10 @@
     lam_ref[...] = jnp.exp(-exact_dot(rates, own, TN) * iota((modes, LANES), 1).astype(F32))
 
 
-def scan_kernel(x_ref, decay_ref, beside_ref, out_ref, state_ref):
+def scan_kernel(x_ref, decay_ref, beside_ref, out_ref):
     decay = decay_ref[...]
     state = jnp.zeros_like(decay)
     for d in range(x_ref.shape[0]):
-        state_ref[d] = state
         out_ref[d] = jnp.concatenate([state, beside_ref[d]], axis=0).astype(BF16)
         state = decay * state + x_ref[d]
 
@@ -257,7 +260,7 @@
         low = lags - lags.astype(BF16).astype(F32)
         out_ref[d] = jnp.concatenate([state, lags, low], axis=0).astype(BF16)
         state = decay * state + x
-        total = total + x * front_ref[d]
+        total = total + x * front_ref[d].astype(F32)[:rows]
     sum_ref[...] = total
 
 
@@ -276,8 +279,8 @@
 
 
 def finish_kernel(scale, per, rows, x_ref, norm_ref, res_ref, tap_ref):
-    count, modes = norm_ref.shape
-    x = x_ref[0:count]
+    modes, count = norm_ref.shape
+    x = x_ref[:count]
     for k in range(count, x_ref.shape[0], count):
         x = x + x_ref[k : k + count]
     tap_ref[...] = x[:, 0, :] * scale
@@ -288,7 +291,7 @@
         moved = rest if delta == 0 else pltpu.roll(rest, delta % count, 0)
         moved = pltpu.roll(moved, (-modes - rows * delta) % LANES, 1)
         total = total + jnp.where(h - j == delta, moved, 0.0)
-    res_ref[...] = total[:, :modes] * norm_ref[...] * scale
+    res_ref[...] = total.T[:modes] * norm_ref[...] * scale
 
 
 def call(body, width, step, chunk, specs, outs, args, micros, room=60):
@@ -330,11 +333,11 @@
     )(*args)
 
 
-def whole(body, outs, args):
+def whole(body, outs, args, room=8):
     return pl.pallas_call(
         body,
         out_shape=[jax.ShapeDtypeStruct(shape, kind) for shape, kind in outs],
-        compiler_params=pltpu.CompilerParams(vmem_limit_bytes=8 * 1024 * 1024),
+        compiler_params=pltpu.CompilerParams(vmem_limit_bytes=room * 1024 * 1024),
         cost_estimate=pl.CostEstimate(flops=2_000_000_000, bytes_accessed=1 << 20, transcendentals=0),
     )(*args)
 
@@ -358,7 +361,7 @@
     reps, count = lax.axis_size("rep"), lax.axis_size("ctx")
     me = lax.axis_index("ctx")
     own_rows = tiles * modes // count
-    step, chunk = min(2048, width), min(1024, width)
+    step = chunk = min(2048, width)
     state_rows = chunk // LANES * modes
     table_rows = per * state_rows
     group_rows = chunk // size
@@ -387,7 +390,7 @@
             jax.ShapeDtypeStruct(shape, F32)
             for shape in (taps.shape, taps.shape, taps.shape, (own_rows, LANES), (modes, LANES))
         ],
-        compiler_params=pltpu.CompilerParams(vmem_limit_bytes=8 * 1024 * 1024),
+        compiler_params=pltpu.CompilerParams(vmem_limit_bytes=60 * 1024 * 1024),
         cost_estimate=pl.CostEstimate(flops=3_000_000_000, bytes_accessed=1 << 20, transcendentals=0),
     )(me.astype(jnp.int32).reshape(1, 1), rates, weight, taps)
 
@@ -401,21 +404,21 @@
     after, filt, filt_back, taps_back, decay, lam_own = lax.optimization_barrier(
         (after, filt, filt_back, taps_back, decay, lam_own)
     )
-    grad_mixer, back_states, lag_cot = call(
+    grad_mixer, back_states = call(
         bind(mixer_back_kernel, size, modes), width, step, chunk,
-        [None, None, None, None, group_rows, table_rows],
-        [(None, F32), (state_rows, F32), (group_rows, F32)],
-        [scaled, after, gate, seq, taps, start_table], 11,
-    )
-    first, entering = whole(
-        scan_kernel, [((count, 2 * own_rows, LANES), BF16), (ends.shape, F32)],
+        [None, None, None, group_rows, table_rows], [(None, F32), (state_rows, F32)],
+        [scaled, after, gate, taps, start_table], 8,
+    )
+    first = whole(
+        scan_kernel, [((count, 2 * own_rows, LANES), BF16)],
         [ends, decay, back_states.reshape(count, own_rows, LANES)],
-    )
+    )[0]
     second = exchange(first)
-    local, front_table, back_table = call(
+    local, front_table, back_table, lag_cot = call(
         bind(local_kernel, size), width, step, chunk,
-        [None, group_rows, tile_rows, tile_rows], [(None, F32), (carry_rows, BF16), (carry_rows, BF16)],
-        [seq, filt_back, rate_row, weight_row], 7,
+        [None, None, None, group_rows, tile_rows, tile_rows],
+        [(None, F32), (carry_rows, BF16), (carry_rows, BF16), (group_rows, F32)],
+        [seq, gate, grad_mixer, filt_back, rate_row, weight_row], 10,
     )
     mixer_in, grad_gate_li, lag_taps = call(
         bind(values_kernel, size, modes), width, step, chunk,
@@ -426,7 +429,7 @@
     before = shifted(mixer_in, 1)
     message, state_sums = whole(
         back_scan_kernel, [(first.shape, BF16), (decay.shape, F32)],
-        [second, decay, entering, lag_taps, lag_cot],
+        [second, decay, first, lag_taps, lag_cot], 60,
     )
     third = exchange(message)
     grad_gate_mr = call(
@@ -445,9 +448,9 @@
     )[0]
     grad_residues, grad_taps = whole(
         bind(finish_kernel, 1.0 / math.sqrt(reps * count * LANES), per, own_rows),
-        [(rates.shape, F32), (taps.shape, F32)], [got, norm],
-    )
-    return grad_inputs[None], grad_gate_li[None], grad_gate_mr[None], grad_residues, grad_taps
+        [((modes, groups), F32), (taps.shape, F32)], [got, norm.T],
+    )
+    return grad_inputs[None], grad_gate_li[None], grad_gate_mr[None], grad_residues.T, grad_taps
 
 
 def solution(mesh):

time: 131 us -> 124 us (0.947)
  local copies, waits for them, and re-layouts: 7.77 us -> 3.24 us
    unnamed x37 -> x31, local copies, waits for them, and re-layouts: 7.33 us -> 2.81 us
    pallas_call x6, Pallas kernels: 42.8 us -> 38.6 us  [call(): pl.pallas_call(kernel, grid=(width // step,), in_specs=[block(rows) for r...]
    all_to_all x4, waiting for transfers between devices: 21.5 us -> 19.8 us  [exchange(): return lax.all_to_all(x, axes, split_axis=0, concat_axis=0, tiled=True)]
    pallas_call x1, Pallas kernels: 1.54 us -> 3.06 us  [on_device(): pl.pallas_call(functools.partial(prepare_kernel, size, own_rows), in_spec...]
    pallas_call x4, Pallas kernels: 4 us -> 5.42 us  [whole(): pl.pallas_call(body, out_shape=[jax.ShapeDtypeStruct(shape, kind) for sha...]
  transfers between devices with their start and end apart: 6 -> 6, of which waited for: 3 -> 5; matrix products, arithmetic and copies ran while one was open for 2% -> 2% of each run, Pallas kernels for 29% -> 30%
where the time goes in v4:
time: 124 us; the launch traced here: 123 us
  starting transfers between devices  47.6 us (38%)
  Pallas kernels  47.1 us (38%)
  waiting for transfers between devices  20.3 us (16%)
  other arithmetic  4.19 us (3%)
  local copies, waits for them, and re-layouts  3.24 us (3%)
    all_to_all x4, starting transfers between devices, exchange(): return lax.all_to_all(x, axes, split_axis=0, concat_axis=0, tiled=True)  39.8 us
    pallas_call x6, Pallas kernels, call(): pl.pallas_call(kernel, grid=(width // step,), in_specs=[block(rows) for r...  38.6 us
    all_to_all x4, waiting for transfers between devices, exchange(): return lax.all_to_all(x, axes, split_axis=0, concat_axis=0, tiled=True)  19.8 us
    ppermute x2, starting transfers between devices, shifted(): lax.ppermute(x, 'ctx', [(i, i + by) for i in range(count) if 0 <= i + by...  7.77 us
    pallas_call x4, Pallas kernels, whole(): pl.pallas_call(body, out_shape=[jax.ShapeDtypeStruct(shape, kind) for sha...  5.42 us
    pallas_call x1, Pallas kernels, on_device(): pl.pallas_call(functools.partial(prepare_kernel, size, own_rows), in_spec...  3.06 us
    unnamed x31, local copies, waits for them, and re-layouts  2.81 us
  transfers between devices with their start and end apart: 6, of which 5 were waited for; matrix products, arithmetic and copies ran while one was open for 2% of the time, Pallas kernels for 30%

profile of v4, /device:TPU:1, one launch (start us, length us, event | category | flops | bytes accessed | tf_op | source)
XLA Modules:
  0.0 123.2 jit_solution(16266017320102566189)
XLA Ops:
  0.6 0.0 copy-start.12
  0.6 0.0 copy-start.13
  0.7 1.8 %fusion.refs_0_.refs_3_ = bf16[128,4096]{1,0:T(8,128)(2,1)S(1)} fusion(bf16[1,128,4096]{2,1,0:T(8,128)(2,1)} %param.9, bf16[1,128,4096]{2,1,0:T(8,128)(2,1)} %param.10), kind=kLoop, calls=%fused_computation.1 | loop fusion | flops 2097152 | bytes 3145728 | tf_op jit(solution)/shard_map/convert_element_type | solution.py:370
  2.5 0.0 copy-start.8
  2.5 5.1 %collective-permute-start = (bf16[128,4096]{1,0:T(8,128)(2,1)S(1)}, bf16[128,4096]{1,0:T(8,128)(2,1)S(1)}, u32[]{:S(2)}, u32[]{:S(2)}) collective-permute-start(bf16[128,4096]{1,0:T(8,128)(2,1)S(1)} %fusion.refs_0_.refs_3_), channel_id=1, source_target_pairs={{1,0},{2,1},{3,2},{4,3},{5,4},{6,5},{7,6},{8,7},{9,8},{10,9},{11,1... | collective-permute-start | bytes 3145736 | tf_op jit(solution)/shard_map/ppermute | solution.py:347
  7.6 0.0 copy-done.12
  7.6 0.0 copy-done.13
  7.7 0.1 copy.17
  7.8 0.1 mul.44
  7.9 1.7 %multiply_exponential_fusion = (f32[2048,128]{1,0:T(8,128)}, f32[2048,128]{1,0:T(8,128)}) fusion(f32[128]{0:T(128)S(1)} %get-tuple-element.62, f32[2048]{0:T(1024)S(1)} %mul.44, f32[128]{0:T(128)S(1)} %get-tuple-element.63), kind=kLoop, calls=%fused_computation.2 | loop fusion | flops 524288 | bytes 2106368 | tf_op jit(solution)/shard_map/exp | solution.py:377
  9.5 2.5 %shard_map.113 = f32[512,128]{1,0:T(8,128)} custom-call(bf16[128,4096]{1,0:T(8,128)(2,1)} %bitcast.23, f32[2048,128]{1,0:T(8,128)} %get-tuple-element.60.refs_1_), custom_call_target="tpu_custom_call" | custom-call | flops 3000000000 | bytes 2097152 | tf_op jit(solution)/shard_map/pallas_call | solution.py:325
  12.0 0.0 copy-done.8
  12.0 10.7 %all-to-all-start = ((f32[128,4,128]{2,1,0:T(4,128)}), f32[128,4,128]{2,1,0:T(4,128)S(1)}, u32[]{:S(2)}, u32[]{:S(2)}) async-start(f32[128,4,128]{2,1,0:T(4,128)} %bitcast.21), calls=%async_computation | async-start | bytes 524288 | tf_op jit(solution)/shard_map/all_to_all | solution.py:351
  22.7 0.1 copy.15.rates_ref
  22.8 0.0 copy-start.9
  22.8 0.1 copy.16.weight_ref
  22.9 0.0 copy-start.10
  22.9 0.1 reshape.50
  23.0 0.1 reshape.49
  23.1 0.7 pad_maximum_fusion
  23.8 0.0 copy-done.9
  23.8 0.0 copy-done.10
  23.8 3.1 %shard_map.110 = (f32[128,128]{1,0:T(8,128)}, f32[128,128]{1,0:T(8,128)}, f32[128,128]{1,0:T(8,128)}, f32[4,128]{1,0:T(4,128)}, f32[16,128]{1,0:T(8,128)}) custom-call(s32[1,1]{1,0:T(1,128)} %bitcast.2.me_ref, f32[128,16]{1,0:T(8,128)} %copy-done.9, f32[128,16]{1,0:T(8,128)} %copy-done.10, f32[128,128]{1,0:T(8,128)} %refs_3_.1), custom_call_target="tpu_custom_call" | custom-call | flops 3000000000 | bytes 1048576 | tf_op jit(solution)/shard_map/pallas_call | solution.py:386
  26.9 0.0 collective-permute-done.refs_1_.refs_4_
  26.9 0.0 copy-start.14
  26.9 1.0 copy-done.14
  27.9 0.0 copy-start.6
  27.9 7.7 %shard_map.111 = (f32[128,4096]{1,0:T(8,128)}, f32[512,128]{1,0:T(8,128)}) custom-call(bf16[128,4096]{1,0:T(8,128)(2,1)} %copy-done.8, bf16[128,4096]{1,0:T(8,128)(2,1)} %copy-done.14, bf16[128,4096]{1,0:T(8,128)(2,1)} %bitcast.25, f32[128,128]{1,0:T(8,128)} %refs_3_.1, f32[2048,128]{1,0:T(8,128)} %get-tuple-element.61.refs_4_), custom_call_target="tpu_custom_call" | custom-call | flops 8000000000 | bytes 4259840 | tf_op jit(solution)/shard_map/pallas_call | solution.py:325
  35.6 0.4 all-to-all-done.x_ref
  36.0 0.0 copy-done.6
  36.0 0.0 copy-start.3
  36.0 0.9 copy-done.3
  36.9 1.0 shard_map.114.front_ref
  37.9 11.3 %all-to-all-start.1 = ((bf16[128,8,128]{2,1,0:T(8,128)(2,1)}), bf16[128,8,128]{2,1,0:T(8,128)(2,1)S(1)}, u32[]{:S(2)}, u32[]{:S(2)}) async-start(bf16[128,8,128]{2,1,0:T(8,128)(2,1)} %shard_map.114.front_ref), calls=%async_computation.1 | async-start | bytes 524288 | tf_op jit(solution)/shard_map/all_to_all | solution.py:351
  49.2 9.2 %shard_map.112 = (f32[128,4096]{1,0:T(8,128)}, bf16[4096,128]{1,0:T(8,128)(2,1)}, bf16[4096,128]{1,0:T(8,128)(2,1)}, f32[128,128]{1,0:T(8,128)}) custom-call(bf16[128,4096]{1,0:T(8,128)(2,1)} %bitcast.24, bf16[128,4096]{1,0:T(8,128)(2,1)} %bitcast.26, f32[128,4096]{1,0:T(8,128)} %get-tuple-element.37.refs_2_.refs_0_, f32[128,128]{1,0:T(8,128)} %get-tuple-element.39.refs_3_, ...), custom_call_target="tpu_custom_call" | custom-call | flops 10000000000 | bytes 4292608 | tf_op jit(solution)/shard_map/pallas_call | solution.py:325
  58.4 4.0 %all-to-all-done.1.x_ref = bf16[128,8,128]{2,1,0:T(8,128)(2,1)S(1)} async-done(((bf16[128,8,128]{2,1,0:T(8,128)(2,1)}), bf16[128,8,128]{2,1,0:T(8,128)(2,1)S(1)}, u32[]{:S(2)}, u32[]{:S(2)}) %all-to-all-start.1) | async-done | bytes 262176 | tf_op jit(solution)/shard_map/all_to_all | solution.py:351
  62.5 0.0 copy-start.11
  62.5 0.7 copy-done.11
  63.2 6.7 %shard_map.115 = (bf16[128,4096]{1,0:T(8,128)(2,1)}, bf16[128,4096]{1,0:T(8,128)(2,1)}, f32[128,128]{1,0:T(8,128)}) custom-call(f32[128,4096]{1,0:T(8,128)} %get-tuple-element.43.refs_0_, bf16[128,4096]{1,0:T(8,128)(2,1)} %bitcast.27, f32[128,4096]{1,0:T(8,128)} %get-tuple-element.37.refs_2_.refs_0_, bf16[128,4096]{1,0:T(8,128)(2,1)} %copy-done.8, ...), custom_call_target="tpu_custom_call" | custom-call | flops 6000000000 | bytes 8650752 | tf_op jit(solution)/shard_map/pallas_call | solution.py:325
  69.9 2.6 %collective-permute-start.1 = (bf16[128,4096]{1,0:T(8,128)(2,1)}, bf16[128,4096]{1,0:T(8,128)(2,1)S(1)}, u32[]{:S(2)}, u32[]{:S(2)}) collective-permute-start(bf16[128,4096]{1,0:T(8,128)(2,1)} %get-tuple-element.48.refs_0_), channel_id=1, source_target_pairs={{0,1},{1,2},{2,3},{3,4},{4,5},{5,6},{6,7},{7,8},{8,9},{9,10},{10,1... | collective-permute-start | bytes 3145736 | tf_op jit(solution)/shard_map/ppermute | solution.py:347
  72.6 0.0 copy-start
  72.6 0.0 copy-start.2
  72.6 0.0 copy-start.4
  72.6 2.2 %shard_map.116 = (bf16[128,8,128]{2,1,0:T(8,128)(2,1)}, f32[4,128]{1,0:T(4,128)}) custom-call(bf16[128,8,128]{2,1,0:T(8,128)(2,1)} %copy-done.11, f32[4,128]{1,0:T(4,128)} %get-tuple-element.41.decay_ref, bf16[128,8,128]{2,1,0:T(8,128)(2,1)} %shard_map.114.front_ref, f32[128,128]{1,0:T(8,128)} %get-tuple-element.45.tap_ref, f32[128,128]{1,0:T(8,128)} %get-tuple-element.46.cot_ref), custom_call_target="tpu_custom_call" | custom-call | flops 2000000000 | bytes 1048576 | tf_op jit(solution)/shard_map/pallas_call | solution.py:337
  74.8 9.2 %all-to-all-start.2 = ((bf16[128,8,128]{2,1,0:T(8,128)(2,1)}), bf16[128,8,128]{2,1,0:T(8,128)(2,1)S(1)}, u32[]{:S(2)}, u32[]{:S(2)}) async-start(bf16[128,8,128]{2,1,0:T(8,128)(2,1)} %get-tuple-element.47), calls=%async_computation.2 | async-start | bytes 524288 | tf_op jit(solution)/shard_map/all_to_all | solution.py:351
  84.1 0.5 collective-permute-done.1.refs_1_
  84.6 0.0 copy-done
  84.6 0.0 copy-done.2
  84.6 0.0 copy-done.4
  84.6 0.0 copy-start.5
  84.6 0.0 copy-start.7
  84.6 5.9 %shard_map.117 = bf16[128,4096]{1,0:T(8,128)(2,1)} custom-call(bf16[128,4096]{1,0:T(8,128)(2,1)S(1)} %copy-done.2, bf16[128,4096]{1,0:T(8,128)(2,1)S(1)} %collective-permute-done.1.refs_1_, f32[128,128]{1,0:T(8,128)S(1)} %copy-done.4, bf16[128,4096]{1,0:T(8,128)(2,1)S(1)} %bitcast.18), custom_call_target="tpu_custom_call" | custom-call | flops 7000000000 | bytes 3211264 | tf_op jit(solution)/shard_map/pallas_call | solution.py:325
  90.5 6.8 %all-to-all-done.2.x_ref = bf16[128,8,128]{2,1,0:T(8,128)(2,1)S(1)} async-done(((bf16[128,8,128]{2,1,0:T(8,128)(2,1)}), bf16[128,8,128]{2,1,0:T(8,128)(2,1)S(1)}, u32[]{:S(2)}, u32[]{:S(2)}) %all-to-all-start.2) | async-done | bytes 262176 | tf_op jit(solution)/shard_map/all_to_all | solution.py:351
  97.3 0.0 copy-start.1
  97.3 0.0 copy-done.5
  97.3 0.0 copy-done.7
  97.3 1.3 %shard_map.119 = f32[256,2,128]{2,1,0:T(2,128)} custom-call(bf16[128,8,128]{2,1,0:T(8,128)(2,1)S(1)} %all-to-all-done.2.x_ref, f32[4,128]{1,0:T(4,128)S(1)} %copy-done.7, f32[16,128]{1,0:T(8,128)S(1)} %copy-done.5), custom_call_target="tpu_custom_call" | custom-call | flops 2000000000 | bytes 1048576 | tf_op jit(solution)/shard_map/pallas_call | solution.py:337
  98.6 0.0 copy-done.1
  98.6 8.6 %all-to-all-start.3 = ((f32[256,2,128]{2,1,0:T(2,128)}), f32[256,2,128]{2,1,0:T(2,128)S(1)}, u32[]{:S(2)}, u32[]{:S(2)}) async-start(f32[256,2,128]{2,1,0:T(2,128)} %shard_map.119), calls=%async_computation.3 | async-start | bytes 524288 | tf_op jit(solution)/shard_map/all_to_all | solution.py:351
  107.2 6.6 %shard_map.118 = bf16[128,4096]{1,0:T(8,128)(2,1)} custom-call(f32[128,4096]{1,0:T(8,128)} %get-tuple-element.37.refs_2_.refs_0_, bf16[128,4096]{1,0:T(8,128)(2,1)} %bitcast.28, f32[128,128]{1,0:T(8,128)} %get-tuple-element.38.refs_2_, bf16[4096,128]{1,0:T(8,128)(2,1)} %get-tuple-element.40.refs_3_, bf16[1024,128]{1,0:T(8,128)(2,1)} %bitcast.19), custom_call_target="tpu_custom_call" | custom-call | flops 7000000000 | bytes 4521984 | tf_op jit(solution)/shard_map/pallas_call | solution.py:325
  113.7 8.6 %all-to-all-done.3.x_ref = f32[256,2,128]{2,1,0:T(2,128)S(1)} async-done(((f32[256,2,128]{2,1,0:T(2,128)}), f32[256,2,128]{2,1,0:T(2,128)S(1)}, u32[]{:S(2)}, u32[]{:S(2)}) %all-to-all-start.3) | async-done | bytes 262176 | tf_op jit(solution)/shard_map/all_to_all | solution.py:351
  122.3 0.9 shard_map.120
  (2 shorter events, 0.0 us)
Async XLA Ops:
  0.6 7.0 %copy-start.12 = (f32[128,16]{0,1:T(8,128)S(1)}, f32[128,16]{0,1:T(8,128)}, u32[]{:S(2)}) copy-start(f32[128,16]{0,1:T(8,128)} %param.12) | copy-start | bytes 24580
  0.6 7.0 %copy-start.13 = (f32[128,16]{0,1:T(8,128)S(1)}, f32[128,16]{0,1:T(8,128)}, u32[]{:S(2)}) copy-start(f32[128,16]{0,1:T(8,128)} %param.11) | copy-start | bytes 24580
  2.5 9.6 %copy-start.8 = (bf16[128,4096]{1,0:T(8,128)(2,1)}, bf16[128,4096]{1,0:T(8,128)(2,1)S(1)}, u32[]{:S(2)}) copy-start(bf16[128,4096]{1,0:T(8,128)(2,1)S(1)} %fusion.refs_0_.refs_3_) | copy-start | bytes 3145732
  2.5 24.4 %collective-permute-start = (bf16[128,4096]{1,0:T(8,128)(2,1)S(1)}, bf16[128,4096]{1,0:T(8,128)(2,1)S(1)}, u32[]{:S(2)}, u32[]{:S(2)}) collective-permute-start(bf16[128,4096]{1,0:T(8,128)(2,1)S(1)} %fusion.refs_0_.refs_3_), channel_id=1, source_target_pairs={{1,0},{2,1},{3,2},{4,3},{5,4},{6,5},{7,6},{8,7},{9,8},{10,9},{11,1... | collective-permute-start | bytes 3145736 | tf_op jit(solution)/shard_map/ppermute | solution.py:347
  12.0 23.9 %all-to-all-start = ((f32[128,4,128]{2,1,0:T(4,128)}), f32[128,4,128]{2,1,0:T(4,128)S(1)}, u32[]{:S(2)}, u32[]{:S(2)}) async-start(f32[128,4,128]{2,1,0:T(4,128)} %bitcast.21), calls=%async_computation | async-start | bytes 524288 | tf_op jit(solution)/shard_map/all_to_all | solution.py:351
  22.8 1.0 copy-start.9
  22.9 0.9 copy-start.10
  26.9 1.0 copy-start.14
  27.9 8.1 %copy-start.6 = (f32[4,128]{1,0:T(4,128)S(1)}, f32[4,128]{1,0:T(4,128)}, u32[]{:S(2)}) copy-start(f32[4,128]{1,0:T(4,128)} %get-tuple-element.41.decay_ref) | copy-start | bytes 6148
  36.0 1.0 copy-start.3
  37.9 24.6 %all-to-all-start.1 = ((bf16[128,8,128]{2,1,0:T(8,128)(2,1)}), bf16[128,8,128]{2,1,0:T(8,128)(2,1)S(1)}, u32[]{:S(2)}, u32[]{:S(2)}) async-start(bf16[128,8,128]{2,1,0:T(8,128)(2,1)} %shard_map.114.front_ref), calls=%async_computation.1 | async-start | bytes 524288 | tf_op jit(solution)/shard_map/all_to_all | solution.py:351
  62.5 0.7 copy-start.11
  69.9 14.7 %collective-permute-start.1 = (bf16[128,4096]{1,0:T(8,128)(2,1)}, bf16[128,4096]{1,0:T(8,128)(2,1)S(1)}, u32[]{:S(2)}, u32[]{:S(2)}) collective-permute-start(bf16[128,4096]{1,0:T(8,128)(2,1)} %get-tuple-element.48.refs_0_), channel_id=1, source_target_pairs={{0,1},{1,2},{2,3},{3,4},{4,5},{5,6},{6,7},{7,8},{8,9},{9,10},{10,1... | collective-permute-start | bytes 3145736 | tf_op jit(solution)/shard_map/ppermute | solution.py:347
  72.6 12.0 %copy-start = (bf16[1,128,4096]{2,1,0:T(8,128)(2,1)S(1)}, bf16[1,128,4096]{2,1,0:T(8,128)(2,1)}, u32[]{:S(2)}) copy-start(bf16[1,128,4096]{2,1,0:T(8,128)(2,1)} %param.10) | copy-start | bytes 3145732
  72.6 12.0 %copy-start.2 = (bf16[128,4096]{1,0:T(8,128)(2,1)S(1)}, bf16[128,4096]{1,0:T(8,128)(2,1)}, u32[]{:S(2)}) copy-start(bf16[128,4096]{1,0:T(8,128)(2,1)} %get-tuple-element.48.refs_0_) | copy-start | bytes 3145732
  72.6 12.0 %copy-start.4 = (f32[128,128]{1,0:T(8,128)S(1)}, f32[128,128]{1,0:T(8,128)}, u32[]{:S(2)}) copy-start(f32[128,128]{1,0:T(8,128)} %get-tuple-element.49.refs_2_) | copy-start | bytes 196612
  74.8 22.5 %all-to-all-start.2 = ((bf16[128,8,128]{2,1,0:T(8,128)(2,1)}), bf16[128,8,128]{2,1,0:T(8,128)(2,1)S(1)}, u32[]{:S(2)}, u32[]{:S(2)}) async-start(bf16[128,8,128]{2,1,0:T(8,128)(2,1)} %get-tuple-element.47), calls=%async_computation.2 | async-start | bytes 524288 | tf_op jit(solution)/shard_map/all_to_all | solution.py:351
  84.6 12.7 %copy-start.5 = (f32[16,128]{1,0:T(8,128)S(1)}, f32[16,128]{1,0:T(8,128)}, u32[]{:S(2)}) copy-start(f32[16,128]{1,0:T(8,128)} %get-tuple-element.54.lam_ref) | copy-start | bytes 24580
  84.6 12.7 %copy-start.7 = (f32[4,128]{1,0:T(4,128)S(1)}, f32[4,128]{1,0:T(4,128)}, u32[]{:S(2)}) copy-start(f32[4,128]{1,0:T(4,128)} %get-tuple-element.53.sum_ref) | copy-start | bytes 6148
  97.3 1.3 %copy-start.1 = (bf16[128,8,128]{2,1,0:T(8,128)(2,1)}, bf16[128,8,128]{2,1,0:T(8,128)(2,1)S(1)}, u32[]{:S(2)}) copy-start(bf16[128,8,128]{2,1,0:T(8,128)(2,1)S(1)} %all-to-all-done.2.x_ref) | copy-start | bytes 786436
  98.6 23.7 %all-to-all-start.3 = ((f32[256,2,128]{2,1,0:T(2,128)}), f32[256,2,128]{2,1,0:T(2,128)S(1)}, u32[]{:S(2)}, u32[]{:S(2)}) async-start(f32[256,2,128]{2,1,0:T(2,128)} %shard_map.119), calls=%async_computation.3 | async-start | bytes 524288 | tf_op jit(solution)/shard_map/all_to_all | solution.py:351

commit v5 on v4

--- a/solution.py
+++ b/solution.py
@@ -106,16 +106,17 @@
     return [slice(i * LANES, (i + 1) * LANES) for i in range(ref.shape[1] // LANES)]
 
 
-def states_kernel(size, modes, x_ref, table_ref, out_ref):
+def states_kernel(size, modes, x_ref, rate_ref, out_ref):
     rows = LANES // size * modes
+    steps = LANES - 1.0 - iota((rows, LANES), 1).astype(F32)
     out = [
-        mode_sums(table_ref[i * rows : (i + 1) * rows, :], x_ref[:, lanes], size, modes)
+        mode_sums(jnp.exp(-rate_ref[i * rows : (i + 1) * rows, :] * steps), x_ref[:, lanes], size, modes)
         for i, lanes in enumerate(tiles_of(x_ref))
     ]
     out_ref[...] = jnp.concatenate(out, axis=0)
 
 
-def mixer_back_kernel(size, modes, own_ref, next_ref, gate_ref, taps_ref, table_ref, gm_ref, out_ref):
+def mixer_back_kernel(size, modes, own_ref, next_ref, gate_ref, taps_ref, rate_ref, gm_ref, out_ref):
     per = LANES // size
     rows = per * modes
     row, col = iota((LANES, LANES), 0), iota((LANES, LANES), 1)
@@ -128,8 +129,10 @@
         grad_mixer = pick_groups(prod, LANES, size)
         gm_ref[:, lanes] = grad_mixer
         cots.append(grad_mixer * gate_ref[:, lanes].astype(F32))
-    for i, lanes in enumerate(tiles):
-        out.append(mode_sums(table_ref[i * rows : (i + 1) * rows, :], cots[i], size, modes))
+    steps = iota((rows, LANES), 1).astype(F32) + 1.0
+    for i, lanes in enumerate(tiles):
+        table = jnp.exp(-rate_ref[i * rows : (i + 1) * rows, :] * steps)
+        out.append(mode_sums(table, cots[i], size, modes))
     out_ref[...] = jnp.concatenate(out, axis=0)
 
 
@@ -160,8 +163,7 @@
 
 
 def values_kernel(
-    size, modes, local_ref, gate_ref, gm_ref, own_ref, next_ref, table_ref, enter_ref,
-    mix_ref, ggl_ref, lag_ref,
+    size, modes, local_ref, gate_ref, own_ref, next_ref, table_ref, enter_ref, mix_ref, lag_ref
 ):
     per = LANES // size
     row, col = iota((LANES, LANES), 0), iota((LANES, LANES), 1)
@@ -170,7 +172,6 @@
     for i, lanes in enumerate(tiles):
         table = table_ref[i * LANES : (i + 1) * LANES, :]
         full = local_ref[:, lanes] + carried_part(table, enter_ref, i, modes, size)
-        ggl_ref[:, lanes] = (gm_ref[:, lanes] * full).astype(BF16)
         mixes.append((gate_ref[:, lanes].astype(F32) * full).astype(BF16))
     for i, lanes in enumerate(tiles):
         mix_ref[:, lanes] = mixes[i]
@@ -180,6 +181,13 @@
             z = pairs[g * LANES : (g + 1) * LANES]
             lag_parts.append(lag_rows(jnp.where(col >= row, z[:, :LANES], z[:, LANES:])))
     lag_ref[...] = lag_sums(lag_parts)
+
+
+def gate_grad_kernel(size, modes, local_ref, gm_ref, table_ref, enter_ref, out_ref):
+    for i, lanes in enumerate(tiles_of(local_ref)):
+        table = table_ref[i * LANES : (i + 1) * LANES, :]
+        full = local_ref[:, lanes] + carried_part(table, enter_ref, i, modes, size)
+        out_ref[:, lanes] = (gm_ref[:, lanes] * full).astype(BF16)
 
 
 def input_grad_kernel(size, modes, gm_ref, gate_ref, filt_ref, table_ref, enter_ref, out_ref):
@@ -213,22 +221,23 @@
     )
 
 
-def prepare_kernel(
-    size, own_rows, me_ref, rates_ref, weight_ref, taps_ref, filt_ref, filt_back_ref, taps_back_ref,
-    decay_ref, lam_ref,
-):
-    me = me_ref[0, 0]
+def filters_kernel(rates_ref, weight_ref, taps_ref, filt_ref, filt_back_ref, taps_back_ref):
     rates, taps = rates_ref[...], taps_ref[...]
     groups, modes = rates.shape
     lag = iota((groups, LANES), 1).astype(F32)
     filt = jnp.zeros((groups, LANES), F32)
     for m in range(modes):
         filt = filt + weight_ref[:, m : m + 1] * jnp.exp(-rates[:, m : m + 1] * lag)
-    row, col = iota((LANES, LANES), 0), iota((LANES, LANES), 1)
-    mirror = ((row + col) % LANES == 0).astype(F32)
+    mirror = ((iota((LANES, LANES), 0) + iota((LANES, LANES), 1)) % LANES == 0).astype(F32)
     filt_ref[...] = filt
     filt_back_ref[...] = exact_dot(filt, mirror)
     taps_back_ref[...] = exact_dot(taps, mirror)
+
+
+def owner_kernel(size, own_rows, me_ref, rates_ref, decay_ref, lam_ref):
+    me = me_ref[0, 0]
+    rates = rates_ref[...]
+    groups, modes = rates.shape
     per, parts = LANES // size, modes // own_rows
     pick = iota((8, modes), 1) == me % parts * own_rows + iota((8, modes), 0)
     chosen = exact_dot(pick.astype(F32), rates, NT)
@@ -370,61 +379,52 @@
     scaled = (cot.astype(F32) * gate_mr[0].astype(F32)).astype(BF16)
     after = shifted(scaled, -1)
 
-    lags = jnp.arange(LANES).astype(F32)
     norm = jnp.sqrt(-jnp.expm1(-2.0 * rates))
     weight = residues * norm
-    rate3, weight3 = rates[:, :, None], weight[:, :, None]
-    to_end = jnp.exp(-rate3 * (LANES - 1.0 - lags))
-    from_start = jnp.exp(-rate3 * (lags + 1.0))
-    flat = (groups * modes, LANES)
-    end_table = to_end.reshape(flat)
-    start_table = from_start.reshape(flat)
+    rate_rows = jnp.broadcast_to(rates.reshape(-1, 1), (groups * modes, LANES))
     rate_row = rates.reshape(tiles, per * modes)
     rate_row = jnp.concatenate([rate_row, rate_row], axis=1)
     weight_row = weight.reshape(tiles, per * modes)
     weight_row = jnp.concatenate([weight_row, weight_row], axis=1)
-    filt, filt_back, taps_back, decay, lam_own = pl.pallas_call(
-        functools.partial(prepare_kernel, size, own_rows),
-        in_specs=[pl.BlockSpec(memory_space=pltpu.SMEM)] + [pl.BlockSpec(memory_space=pltpu.VMEM)] * 3,
+    decay, lam_own = pl.pallas_call(
+        functools.partial(owner_kernel, size, own_rows),
+        in_specs=[pl.BlockSpec(memory_space=pltpu.SMEM), pl.BlockSpec(memory_space=pltpu.VMEM)],
         out_shape=[
-            jax.ShapeDtypeStruct(shape, F32)
-            for shape in (taps.shape, taps.shape, taps.shape, (own_rows, LANES), (modes, LANES))
+            jax.ShapeDtypeStruct((own_rows, LANES), F32), jax.ShapeDtypeStruct((modes, LANES), F32)
         ],
-        compiler_params=pltpu.CompilerParams(vmem_limit_bytes=60 * 1024 * 1024),
-        cost_estimate=pl.CostEstimate(flops=3_000_000_000, bytes_accessed=1 << 20, transcendentals=0),
-    )(me.astype(jnp.int32).reshape(1, 1), rates, weight, taps)
-
+        compiler_params=pltpu.CompilerParams(vmem_limit_bytes=8 * 1024 * 1024),
+        cost_estimate=pl.CostEstimate(flops=1_000_000_000, bytes_accessed=1 << 16, transcendentals=0),
+    )(me.astype(jnp.int32).reshape(1, 1), rates)
     bind = functools.partial
     states = call(
         bind(states_kernel, size, modes), width, step, chunk, [None, table_rows], [(state_rows, F32)],
-        [seq, end_table], 3,
+        [seq, rate_rows], 3,
     )[0]
     ends = exchange(states.reshape(count, own_rows, LANES))
 
-    after, filt, filt_back, taps_back, decay, lam_own = lax.optimization_barrier(
-        (after, filt, filt_back, taps_back, decay, lam_own)
-    )
+    after, decay, lam_own = lax.optimization_barrier((after, decay, lam_own))
     grad_mixer, back_states = call(
         bind(mixer_back_kernel, size, modes), width, step, chunk,
         [None, None, None, group_rows, table_rows], [(None, F32), (state_rows, F32)],
-        [scaled, after, gate, taps, start_table], 8,
+        [scaled, after, gate, taps, rate_rows], 8,
     )
     first = whole(
         scan_kernel, [((count, 2 * own_rows, LANES), BF16)],
         [ends, decay, back_states.reshape(count, own_rows, LANES)],
     )[0]
     second = exchange(first)
+    late = lax.optimization_barrier((rates, weight, taps, first))[:3]
+    filt, filt_back, taps_back = whole(filters_kernel, [(taps.shape, F32)] * 3, late, 60)
     local, front_table, back_table, lag_cot = call(
         bind(local_kernel, size), width, step, chunk,
         [None, None, None, group_rows, tile_rows, tile_rows],
         [(None, F32), (carry_rows, BF16), (carry_rows, BF16), (group_rows, F32)],
         [seq, gate, grad_mixer, filt_back, rate_row, weight_row], 10,
     )
-    mixer_in, grad_gate_li, lag_taps = call(
+    mixer_in, lag_taps = call(
         bind(values_kernel, size, modes), width, step, chunk,
-        [None, None, None, None, None, carry_rows, 2 * state_rows],
-        [(None, BF16), (None, BF16), (group_rows, F32)],
-        [local, gate, grad_mixer, scaled, after, front_table, second.reshape(-1, LANES)], 6,
+        [None, None, None, None, carry_rows, 2 * state_rows], [(None, BF16), (group_rows, F32)],
+        [local, gate, scaled, after, front_table, second.reshape(-1, LANES)], 6,
     )
     before = shifted(mixer_in, 1)
     message, state_sums = whole(
@@ -432,11 +432,15 @@
         [second, decay, first, lag_taps, lag_cot], 60,
     )
     third = exchange(message)
+    grad_gate_li = call(
+        bind(gate_grad_kernel, size, modes), width, step, chunk,
+        [None, None, carry_rows, 2 * state_rows], [(None, BF16)],
+        [local, grad_mixer, front_table, second.reshape(-1, LANES)], 4,
+    )[0]
     grad_gate_mr = call(
         bind(mixer_kernel, size), width, step, chunk, [None, None, group_rows, None], [(None, BF16)],
         [mixer_in, before, taps_back, cot], 7, 32,
     )[0]
-    third, grad_gate_mr = lax.optimization_barrier((third, grad_gate_mr))
     spread = whole(
         bind(collect_kernel, size), [((reps * count, 2, LANES), F32)], [third, state_sums, lam_own]
     )[0]
@@ -446,6 +450,7 @@
         [None, None, group_rows, carry_rows, 2 * state_rows], [(None, BF16)],
         [grad_mixer, gate, filt, back_table, third.reshape(-1, LANES)], 7,
     )[0]
+    got, grad_gate_mr = lax.optimization_barrier((got, grad_gate_mr))
     grad_residues, grad_taps = whole(
         bind(finish_kernel, 1.0 / math.sqrt(reps * count * LANES), per, own_rows),
         [((modes, groups), F32), (taps.shape, F32)], [got, norm.T],

time: 124 us -> 133 us (1.073)
  starting transfers between devices: 47.6 us -> 50.9 us
  Pallas kernels: 47.1 us -> 50.1 us
  local copies, waits for them, and re-layouts: 3.24 us -> 5.89 us
  waiting for transfers between devices: 20.3 us -> 22.7 us
  other arithmetic: 4.19 us -> 2.52 us
    pallas_call x6 -> x7, Pallas kernels: 38.6 us -> 41.7 us  [call(): pl.pallas_call(kernel, grid=(width // step,), in_specs=[block(rows) for r...]
    all_to_all x4, waiting for transfers between devices: 19.8 us -> 22.6 us  [exchange(): return lax.all_to_all(x, axes, split_axis=0, concat_axis=0, tiled=True)]
    pallas_call x1, Pallas kernels: 3.06 us -> 0.62 us  [on_device(): pl.pallas_call(functools.partial(owner_kernel, size, own_rows), in_specs=...]
    pallas_call x4 -> x5, Pallas kernels: 5.42 us -> 7.82 us  [whole(): pl.pallas_call(body, out_shape=[jax.ShapeDtypeStruct(shape, kind) for sha...]
    all_to_all x4, starting transfers between devices: 39.8 us -> 42.2 us  [exchange(): return lax.all_to_all(x, axes, split_axis=0, concat_axis=0, tiled=True)]
    exp x1 -> x0, other arithmetic: 1.67 us -> none  [on_device(): to_end = jnp.exp(-rate3 * (LANES - 1.0 - lags))]
    optimization_barrier x0 -> x2, local copies, waits for them, and re-layouts: none -> 1.46 us  [on_device(): late = lax.optimization_barrier((rates, weight, taps, first))[:3]]
    broadcast_in_dim x0 -> x2, local copies, waits for them, and re-layouts: none -> 1.4 us  [on_device(): rate_rows = jnp.broadcast_to(rates.reshape(-1, 1), (groups * modes, LANES))]
  transfers between devices with their start and end apart: 6 -> 6, of which waited for: 5 -> 4; matrix products, arithmetic and copies ran while one was open for 2% -> 3% of each run, Pallas kernels for 30% -> 30%
where the time goes in v5:
time: 133 us
  starting transfers between devices  50.9 us (38%)
  Pallas kernels  50.1 us (38%)
  waiting for transfers between devices  22.7 us (17%)
  local copies, waits for them, and re-layouts  5.89 us (4%)
  other arithmetic  2.52 us (2%)
    all_to_all x4, starting transfers between devices, exchange(): return lax.all_to_all(x, axes, split_axis=0, concat_axis=0, tiled=True)  42.2 us
    pallas_call x7, Pallas kernels, call(): pl.pallas_call(kernel, grid=(width // step,), in_specs=[block(rows) for r...  41.7 us
    all_to_all x4, waiting for transfers between devices, exchange(): return lax.all_to_all(x, axes, split_axis=0, concat_axis=0, tiled=True)  22.6 us
    ppermute x2, starting transfers between devices, shifted(): lax.ppermute(x, 'ctx', [(i, i + by) for i in range(count) if 0 <= i + by...  8.69 us
    pallas_call x5, Pallas kernels, whole(): pl.pallas_call(body, out_shape=[jax.ShapeDtypeStruct(shape, kind) for sha...  7.82 us
    unnamed x25, local copies, waits for them, and re-layouts  2.78 us
  transfers between devices with their start and end apart: 6, of which 4 were waited for; matrix products, arithmetic and copies ran while one was open for 3% of the time, Pallas kernels for 30%

profile of v5, /device:TPU:1, one launch (start us, length us, event | category | flops | bytes accessed | tf_op | source)
XLA Modules:
  0.0 132.9 jit_solution(94779943131446078)
XLA Ops:
  0.6 0.0 copy-start.9
  0.6 1.8 %fusion.refs_0_.refs_2_ = bf16[128,4096]{1,0:T(8,128)(2,1)S(1)} fusion(bf16[1,128,4096]{2,1,0:T(8,128)(2,1)} %param.9, bf16[1,128,4096]{2,1,0:T(8,128)(2,1)} %param.10), kind=kLoop, calls=%fused_computation.1 | loop fusion | flops 2097152 | bytes 3145728 | tf_op jit(solution)/shard_map/convert_element_type | solution.py:379
  2.4 0.0 copy-start.7
  2.5 5.1 %collective-permute-start = (bf16[128,4096]{1,0:T(8,128)(2,1)S(1)}, bf16[128,4096]{1,0:T(8,128)(2,1)S(1)}, u32[]{:S(2)}, u32[]{:S(2)}) collective-permute-start(bf16[128,4096]{1,0:T(8,128)(2,1)S(1)} %fusion.refs_0_.refs_2_), channel_id=1, source_target_pairs={{1,0},{2,1},{3,2},{4,3},{5,4},{6,5},{7,6},{8,7},{9,8},{10,9},{11,1... | collective-permute-start | bytes 3145736 | tf_op jit(solution)/shard_map/ppermute | solution.py:356
  7.6 0.0 copy-done.9
  7.6 0.1 copy.16.rates_ref
  7.7 0.1 broadcast_in_dim.16
  7.8 1.3 broadcast_in_dim.17.refs_4_.refs_1_
  9.1 0.0 copy-start.10
  9.1 2.5 %shard_map.112 = f32[512,128]{1,0:T(8,128)} custom-call(bf16[128,4096]{1,0:T(8,128)(2,1)} %bitcast.24, f32[2048,128]{1,0:T(8,128)} %broadcast_in_dim.17.refs_4_.refs_1_), custom_call_target="tpu_custom_call" | custom-call | flops 3000000000 | bytes 2097152 | tf_op jit(solution)/shard_map/pallas_call | solution.py:334
  11.6 0.0 copy-done.7
  11.6 10.7 %all-to-all-start = ((f32[128,4,128]{2,1,0:T(4,128)}), f32[128,4,128]{2,1,0:T(4,128)S(1)}, u32[]{:S(2)}, u32[]{:S(2)}) async-start(f32[128,4,128]{2,1,0:T(4,128)} %bitcast.23), calls=%async_computation | async-start | bytes 524288 | tf_op jit(solution)/shard_map/all_to_all | solution.py:360
  22.3 0.1 reshape.39
  22.4 0.0 copy-done.10
  22.4 0.1 copy.21
  22.5 0.1 reshape.40
  22.6 0.6 shard_map.110
  23.2 0.0 copy-start.5
  23.2 0.7 pad_maximum_fusion
  24.0 0.0 collective-permute-done.refs_1_.refs_3_
  24.0 0.0 copy-start.11
  24.0 1.0 copy-done.11
  24.9 7.7 %shard_map.111 = (f32[128,4096]{1,0:T(8,128)}, f32[512,128]{1,0:T(8,128)}) custom-call(bf16[128,4096]{1,0:T(8,128)(2,1)} %copy-done.7, bf16[128,4096]{1,0:T(8,128)(2,1)} %copy-done.11, bf16[128,4096]{1,0:T(8,128)(2,1)} %bitcast.26, f32[128,128]{1,0:T(8,128)} %taps_ref, f32[2048,128]{1,0:T(8,128)} %broadcast_in_dim.17.refs_4_.refs_1_), custom_call_target="tpu_custom_call" | custom-call | flops 8000000000 | bytes 4259840 | tf_op jit(solution)/shard_map/pallas_call | solution.py:334
  32.6 2.9 %all-to-all-done.x_ref = f32[128,4,128]{2,1,0:T(4,128)S(1)} async-done(((f32[128,4,128]{2,1,0:T(4,128)}), f32[128,4,128]{2,1,0:T(4,128)S(1)}, u32[]{:S(2)}, u32[]{:S(2)}) %all-to-all-start) | async-done | bytes 262176 | tf_op jit(solution)/shard_map/all_to_all | solution.py:360
  35.6 0.0 copy-done.5
  35.6 0.0 copy-start.3
  35.6 0.9 copy-done.3
  36.5 1.0 shard_map.113.front_ref
  37.5 11.7 %all-to-all-start.1 = ((bf16[128,8,128]{2,1,0:T(8,128)(2,1)}), bf16[128,8,128]{2,1,0:T(8,128)(2,1)S(1)}, u32[]{:S(2)}, u32[]{:S(2)}) async-start(bf16[128,8,128]{2,1,0:T(8,128)(2,1)} %shard_map.113.front_ref), calls=%async_computation.1 | async-start | bytes 524288 | tf_op jit(solution)/shard_map/all_to_all | solution.py:360
  49.2 0.7 copy.18.rates_ref
  50.0 0.7 copy.19.weight_ref
  50.7 2.5 %shard_map.114 = (f32[128,128]{1,0:T(8,128)}, f32[128,128]{1,0:T(8,128)}, f32[128,128]{1,0:T(8,128)}) custom-call(f32[128,16]{1,0:T(8,128)} %copy.18.rates_ref, f32[128,16]{1,0:T(8,128)} %copy.19.weight_ref, f32[128,128]{1,0:T(8,128)} %taps_ref), custom_call_target="tpu_custom_call" | custom-call | flops 2000000000 | bytes 1048576 | tf_op jit(solution)/shard_map/pallas_call | solution.py:346
  53.2 9.2 %shard_map.115 = (f32[128,4096]{1,0:T(8,128)}, bf16[4096,128]{1,0:T(8,128)(2,1)}, bf16[4096,128]{1,0:T(8,128)(2,1)}, f32[128,128]{1,0:T(8,128)}) custom-call(bf16[128,4096]{1,0:T(8,128)(2,1)} %bitcast.25, bf16[128,4096]{1,0:T(8,128)(2,1)} %bitcast.27, f32[128,4096]{1,0:T(8,128)} %get-tuple-element.33.refs_2_.refs_0_.refs_1_, ...), custom_call_target="tpu_custom_call" | custom-call | flops 10000000000 | bytes 4292608 | tf_op jit(solution)/shard_map/pallas_call | solution.py:334
  62.3 0.1 all-to-all-done.1.x_ref
  62.5 0.0 copy-start.8
  62.5 0.7 copy-done.8
  63.2 6.1 %shard_map.116 = (bf16[128,4096]{1,0:T(8,128)(2,1)}, f32[128,128]{1,0:T(8,128)}) custom-call(f32[128,4096]{1,0:T(8,128)} %get-tuple-element.42.refs_0_, bf16[128,4096]{1,0:T(8,128)(2,1)} %bitcast.28, bf16[128,4096]{1,0:T(8,128)(2,1)} %copy-done.7, bf16[128,4096]{1,0:T(8,128)(2,1)} %copy-done.11, bf16[4096,128]{1,0:T(8,128)(2,1)} %get-tuple-element.43.refs_4_.refs_2_, ...), custom_call_target="tpu_custom_call" | custom-call | flops 6000000000 | bytes 6553600 | tf_op jit(solution)/shard_map/pallas_call | solution.py:334
  69.3 0.0 copy-start.2
  69.3 2.2 %shard_map.117 = (bf16[128,8,128]{2,1,0:T(8,128)(2,1)}, f32[4,128]{1,0:T(4,128)}) custom-call(bf16[128,8,128]{2,1,0:T(8,128)(2,1)} %copy-done.8, f32[4,128]{1,0:T(4,128)} %copy-done.5, bf16[128,8,128]{2,1,0:T(8,128)(2,1)} %shard_map.113.front_ref, f32[128,128]{1,0:T(8,128)} %get-tuple-element.44.tap_ref, f32[128,128]{1,0:T(8,128)} %get-tuple-element.45.cot_ref), custom_call_target="tpu_custom_call" | custom-call | flops 2000000000 | bytes 1048576 | tf_op jit(solution)/shard_map/pallas_call | solution.py:346
  71.5 11.6 %all-to-all-start.2 = ((bf16[128,8,128]{2,1,0:T(8,128)(2,1)}), bf16[128,8,128]{2,1,0:T(8,128)(2,1)S(1)}, u32[]{:S(2)}, u32[]{:S(2)}) async-start(bf16[128,8,128]{2,1,0:T(8,128)(2,1)} %get-tuple-element.46), calls=%async_computation.2 | async-start | bytes 524288 | tf_op jit(solution)/shard_map/all_to_all | solution.py:360
  83.1 0.0 copy-done.2
  83.1 0.0 copy-start.6
  83.1 3.5 %collective-permute-start.1 = (bf16[128,4096]{1,0:T(8,128)(2,1)S(1)}, bf16[128,4096]{1,0:T(8,128)(2,1)S(1)}, u32[]{:S(2)}, u32[]{:S(2)}) collective-permute-start(bf16[128,4096]{1,0:T(8,128)(2,1)S(1)} %copy-done.2), channel_id=1, source_target_pairs={{0,1},{1,2},{2,3},{3,4},{4,5},{5,6},{6,7},{7,8},{8,9},{9,10},{10,1... | collective-permute-start | bytes 3145736 | tf_op jit(solution)/shard_map/ppermute | solution.py:356
  86.7 3.6 %shard_map.119 = bf16[128,4096]{1,0:T(8,128)(2,1)} custom-call(f32[128,4096]{1,0:T(8,128)} %get-tuple-element.42.refs_0_, f32[128,4096]{1,0:T(8,128)} %get-tuple-element.33.refs_2_.refs_0_.refs_1_, bf16[4096,128]{1,0:T(8,128)(2,1)} %get-tuple-element.43.refs_4_.refs_2_, bf16[1024,128]{1,0:T(8,128)(2,1)} %bitcast.22), custom_call_target="tpu_custom_call" | custom-call | flops 4000000000 | bytes 5505024 | tf_op jit(solution)/shard_map/pallas_call | solution.py:334
  90.3 17.0 %all-to-all-done.2.x_ref = bf16[128,8,128]{2,1,0:T(8,128)(2,1)S(1)} async-done(((bf16[128,8,128]{2,1,0:T(8,128)(2,1)}), bf16[128,8,128]{2,1,0:T(8,128)(2,1)S(1)}, u32[]{:S(2)}, u32[]{:S(2)}) %all-to-all-start.2) | async-done | bytes 262176 | tf_op jit(solution)/shard_map/all_to_all | solution.py:360
  107.3 0.0 copy-start.1
  107.3 0.0 copy-done.6
  107.3 1.3 shard_map.120
  108.6 0.0 copy-done.1
  108.6 8.1 %all-to-all-start.3 = ((f32[256,2,128]{2,1,0:T(2,128)}), f32[256,2,128]{2,1,0:T(2,128)S(1)}, u32[]{:S(2)}, u32[]{:S(2)}) async-start(f32[256,2,128]{2,1,0:T(2,128)} %shard_map.120), calls=%async_computation.3 | async-start | bytes 524288 | tf_op jit(solution)/shard_map/all_to_all | solution.py:360
  116.7 0.0 copy-start
  116.7 0.0 copy-start.4
  116.7 6.7 %shard_map.118 = bf16[128,4096]{1,0:T(8,128)(2,1)} custom-call(f32[128,4096]{1,0:T(8,128)} %get-tuple-element.33.refs_2_.refs_0_.refs_1_, bf16[128,4096]{1,0:T(8,128)(2,1)} %bitcast.29, f32[128,128]{1,0:T(8,128)} %get-tuple-element.39.refs_2_, bf16[4096,128]{1,0:T(8,128)(2,1)} %get-tuple-element.41.refs_3_, bf16[1024,128]{1,0:T(8,128)(2,1)} %bitcast.19), custom_call_target="tpu_custom_call" | custom-call | flops 7000000000 | bytes 4521984 | tf_op jit(solution)/shard_map/pallas_call | solution.py:334
  123.4 0.0 collective-permute-done.1.refs_1_
  123.4 0.0 copy-done
  123.4 0.0 copy-done.4
  123.4 5.9 %shard_map.121 = bf16[128,4096]{1,0:T(8,128)(2,1)} custom-call(bf16[128,4096]{1,0:T(8,128)(2,1)S(1)} %copy-done.2, bf16[128,4096]{1,0:T(8,128)(2,1)S(1)} %collective-permute-done.1.refs_1_, f32[128,128]{1,0:T(8,128)S(1)} %copy-done.4, bf16[128,4096]{1,0:T(8,128)(2,1)S(1)} %bitcast.18), custom_call_target="tpu_custom_call" | custom-call | flops 7000000000 | bytes 3211264 | tf_op jit(solution)/shard_map/pallas_call | solution.py:334
  129.3 2.6 %all-to-all-done.3.x_ref = f32[256,2,128]{2,1,0:T(2,128)S(1)} async-done(((f32[256,2,128]{2,1,0:T(2,128)}), f32[256,2,128]{2,1,0:T(2,128)S(1)}, u32[]{:S(2)}, u32[]{:S(2)}) %all-to-all-start.3) | async-done | bytes 262176 | tf_op jit(solution)/shard_map/all_to_all | solution.py:360
  131.9 0.9 shard_map.122
  (1 shorter events, 0.0 us)
Async XLA Ops:
  0.6 7.0 %copy-start.9 = (f32[128,16]{0,1:T(8,128)S(1)}, f32[128,16]{0,1:T(8,128)}, u32[]{:S(2)}) copy-start(f32[128,16]{0,1:T(8,128)} %param.12) | copy-start | bytes 24580
  2.4 9.2 %copy-start.7 = (bf16[128,4096]{1,0:T(8,128)(2,1)}, bf16[128,4096]{1,0:T(8,128)(2,1)S(1)}, u32[]{:S(2)}) copy-start(bf16[128,4096]{1,0:T(8,128)(2,1)S(1)} %fusion.refs_0_.refs_2_) | copy-start | bytes 3145732
  2.5 21.5 %collective-permute-start = (bf16[128,4096]{1,0:T(8,128)(2,1)S(1)}, bf16[128,4096]{1,0:T(8,128)(2,1)S(1)}, u32[]{:S(2)}, u32[]{:S(2)}) collective-permute-start(bf16[128,4096]{1,0:T(8,128)(2,1)S(1)} %fusion.refs_0_.refs_2_), channel_id=1, source_target_pairs={{1,0},{2,1},{3,2},{4,3},{5,4},{6,5},{7,6},{8,7},{9,8},{10,9},{11,1... | collective-permute-start | bytes 3145736 | tf_op jit(solution)/shard_map/ppermute | solution.py:356
  9.1 13.3 %copy-start.10 = (f32[128,16]{0,1:T(8,128)S(1)}, f32[128,16]{0,1:T(8,128)}, u32[]{:S(2)}) copy-start(f32[128,16]{0,1:T(8,128)} %param.11) | copy-start | bytes 24580
  11.6 23.9 %all-to-all-start = ((f32[128,4,128]{2,1,0:T(4,128)}), f32[128,4,128]{2,1,0:T(4,128)S(1)}, u32[]{:S(2)}, u32[]{:S(2)}) async-start(f32[128,4,128]{2,1,0:T(4,128)} %bitcast.23), calls=%async_computation | async-start | bytes 524288 | tf_op jit(solution)/shard_map/all_to_all | solution.py:360
  23.2 12.3 %copy-start.5 = (f32[4,128]{1,0:T(4,128)}, f32[4,128]{1,0:T(4,128)S(1)}, u32[]{:S(2)}) copy-start(f32[4,128]{1,0:T(4,128)S(1)} %get-tuple-element.34.decay_ref) | copy-start | bytes 6148
  24.0 1.0 copy-start.11
  35.6 1.0 copy-start.3
  37.5 25.0 %all-to-all-start.1 = ((bf16[128,8,128]{2,1,0:T(8,128)(2,1)}), bf16[128,8,128]{2,1,0:T(8,128)(2,1)S(1)}, u32[]{:S(2)}, u32[]{:S(2)}) async-start(bf16[128,8,128]{2,1,0:T(8,128)(2,1)} %shard_map.113.front_ref), calls=%async_computation.1 | async-start | bytes 524288 | tf_op jit(solution)/shard_map/all_to_all | solution.py:360
  62.5 0.7 copy-start.8
  69.3 13.8 %copy-start.2 = (bf16[128,4096]{1,0:T(8,128)(2,1)S(1)}, bf16[128,4096]{1,0:T(8,128)(2,1)}, u32[]{:S(2)}) copy-start(bf16[128,4096]{1,0:T(8,128)(2,1)} %get-tuple-element.49.refs_0_) | copy-start | bytes 3145732
  71.5 35.8 %all-to-all-start.2 = ((bf16[128,8,128]{2,1,0:T(8,128)(2,1)}), bf16[128,8,128]{2,1,0:T(8,128)(2,1)S(1)}, u32[]{:S(2)}, u32[]{:S(2)}) async-start(bf16[128,8,128]{2,1,0:T(8,128)(2,1)} %get-tuple-element.46), calls=%async_computation.2 | async-start | bytes 524288 | tf_op jit(solution)/shard_map/all_to_all | solution.py:360
  83.1 24.2 %copy-start.6 = (f32[4,128]{1,0:T(4,128)S(1)}, f32[4,128]{1,0:T(4,128)}, u32[]{:S(2)}) copy-start(f32[4,128]{1,0:T(4,128)} %get-tuple-element.47.sum_ref) | copy-start | bytes 6148
  83.1 40.3 %collective-permute-start.1 = (bf16[128,4096]{1,0:T(8,128)(2,1)S(1)}, bf16[128,4096]{1,0:T(8,128)(2,1)S(1)}, u32[]{:S(2)}, u32[]{:S(2)}) collective-permute-start(bf16[128,4096]{1,0:T(8,128)(2,1)S(1)} %copy-done.2), channel_id=1, source_target_pairs={{0,1},{1,2},{2,3},{3,4},{4,5},{5,6},{6,7},{7,8},{8,9},{9,10},{10,1... | collective-permute-start | bytes 3145736 | tf_op jit(solution)/shard_map/ppermute | solution.py:356
  107.3 1.3 copy-start.1
  108.6 23.3 %all-to-all-start.3 = ((f32[256,2,128]{2,1,0:T(2,128)}), f32[256,2,128]{2,1,0:T(2,128)S(1)}, u32[]{:S(2)}, u32[]{:S(2)}) async-start(f32[256,2,128]{2,1,0:T(2,128)} %shard_map.120), calls=%async_computation.3 | async-start | bytes 524288 | tf_op jit(solution)/shard_map/all_to_all | solution.py:360
  116.7 6.7 %copy-start = (bf16[1,128,4096]{2,1,0:T(8,128)(2,1)S(1)}, bf16[1,128,4096]{2,1,0:T(8,128)(2,1)}, u32[]{:S(2)}) copy-start(bf16[1,128,4096]{2,1,0:T(8,128)(2,1)} %param.10) | copy-start | bytes 3145732
  116.7 6.7 %copy-start.4 = (f32[128,128]{1,0:T(8,128)S(1)}, f32[128,128]{1,0:T(8,128)}, u32[]{:S(2)}) copy-start(f32[128,128]{1,0:T(8,128)} %get-tuple-element.50.refs_2_) | copy-start | bytes 196612

commit v6 on v5

--- a/solution.py
+++ b/solution.py
@@ -80,6 +80,11 @@
     for bit in (4, 2, 1):
         rows = jnp.where((sub & bit) != 0, roll_left(rows, bit), rows)
     return jnp.sum(rows.reshape(-1, 8, LANES), axis=1)
+
+
+def carry_table(rate_ref, weight_ref, i, steps):
+    high, low = split(weight_ref[i : i + 1, :] * jnp.exp(-rate_ref[i : i + 1, :] * steps))
+    return jnp.where(iota(steps.shape, 1) < LANES // 2, high, low)
 
 
 def carried_part(table, ref, i, modes, size):
@@ -113,7 +118,7 @@
         mode_sums(jnp.exp(-rate_ref[i * rows : (i + 1) * rows, :] * steps), x_ref[:, lanes], size, modes)
         for i, lanes in enumerate(tiles_of(x_ref))
     ]
-    out_ref[...] = jnp.concatenate(out, axis=0)
+    out_ref[...] = jnp.concatenate(out, axis=0).astype(out_ref.dtype)
 
 
 def mixer_back_kernel(size, modes, own_ref, next_ref, gate_ref, taps_ref, rate_ref, gm_ref, out_ref):
@@ -137,8 +142,7 @@
 
 
 def local_kernel(
-    size, x_ref, gate_ref, gm_ref, filt_ref, rate_ref, weight_ref,
-    out_ref, front_ref, back_ref, lag_ref,
+    size, x_ref, gate_ref, gm_ref, filt_ref, rate_ref, weight_ref, out_ref, table_ref, lag_ref
 ):
     per = LANES // size
     row, col = iota((LANES, LANES), 0), iota((LANES, LANES), 1)
@@ -150,10 +154,7 @@
         prod = dot(toeplitz(filt_ref, i, per, [col <= row]), jnp.concatenate([x, x], axis=0))
         out_ref[:, lanes] = pick_groups(prod, LANES, size)
     for i in range(len(tiles)):
-        rate, weight = rate_ref[i : i + 1, :], weight_ref[i : i + 1, :]
-        for ref, steps in ((front_ref, up + 1.0), (back_ref, LANES - 1.0 - up)):
-            high, low = split(weight * jnp.exp(-rate * steps))
-            ref[i * LANES : (i + 1) * LANES, :] = jnp.where(col < LANES // 2, high, low)
+        table_ref[i * LANES : (i + 1) * LANES, :] = carry_table(rate_ref, weight_ref, i, up + 1.0)
     for i, lanes in enumerate(tiles):
         cot = (gm_ref[:, lanes] * gate_ref[:, lanes].astype(F32)).astype(BF16)
         pairs = dot(spread_groups(x_ref[:, lanes], size), cot, NT)
@@ -190,7 +191,9 @@
         out_ref[:, lanes] = (gm_ref[:, lanes] * full).astype(BF16)
 
 
-def input_grad_kernel(size, modes, gm_ref, gate_ref, filt_ref, table_ref, enter_ref, out_ref):
+def input_grad_kernel(
+    size, modes, gm_ref, gate_ref, filt_ref, rate_ref, weight_ref, enter_ref, out_ref
+):
     per = LANES // size
     row, col = iota((LANES, LANES), 0), iota((LANES, LANES), 1)
     for i, lanes in enumerate(tiles_of(gm_ref)):
@@ -199,7 +202,7 @@
         prod = dot(
             jnp.concatenate([left, left[:, :LANES]], axis=1), jnp.concatenate([high, high, low], axis=0)
         )
-        table = table_ref[i * LANES : (i + 1) * LANES, :]
+        table = carry_table(rate_ref, weight_ref, i, LANES - 1.0 - row.astype(F32))
         carried = carried_part(table, enter_ref, i, modes, size)
         out_ref[:, lanes] = (pick_groups(prod, LANES, size) + carried).astype(BF16)
 
@@ -222,12 +225,12 @@
 
 
 def filters_kernel(rates_ref, weight_ref, taps_ref, filt_ref, filt_back_ref, taps_back_ref):
-    rates, taps = rates_ref[...], taps_ref[...]
+    rates, weight, taps = rates_ref[...].T, weight_ref[...].T, taps_ref[...]
     groups, modes = rates.shape
     lag = iota((groups, LANES), 1).astype(F32)
     filt = jnp.zeros((groups, LANES), F32)
     for m in range(modes):
-        filt = filt + weight_ref[:, m : m + 1] * jnp.exp(-rates[:, m : m + 1] * lag)
+        filt = filt + weight[:, m : m + 1] * jnp.exp(-rates[:, m : m + 1] * lag)
     mirror = ((iota((LANES, LANES), 0) + iota((LANES, LANES), 1)) % LANES == 0).astype(F32)
     filt_ref[...] = filt
     filt_back_ref[...] = exact_dot(filt, mirror)
@@ -252,7 +255,7 @@
     state = jnp.zeros_like(decay)
     for d in range(x_ref.shape[0]):
         out_ref[d] = jnp.concatenate([state, beside_ref[d]], axis=0).astype(BF16)
-        state = decay * state + x_ref[d]
+        state = decay * state + x_ref[d].astype(F32)
 
 
 def back_scan_kernel(x_ref, decay_ref, front_ref, tap_ref, cot_ref, out_ref, sum_ref):
@@ -397,7 +400,7 @@
     )(me.astype(jnp.int32).reshape(1, 1), rates)
     bind = functools.partial
     states = call(
-        bind(states_kernel, size, modes), width, step, chunk, [None, table_rows], [(state_rows, F32)],
+        bind(states_kernel, size, modes), width, step, chunk, [None, table_rows], [(state_rows, BF16)],
         [seq, rate_rows], 3,
     )[0]
     ends = exchange(states.reshape(count, own_rows, LANES))
@@ -413,12 +416,12 @@
         [ends, decay, back_states.reshape(count, own_rows, LANES)],
     )[0]
     second = exchange(first)
-    late = lax.optimization_barrier((rates, weight, taps, first))[:3]
+    late = lax.optimization_barrier((rates.T, weight.T, taps, first))[:3]
     filt, filt_back, taps_back = whole(filters_kernel, [(taps.shape, F32)] * 3, late, 60)
-    local, front_table, back_table, lag_cot = call(
+    local, front_table, lag_cot = call(
         bind(local_kernel, size), width, step, chunk,
         [None, None, None, group_rows, tile_rows, tile_rows],
-        [(None, F32), (carry_rows, BF16), (carry_rows, BF16), (group_rows, F32)],
+        [(None, F32), (carry_rows, BF16), (group_rows, F32)],
         [seq, gate, grad_mixer, filt_back, rate_row, weight_row], 10,
     )
     mixer_in, lag_taps = call(
@@ -432,25 +435,26 @@
         [second, decay, first, lag_taps, lag_cot], 60,
     )
     third = exchange(message)
+    grad_gate_mr = call(
+        bind(mixer_kernel, size), width, step, chunk, [None, None, group_rows, None], [(None, BF16)],
+        [mixer_in, before, taps_back, cot], 7, 32,
+    )[0]
+    third, grad_gate_mr = lax.optimization_barrier((third, grad_gate_mr))
+    spread = whole(
+        bind(collect_kernel, size), [((reps * count, 2, LANES), F32)], [third, state_sums, lam_own]
+    )[0]
+    got = exchange(spread, ("rep", "ctx"))
+    local = lax.optimization_barrier((local, spread))[0]
     grad_gate_li = call(
         bind(gate_grad_kernel, size, modes), width, step, chunk,
         [None, None, carry_rows, 2 * state_rows], [(None, BF16)],
         [local, grad_mixer, front_table, second.reshape(-1, LANES)], 4,
     )[0]
-    grad_gate_mr = call(
-        bind(mixer_kernel, size), width, step, chunk, [None, None, group_rows, None], [(None, BF16)],
-        [mixer_in, before, taps_back, cot], 7, 32,
-    )[0]
-    spread = whole(
-        bind(collect_kernel, size), [((reps * count, 2, LANES), F32)], [third, state_sums, lam_own]
-    )[0]
-    got = exchange(spread, ("rep", "ctx"))
     grad_inputs = call(
         bind(input_grad_kernel, size, modes), width, step, chunk,
-        [None, None, group_rows, carry_rows, 2 * state_rows], [(None, BF16)],
-        [grad_mixer, gate, filt, back_table, third.reshape(-1, LANES)], 7,
-    )[0]
-    got, grad_gate_mr = lax.optimization_barrier((got, grad_gate_mr))
+        [None, None, group_rows, tile_rows, tile_rows, 2 * state_rows], [(None, BF16)],
+        [grad_mixer, gate, filt, rate_row, weight_row, third.reshape(-1, LANES)], 7,
+    )[0]
     grad_residues, grad_taps = whole(
         bind(finish_kernel, 1.0 / math.sqrt(reps * count * LANES), per, own_rows),
         [((modes, groups), F32), (taps.shape, F32)], [got, norm.T],

time: 133 us -> 122 us (0.917)
  waiting for transfers between devices: 22.7 us -> 15.1 us
  local copies, waits for them, and re-layouts: 5.89 us -> 4.43 us
  starting transfers between devices: 50.9 us -> 49.5 us
    all_to_all x4, waiting for transfers between devices: 22.6 us -> 15 us  [exchange(): return lax.all_to_all(x, axes, split_axis=0, concat_axis=0, tiled=True)]
    optimization_barrier x2 -> x0, local copies, waits for them, and re-layouts: 1.46 us -> none  [on_device(): late = lax.optimization_barrier((rates, weight, taps, first))[:3]]
    unnamed x25 -> x27, local copies, waits for them, and re-layouts: 2.78 us -> 2.78 us
  transfers between devices with their start and end apart: 6 -> 6, of which waited for: 4 -> 5; matrix products, arithmetic and copies ran while one was open for 3% -> 2% of each run, Pallas kernels for 30% -> 33%
where the time goes in v6:
time: 122 us
  starting transfers between devices  49.5 us (41%)
  Pallas kernels  49.3 us (40%)
  waiting for transfers between devices  15.1 us (12%)
  local copies, waits for them, and re-layouts  4.43 us (4%)
  other arithmetic  2.51 us (2%)
    all_to_all x4, starting transfers between devices, exchange(): return lax.all_to_all(x, axes, split_axis=0, concat_axis=0, tiled=True)  41.8 us
    pallas_call x7, Pallas kernels, call(): pl.pallas_call(kernel, grid=(width // step,), in_specs=[block(rows) for r...  40.7 us
    all_to_all x4, waiting for transfers between devices, exchange(): return lax.all_to_all(x, axes, split_axis=0, concat_axis=0, tiled=True)  15 us
    pallas_call x5, Pallas kernels, whole(): pl.pallas_call(body, out_shape=[jax.ShapeDtypeStruct(shape, kind) for sha...  7.93 us
    ppermute x2, starting transfers between devices, shifted(): lax.ppermute(x, 'ctx', [(i, i + by) for i in range(count) if 0 <= i + by...  7.76 us
    unnamed x27, local copies, waits for them, and re-layouts  2.78 us
  transfers between devices with their start and end apart: 6, of which 5 were waited for; matrix products, arithmetic and copies ran while one was open for 2% of the time, Pallas kernels for 33%

profile of v6, /device:TPU:1, one launch (start us, length us, event | category | flops | bytes accessed | tf_op | source)
XLA Modules:
  0.0 121.6 jit_solution(14377031577465257833)
XLA Ops:
  0.6 0.0 copy-start.9
  0.6 1.8 %fusion.refs_0_.refs_2_ = bf16[128,4096]{1,0:T(8,128)(2,1)S(1)} fusion(bf16[1,128,4096]{2,1,0:T(8,128)(2,1)} %param.9, bf16[1,128,4096]{2,1,0:T(8,128)(2,1)} %param.10), kind=kLoop, calls=%fused_computation.1 | loop fusion | flops 2097152 | bytes 3145728 | tf_op jit(solution)/shard_map/convert_element_type | solution.py:382
  2.4 0.0 copy-start.7
  2.5 5.1 %collective-permute-start = (bf16[128,4096]{1,0:T(8,128)(2,1)S(1)}, bf16[128,4096]{1,0:T(8,128)(2,1)S(1)}, u32[]{:S(2)}, u32[]{:S(2)}) collective-permute-start(bf16[128,4096]{1,0:T(8,128)(2,1)S(1)} %fusion.refs_0_.refs_2_), channel_id=1, source_target_pairs={{1,0},{2,1},{3,2},{4,3},{5,4},{6,5},{7,6},{8,7},{9,8},{10,9},{11,1... | collective-permute-start | bytes 3145736 | tf_op jit(solution)/shard_map/ppermute | solution.py:359
  7.6 0.0 copy-done.9
  7.6 0.1 copy.14.rates_ref
  7.7 0.1 broadcast_in_dim.16
  7.8 1.3 %broadcast_in_dim.17.refs_4_.refs_1_ = f32[2048,128]{1,0:T(8,128)} broadcast(f32[2048]{0:T(1024)S(1)} %broadcast_in_dim.16), dimensions={0} | broadcast | bytes 1056768 | tf_op jit(solution)/shard_map/broadcast_in_dim | solution.py:387
  9.1 0.0 copy-start.11
  9.1 2.4 %shard_map.112 = bf16[512,128]{1,0:T(8,128)(2,1)} custom-call(bf16[128,4096]{1,0:T(8,128)(2,1)} %bitcast.28, f32[2048,128]{1,0:T(8,128)} %broadcast_in_dim.17.refs_4_.refs_1_), custom_call_target="tpu_custom_call" | custom-call | flops 3000000000 | bytes 2097152 | tf_op jit(solution)/shard_map/pallas_call | solution.py:337
  11.6 0.0 copy-done.7
  11.6 10.7 %all-to-all-start = ((bf16[128,4,128]{2,1,0:T(4,128)(2,1)}), bf16[128,4,128]{2,1,0:T(4,128)(2,1)S(1)}, u32[]{:S(2)}, u32[]{:S(2)}) async-start(bf16[128,4,128]{2,1,0:T(4,128)(2,1)} %bitcast.25), calls=%async_computation | async-start | bytes 262144 | tf_op jit(solution)/shard_map/all_to_all | solution.py:363
  22.3 0.1 reshape.39
  22.4 0.0 copy-done.11
  22.4 0.0 copy-start.10
  22.4 0.1 copy.17
  22.5 0.1 reshape.40
  22.6 0.6 shard_map.110
  23.2 0.0 copy-start.5
  23.2 0.7 pad_maximum_fusion
  23.9 0.0 collective-permute-done.refs_1_.refs_3_
  23.9 0.0 copy-start.12
  23.9 1.0 copy-done.12
  24.9 7.7 %shard_map.111 = (f32[128,4096]{1,0:T(8,128)}, f32[512,128]{1,0:T(8,128)}) custom-call(bf16[128,4096]{1,0:T(8,128)(2,1)} %copy-done.7, bf16[128,4096]{1,0:T(8,128)(2,1)} %copy-done.12, bf16[128,4096]{1,0:T(8,128)(2,1)} %bitcast.30, f32[128,128]{1,0:T(8,128)} %taps_ref, f32[2048,128]{1,0:T(8,128)} %broadcast_in_dim.17.refs_4_.refs_1_), custom_call_target="tpu_custom_call" | custom-call | flops 8000000000 | bytes 4259840 | tf_op jit(solution)/shard_map/pallas_call | solution.py:337
  32.6 0.0 copy-done.10
  32.6 0.5 all-to-all-done.x_ref
  33.0 0.0 copy-done.5
  33.0 0.0 copy-start.3
  33.0 0.9 copy-done.3
  34.0 1.0 shard_map.113.front_ref
  35.0 13.5 %all-to-all-start.1 = ((bf16[128,8,128]{2,1,0:T(8,128)(2,1)}), bf16[128,8,128]{2,1,0:T(8,128)(2,1)S(1)}, u32[]{:S(2)}, u32[]{:S(2)}) async-start(bf16[128,8,128]{2,1,0:T(8,128)(2,1)} %shard_map.113.front_ref), calls=%async_computation.1 | async-start | bytes 524288 | tf_op jit(solution)/shard_map/all_to_all | solution.py:363
  48.4 2.5 %shard_map.114 = (f32[128,128]{1,0:T(8,128)}, f32[128,128]{1,0:T(8,128)}, f32[128,128]{1,0:T(8,128)}) custom-call(f32[16,128]{1,0:T(8,128)} %bitcast.26, f32[16,128]{1,0:T(8,128)} %bitcast.27, f32[128,128]{1,0:T(8,128)} %taps_ref), custom_call_target="tpu_custom_call" | custom-call | flops 2000000000 | bytes 1048576 | tf_op jit(solution)/shard_map/pallas_call | solution.py:349
  51.0 8.5 %shard_map.115 = (f32[128,4096]{1,0:T(8,128)}, bf16[4096,128]{1,0:T(8,128)(2,1)}, f32[128,128]{1,0:T(8,128)}) custom-call(bf16[128,4096]{1,0:T(8,128)(2,1)} %bitcast.29, bf16[128,4096]{1,0:T(8,128)(2,1)} %bitcast.31, f32[128,4096]{1,0:T(8,128)} %get-tuple-element.33.refs_2_.refs_0_.refs_1_, f32[128,128]{1,0:T(8,128)} %get-tuple-element.40.refs_3_, ...), custom_call_target="tpu_custom_call" | custom-call | flops 10000000000 | bytes 4292608 | tf_op jit(solution)/shard_map/pallas_call | solution.py:337
  59.5 2.2 %all-to-all-done.1.x_ref = bf16[128,8,128]{2,1,0:T(8,128)(2,1)S(1)} async-done(((bf16[128,8,128]{2,1,0:T(8,128)(2,1)}), bf16[128,8,128]{2,1,0:T(8,128)(2,1)S(1)}, u32[]{:S(2)}, u32[]{:S(2)}) %all-to-all-start.1) | async-done | bytes 262176 | tf_op jit(solution)/shard_map/all_to_all | solution.py:363
  61.7 0.0 copy-start.8
  61.7 0.7 copy-done.8
  62.4 6.1 %shard_map.116 = (bf16[128,4096]{1,0:T(8,128)(2,1)}, f32[128,128]{1,0:T(8,128)}) custom-call(f32[128,4096]{1,0:T(8,128)} %get-tuple-element.51.refs_0_, bf16[128,4096]{1,0:T(8,128)(2,1)} %bitcast.32, bf16[128,4096]{1,0:T(8,128)(2,1)} %copy-done.7, bf16[128,4096]{1,0:T(8,128)(2,1)} %copy-done.12, bf16[4096,128]{1,0:T(8,128)(2,1)} %get-tuple-element.42.refs_4_.refs_2_, ...), custom_call_target="tpu_custom_call" | custom-call | flops 6000000000 | bytes 6553600 | tf_op jit(solution)/shard_map/pallas_call | solution.py:337
  68.5 2.6 %collective-permute-start.1 = (bf16[128,4096]{1,0:T(8,128)(2,1)}, bf16[128,4096]{1,0:T(8,128)(2,1)S(1)}, u32[]{:S(2)}, u32[]{:S(2)}) collective-permute-start(bf16[128,4096]{1,0:T(8,128)(2,1)} %get-tuple-element.46.refs_0_), channel_id=1, source_target_pairs={{0,1},{1,2},{2,3},{3,4},{4,5},{5,6},{6,7},{7,8},{8,9},{9,10},{10,1... | collective-permute-start | bytes 3145736 | tf_op jit(solution)/shard_map/ppermute | solution.py:359
  71.1 0.0 copy-start
  71.1 0.0 copy-start.2
  71.1 0.0 copy-start.4
  71.1 2.2 %shard_map.117 = (bf16[128,8,128]{2,1,0:T(8,128)(2,1)}, f32[4,128]{1,0:T(4,128)}) custom-call(bf16[128,8,128]{2,1,0:T(8,128)(2,1)} %copy-done.8, f32[4,128]{1,0:T(4,128)} %copy-done.5, bf16[128,8,128]{2,1,0:T(8,128)(2,1)} %shard_map.113.front_ref, f32[128,128]{1,0:T(8,128)} %get-tuple-element.43.tap_ref, f32[128,128]{1,0:T(8,128)} %get-tuple-element.44.cot_ref), custom_call_target="tpu_custom_call" | custom-call | flops 2000000000 | bytes 1048576 | tf_op jit(solution)/shard_map/pallas_call | solution.py:349
  73.3 9.7 %all-to-all-start.2 = ((bf16[128,8,128]{2,1,0:T(8,128)(2,1)}), bf16[128,8,128]{2,1,0:T(8,128)(2,1)S(1)}, u32[]{:S(2)}, u32[]{:S(2)}) async-start(bf16[128,8,128]{2,1,0:T(8,128)(2,1)} %get-tuple-element.45), calls=%async_computation.2 | async-start | bytes 524288 | tf_op jit(solution)/shard_map/all_to_all | solution.py:363
  83.0 0.1 collective-permute-done.1.refs_1_
  83.1 0.0 copy-done
  83.1 0.0 copy-done.2
  83.1 0.0 copy-done.4
  83.1 0.0 copy-start.6
  83.1 5.9 %shard_map.118 = bf16[128,4096]{1,0:T(8,128)(2,1)} custom-call(bf16[128,4096]{1,0:T(8,128)(2,1)S(1)} %copy-done.2, bf16[128,4096]{1,0:T(8,128)(2,1)S(1)} %collective-permute-done.1.refs_1_, f32[128,128]{1,0:T(8,128)S(1)} %copy-done.4, bf16[128,4096]{1,0:T(8,128)(2,1)S(1)} %bitcast.20), custom_call_target="tpu_custom_call" | custom-call | flops 7000000000 | bytes 3211264 | tf_op jit(solution)/shard_map/pallas_call | solution.py:337
  89.0 7.2 %all-to-all-done.2.x_ref = bf16[128,8,128]{2,1,0:T(8,128)(2,1)S(1)} async-done(((bf16[128,8,128]{2,1,0:T(8,128)(2,1)}), bf16[128,8,128]{2,1,0:T(8,128)(2,1)S(1)}, u32[]{:S(2)}, u32[]{:S(2)}) %all-to-all-start.2) | async-done | bytes 262176 | tf_op jit(solution)/shard_map/all_to_all | solution.py:363
  96.3 0.0 copy-start.1
  96.3 0.0 copy-done.6
  96.3 1.3 %shard_map.120 = f32[256,2,128]{2,1,0:T(2,128)} custom-call(bf16[128,8,128]{2,1,0:T(8,128)(2,1)S(1)} %all-to-all-done.2.x_ref, f32[4,128]{1,0:T(4,128)S(1)} %copy-done.6, f32[16,128]{1,0:T(8,128)S(1)} %get-tuple-element.50.lam_ref), custom_call_target="tpu_custom_call" | custom-call | flops 2000000000 | bytes 1048576 | tf_op jit(solution)/shard_map/pallas_call | solution.py:349
  97.6 0.0 copy-done.1
  97.6 7.9 %all-to-all-start.3 = ((f32[256,2,128]{2,1,0:T(2,128)}), f32[256,2,128]{2,1,0:T(2,128)S(1)}, u32[]{:S(2)}, u32[]{:S(2)}) async-start(f32[256,2,128]{2,1,0:T(2,128)} %shard_map.120), calls=%async_computation.3 | async-start | bytes 524288 | tf_op jit(solution)/shard_map/all_to_all | solution.py:363
  105.5 3.6 %shard_map.121 = bf16[128,4096]{1,0:T(8,128)(2,1)} custom-call(f32[128,4096]{1,0:T(8,128)} %get-tuple-element.51.refs_0_, f32[128,4096]{1,0:T(8,128)} %get-tuple-element.33.refs_2_.refs_0_.refs_1_, bf16[4096,128]{1,0:T(8,128)(2,1)} %get-tuple-element.42.refs_4_.refs_2_, bf16[1024,128]{1,0:T(8,128)(2,1)} %bitcast.24), custom_call_target="tpu_custom_call" | custom-call | flops 4000000000 | bytes 5505024 | tf_op jit(solution)/shard_map/pallas_call | solution.py:337
  109.1 6.5 %shard_map.119 = bf16[128,4096]{1,0:T(8,128)(2,1)} custom-call(f32[128,4096]{1,0:T(8,128)} %get-tuple-element.33.refs_2_.refs_0_.refs_1_, bf16[128,4096]{1,0:T(8,128)(2,1)} %bitcast.33, f32[128,128]{1,0:T(8,128)} %get-tuple-element.39.refs_2_, f32[32,128]{1,0:T(8,128)} %get-tuple-element.57.refs_4_.refs_3_, f32[32,128]{1,0:T(8,128)} %get-tuple-element.58.refs_5_.refs_4_, ...), custom_call_target="tpu_custom_call" | custom-call | flops 7000000000 | bytes 3506176 | tf_op jit(solution)/shard_map/pallas_call | solution.py:337
  115.6 5.1 %all-to-all-done.3.x_ref = f32[256,2,128]{2,1,0:T(2,128)S(1)} async-done(((f32[256,2,128]{2,1,0:T(2,128)}), f32[256,2,128]{2,1,0:T(2,128)S(1)}, u32[]{:S(2)}, u32[]{:S(2)}) %all-to-all-start.3) | async-done | bytes 262176 | tf_op jit(solution)/shard_map/all_to_all | solution.py:363
  120.7 0.9 shard_map.122
  (1 shorter events, 0.0 us)
Async XLA Ops:
  0.6 7.0 %copy-start.9 = (f32[128,16]{0,1:T(8,128)S(1)}, f32[128,16]{0,1:T(8,128)}, u32[]{:S(2)}) copy-start(f32[128,16]{0,1:T(8,128)} %param.12) | copy-start | bytes 24580
  2.4 9.1 %copy-start.7 = (bf16[128,4096]{1,0:T(8,128)(2,1)}, bf16[128,4096]{1,0:T(8,128)(2,1)S(1)}, u32[]{:S(2)}) copy-start(bf16[128,4096]{1,0:T(8,128)(2,1)S(1)} %fusion.refs_0_.refs_2_) | copy-start | bytes 3145732
  2.5 21.5 %collective-permute-start = (bf16[128,4096]{1,0:T(8,128)(2,1)S(1)}, bf16[128,4096]{1,0:T(8,128)(2,1)S(1)}, u32[]{:S(2)}, u32[]{:S(2)}) collective-permute-start(bf16[128,4096]{1,0:T(8,128)(2,1)S(1)} %fusion.refs_0_.refs_2_), channel_id=1, source_target_pairs={{1,0},{2,1},{3,2},{4,3},{5,4},{6,5},{7,6},{8,7},{9,8},{10,9},{11,1... | collective-permute-start | bytes 3145736 | tf_op jit(solution)/shard_map/ppermute | solution.py:359
  9.1 13.2 %copy-start.11 = (f32[128,16]{0,1:T(8,128)S(1)}, f32[128,16]{0,1:T(8,128)}, u32[]{:S(2)}) copy-start(f32[128,16]{0,1:T(8,128)} %param.11) | copy-start | bytes 24580
  11.6 21.5 %all-to-all-start = ((bf16[128,4,128]{2,1,0:T(4,128)(2,1)}), bf16[128,4,128]{2,1,0:T(4,128)(2,1)S(1)}, u32[]{:S(2)}, u32[]{:S(2)}) async-start(bf16[128,4,128]{2,1,0:T(4,128)(2,1)} %bitcast.25), calls=%async_computation | async-start | bytes 262144 | tf_op jit(solution)/shard_map/all_to_all | solution.py:363
  22.4 10.2 %copy-start.10 = (f32[128,16]{0,1:T(8,128)}, f32[128,16]{0,1:T(8,128)S(1)}, u32[]{:S(2)}) copy-start(f32[128,16]{0,1:T(8,128)S(1)} %get-tuple-element.56) | copy-start | bytes 24580
  23.2 9.8 %copy-start.5 = (f32[4,128]{1,0:T(4,128)}, f32[4,128]{1,0:T(4,128)S(1)}, u32[]{:S(2)}) copy-start(f32[4,128]{1,0:T(4,128)S(1)} %get-tuple-element.34.decay_ref) | copy-start | bytes 6148
  23.9 1.0 copy-start.12
  33.0 1.0 copy-start.3
  35.0 26.7 %all-to-all-start.1 = ((bf16[128,8,128]{2,1,0:T(8,128)(2,1)}), bf16[128,8,128]{2,1,0:T(8,128)(2,1)S(1)}, u32[]{:S(2)}, u32[]{:S(2)}) async-start(bf16[128,8,128]{2,1,0:T(8,128)(2,1)} %shard_map.113.front_ref), calls=%async_computation.1 | async-start | bytes 524288 | tf_op jit(solution)/shard_map/all_to_all | solution.py:363
  61.7 0.7 copy-start.8
  68.5 14.7 %collective-permute-start.1 = (bf16[128,4096]{1,0:T(8,128)(2,1)}, bf16[128,4096]{1,0:T(8,128)(2,1)S(1)}, u32[]{:S(2)}, u32[]{:S(2)}) collective-permute-start(bf16[128,4096]{1,0:T(8,128)(2,1)} %get-tuple-element.46.refs_0_), channel_id=1, source_target_pairs={{0,1},{1,2},{2,3},{3,4},{4,5},{5,6},{6,7},{7,8},{8,9},{9,10},{10,1... | collective-permute-start | bytes 3145736 | tf_op jit(solution)/shard_map/ppermute | solution.py:359
  71.1 12.0 %copy-start = (bf16[1,128,4096]{2,1,0:T(8,128)(2,1)S(1)}, bf16[1,128,4096]{2,1,0:T(8,128)(2,1)}, u32[]{:S(2)}) copy-start(bf16[1,128,4096]{2,1,0:T(8,128)(2,1)} %param.10) | copy-start | bytes 3145732
  71.1 12.0 %copy-start.2 = (bf16[128,4096]{1,0:T(8,128)(2,1)S(1)}, bf16[128,4096]{1,0:T(8,128)(2,1)}, u32[]{:S(2)}) copy-start(bf16[128,4096]{1,0:T(8,128)(2,1)} %get-tuple-element.46.refs_0_) | copy-start | bytes 3145732
  71.1 12.0 %copy-start.4 = (f32[128,128]{1,0:T(8,128)S(1)}, f32[128,128]{1,0:T(8,128)}, u32[]{:S(2)}) copy-start(f32[128,128]{1,0:T(8,128)} %get-tuple-element.47.refs_2_) | copy-start | bytes 196612
  73.3 22.9 %all-to-all-start.2 = ((bf16[128,8,128]{2,1,0:T(8,128)(2,1)}), bf16[128,8,128]{2,1,0:T(8,128)(2,1)S(1)}, u32[]{:S(2)}, u32[]{:S(2)}) async-start(bf16[128,8,128]{2,1,0:T(8,128)(2,1)} %get-tuple-element.45), calls=%async_computation.2 | async-start | bytes 524288 | tf_op jit(solution)/shard_map/all_to_all | solution.py:363
  83.1 13.2 %copy-start.6 = (f32[4,128]{1,0:T(4,128)S(1)}, f32[4,128]{1,0:T(4,128)}, u32[]{:S(2)}) copy-start(f32[4,128]{1,0:T(4,128)} %get-tuple-element.49.sum_ref) | copy-start | bytes 6148
  96.3 1.3 %copy-start.1 = (bf16[128,8,128]{2,1,0:T(8,128)(2,1)}, bf16[128,8,128]{2,1,0:T(8,128)(2,1)S(1)}, u32[]{:S(2)}) copy-start(bf16[128,8,128]{2,1,0:T(8,128)(2,1)S(1)} %all-to-all-done.2.x_ref) | copy-start | bytes 786436
  97.6 23.1 %all-to-all-start.3 = ((f32[256,2,128]{2,1,0:T(2,128)}), f32[256,2,128]{2,1,0:T(2,128)S(1)}, u32[]{:S(2)}, u32[]{:S(2)}) async-start(f32[256,2,128]{2,1,0:T(2,128)} %shard_map.120), calls=%async_computation.3 | async-start | bytes 524288 | tf_op jit(solution)/shard_map/all_to_all | solution.py:363

commit v7 on v6

--- a/solution.py
+++ b/solution.py
@@ -409,7 +409,7 @@
     grad_mixer, back_states = call(
         bind(mixer_back_kernel, size, modes), width, step, chunk,
         [None, None, None, group_rows, table_rows], [(None, F32), (state_rows, F32)],
-        [scaled, after, gate, taps, rate_rows], 8,
+        [scaled, after, gate, taps, rate_rows], 8, 52,
     )
     first = whole(
         scan_kernel, [((count, 2 * own_rows, LANES), BF16)],

time: 122 us -> 121 us (level)
  no operation moved by 1% of the time
where the time goes in v7:
time: 121 us
  starting transfers between devices  49.5 us (41%)
  Pallas kernels  49.1 us (41%)
  waiting for transfers between devices  15.2 us (13%)
  local copies, waits for them, and re-layouts  3.48 us (3%)
  other arithmetic  2.51 us (2%)
    all_to_all x4, starting transfers between devices, exchange(): return lax.all_to_all(x, axes, split_axis=0, concat_axis=0, tiled=True)  41.7 us
    pallas_call x7, Pallas kernels, call(): pl.pallas_call(kernel, grid=(width // step,), in_specs=[block(rows) for r...  40.6 us
    all_to_all x4, waiting for transfers between devices, exchange(): return lax.all_to_all(x, axes, split_axis=0, concat_axis=0, tiled=True)  15.2 us
    pallas_call x5, Pallas kernels, whole(): pl.pallas_call(body, out_shape=[jax.ShapeDtypeStruct(shape, kind) for sha...  7.94 us
    ppermute x2, starting transfers between devices, shifted(): lax.ppermute(x, 'ctx', [(i, i + by) for i in range(count) if 0 <= i + by...  7.75 us
  transfers between devices with their start and end apart: 6, of which 5 were waited for; matrix products, arithmetic and copies ran while one was open for 2% of the time, Pallas kernels for 33%

profile of v7, /device:TPU:1, one launch (start us, length us, event | category | flops | bytes accessed | tf_op | source)
XLA Modules:
  0.0 120.6 jit_solution(17295806703729840511)
XLA Ops:
  0.6 0.0 copy-start.9
  0.6 1.8 %fusion.refs_0_.refs_2_ = bf16[128,4096]{1,0:T(8,128)(2,1)S(1)} fusion(bf16[1,128,4096]{2,1,0:T(8,128)(2,1)} %param.9, bf16[1,128,4096]{2,1,0:T(8,128)(2,1)} %param.10), kind=kLoop, calls=%fused_computation.1 | loop fusion | flops 2097152 | bytes 3145728 | tf_op jit(solution)/shard_map/convert_element_type | solution.py:382
  2.4 0.0 copy-start.1
  2.5 5.1 %collective-permute-start = (bf16[128,4096]{1,0:T(8,128)(2,1)S(1)}, bf16[128,4096]{1,0:T(8,128)(2,1)S(1)}, u32[]{:S(2)}, u32[]{:S(2)}) collective-permute-start(bf16[128,4096]{1,0:T(8,128)(2,1)S(1)} %fusion.refs_0_.refs_2_), channel_id=1, source_target_pairs={{1,0},{2,1},{3,2},{4,3},{5,4},{6,5},{7,6},{8,7},{9,8},{10,9},{11,1... | collective-permute-start | bytes 3145736 | tf_op jit(solution)/shard_map/ppermute | solution.py:359
  7.6 0.0 copy-done.9
  7.6 0.1 copy.14.rates_ref
  7.7 0.1 broadcast_in_dim.16
  7.8 1.3 %broadcast_in_dim.17.refs_4_.refs_1_ = f32[2048,128]{1,0:T(8,128)} broadcast(f32[2048]{0:T(1024)S(1)} %broadcast_in_dim.16), dimensions={0} | broadcast | bytes 1056768 | tf_op jit(solution)/shard_map/broadcast_in_dim | solution.py:387
  9.1 0.0 copy-start.11
  9.1 2.5 %shard_map.112 = bf16[512,128]{1,0:T(8,128)(2,1)} custom-call(bf16[128,4096]{1,0:T(8,128)(2,1)} %bitcast.28, f32[2048,128]{1,0:T(8,128)} %broadcast_in_dim.17.refs_4_.refs_1_), custom_call_target="tpu_custom_call" | custom-call | flops 3000000000 | bytes 2097152 | tf_op jit(solution)/shard_map/pallas_call | solution.py:337
  11.6 0.0 copy-start.4
  11.6 10.8 %all-to-all-start = ((bf16[128,4,128]{2,1,0:T(4,128)(2,1)}), bf16[128,4,128]{2,1,0:T(4,128)(2,1)S(1)}, u32[]{:S(2)}, u32[]{:S(2)}) async-start(bf16[128,4,128]{2,1,0:T(4,128)(2,1)} %bitcast.25), calls=%async_computation | async-start | bytes 262144 | tf_op jit(solution)/shard_map/all_to_all | solution.py:363
  22.4 0.1 reshape.39
  22.5 0.0 copy-done.11
  22.5 0.0 copy-start.10
  22.6 0.1 copy.17
  22.7 0.1 reshape.40
  22.7 0.6 shard_map.110
  23.3 0.0 copy-start.6
  23.3 0.7 pad_maximum_fusion
  24.1 0.0 collective-permute-done.refs_1_.refs_3_
  24.1 0.0 copy-start.12
  24.1 0.0 copy-done.1
  24.1 1.0 copy-done.12
  25.0 0.0 copy-done.4
  25.0 7.5 %shard_map.111 = (f32[128,4096]{1,0:T(8,128)}, f32[512,128]{1,0:T(8,128)S(1)}) custom-call(bf16[128,4096]{1,0:T(8,128)(2,1)S(1)} %fusion.refs_0_.refs_2_, bf16[128,4096]{1,0:T(8,128)(2,1)} %copy-done.12, bf16[128,4096]{1,0:T(8,128)(2,1)} %bitcast.30, f32[128,128]{1,0:T(8,128)S(1)} %copy-done.4, f32[2048,128]{1,0:T(8,128)} %broadcast_in_dim.17.refs_4_.refs_1_), custom_call_target="tpu_custom_call" | custom-call | flops 8000000000 | bytes 4259840 | tf_op jit(solution)/shard_map/pallas_call | solution.py:337
  32.5 0.0 copy-done.10
  32.5 0.6 all-to-all-done.x_ref
  33.2 0.0 copy-done.6
  33.2 1.0 shard_map.113.front_ref
  34.2 13.2 %all-to-all-start.1 = ((bf16[128,8,128]{2,1,0:T(8,128)(2,1)}), bf16[128,8,128]{2,1,0:T(8,128)(2,1)S(1)}, u32[]{:S(2)}, u32[]{:S(2)}) async-start(bf16[128,8,128]{2,1,0:T(8,128)(2,1)} %shard_map.113.front_ref), calls=%async_computation.1 | async-start | bytes 524288 | tf_op jit(solution)/shard_map/all_to_all | solution.py:363
  47.3 2.5 %shard_map.114 = (f32[128,128]{1,0:T(8,128)}, f32[128,128]{1,0:T(8,128)}, f32[128,128]{1,0:T(8,128)}) custom-call(f32[16,128]{1,0:T(8,128)} %bitcast.26, f32[16,128]{1,0:T(8,128)} %bitcast.27, f32[128,128]{1,0:T(8,128)} %taps_ref), custom_call_target="tpu_custom_call" | custom-call | flops 2000000000 | bytes 1048576 | tf_op jit(solution)/shard_map/pallas_call | solution.py:349
  49.8 8.5 %shard_map.115 = (f32[128,4096]{1,0:T(8,128)}, bf16[4096,128]{1,0:T(8,128)(2,1)}, f32[128,128]{1,0:T(8,128)}) custom-call(bf16[128,4096]{1,0:T(8,128)(2,1)} %bitcast.29, bf16[128,4096]{1,0:T(8,128)(2,1)} %bitcast.31, f32[128,4096]{1,0:T(8,128)} %get-tuple-element.33.refs_2_.refs_0_.refs_1_, f32[128,128]{1,0:T(8,128)} %get-tuple-element.40.refs_3_, ...), custom_call_target="tpu_custom_call" | custom-call | flops 10000000000 | bytes 4292608 | tf_op jit(solution)/shard_map/pallas_call | solution.py:337
  58.3 2.2 %all-to-all-done.1.x_ref = bf16[128,8,128]{2,1,0:T(8,128)(2,1)S(1)} async-done(((bf16[128,8,128]{2,1,0:T(8,128)(2,1)}), bf16[128,8,128]{2,1,0:T(8,128)(2,1)S(1)}, u32[]{:S(2)}, u32[]{:S(2)}) %all-to-all-start.1) | async-done | bytes 262176 | tf_op jit(solution)/shard_map/all_to_all | solution.py:363
  60.6 0.0 copy-start.8
  60.6 0.7 copy-done.8
  61.3 6.1 %shard_map.116 = (bf16[128,4096]{1,0:T(8,128)(2,1)}, f32[128,128]{1,0:T(8,128)}) custom-call(f32[128,4096]{1,0:T(8,128)} %get-tuple-element.51.refs_0_, bf16[128,4096]{1,0:T(8,128)(2,1)} %bitcast.32, bf16[128,4096]{1,0:T(8,128)(2,1)} %copy-done.1, bf16[128,4096]{1,0:T(8,128)(2,1)} %copy-done.12, bf16[4096,128]{1,0:T(8,128)(2,1)} %get-tuple-element.42.refs_4_.refs_2_, ...), custom_call_target="tpu_custom_call" | custom-call | flops 6000000000 | bytes 6553600 | tf_op jit(solution)/shard_map/pallas_call | solution.py:337
  67.3 2.6 %collective-permute-start.1 = (bf16[128,4096]{1,0:T(8,128)(2,1)}, bf16[128,4096]{1,0:T(8,128)(2,1)S(1)}, u32[]{:S(2)}, u32[]{:S(2)}) collective-permute-start(bf16[128,4096]{1,0:T(8,128)(2,1)} %get-tuple-element.46.refs_0_), channel_id=1, source_target_pairs={{0,1},{1,2},{2,3},{3,4},{4,5},{5,6},{6,7},{7,8},{8,9},{9,10},{10,1... | collective-permute-start | bytes 3145736 | tf_op jit(solution)/shard_map/ppermute | solution.py:359
  70.0 0.0 copy-start
  70.0 0.0 copy-start.3
  70.0 0.0 copy-start.5
  70.0 2.2 %shard_map.117 = (bf16[128,8,128]{2,1,0:T(8,128)(2,1)}, f32[4,128]{1,0:T(4,128)}) custom-call(bf16[128,8,128]{2,1,0:T(8,128)(2,1)} %copy-done.8, f32[4,128]{1,0:T(4,128)} %copy-done.6, bf16[128,8,128]{2,1,0:T(8,128)(2,1)} %shard_map.113.front_ref, f32[128,128]{1,0:T(8,128)} %get-tuple-element.43.tap_ref, f32[128,128]{1,0:T(8,128)} %get-tuple-element.44.cot_ref), custom_call_target="tpu_custom_call" | custom-call | flops 2000000000 | bytes 1048576 | tf_op jit(solution)/shard_map/pallas_call | solution.py:349
  72.2 9.7 %all-to-all-start.2 = ((bf16[128,8,128]{2,1,0:T(8,128)(2,1)}), bf16[128,8,128]{2,1,0:T(8,128)(2,1)S(1)}, u32[]{:S(2)}, u32[]{:S(2)}) async-start(bf16[128,8,128]{2,1,0:T(8,128)(2,1)} %get-tuple-element.45), calls=%async_computation.2 | async-start | bytes 524288 | tf_op jit(solution)/shard_map/all_to_all | solution.py:363
  81.9 0.1 collective-permute-done.1.refs_1_
  82.0 0.0 copy-done
  82.0 0.0 copy-done.3
  82.0 0.0 copy-done.5
  82.0 0.0 copy-start.7
  82.0 5.9 %shard_map.118 = bf16[128,4096]{1,0:T(8,128)(2,1)} custom-call(bf16[128,4096]{1,0:T(8,128)(2,1)S(1)} %copy-done.3, bf16[128,4096]{1,0:T(8,128)(2,1)S(1)} %collective-permute-done.1.refs_1_, f32[128,128]{1,0:T(8,128)S(1)} %copy-done.5, bf16[128,4096]{1,0:T(8,128)(2,1)S(1)} %bitcast.20), custom_call_target="tpu_custom_call" | custom-call | flops 7000000000 | bytes 3211264 | tf_op jit(solution)/shard_map/pallas_call | solution.py:337
  87.9 7.3 %all-to-all-done.2.x_ref = bf16[128,8,128]{2,1,0:T(8,128)(2,1)S(1)} async-done(((bf16[128,8,128]{2,1,0:T(8,128)(2,1)}), bf16[128,8,128]{2,1,0:T(8,128)(2,1)S(1)}, u32[]{:S(2)}, u32[]{:S(2)}) %all-to-all-start.2) | async-done | bytes 262176 | tf_op jit(solution)/shard_map/all_to_all | solution.py:363
  95.2 0.0 copy-start.2
  95.2 0.0 copy-done.7
  95.2 1.3 %shard_map.120 = f32[256,2,128]{2,1,0:T(2,128)} custom-call(bf16[128,8,128]{2,1,0:T(8,128)(2,1)S(1)} %all-to-all-done.2.x_ref, f32[4,128]{1,0:T(4,128)S(1)} %copy-done.7, f32[16,128]{1,0:T(8,128)S(1)} %get-tuple-element.50.lam_ref), custom_call_target="tpu_custom_call" | custom-call | flops 2000000000 | bytes 1048576 | tf_op jit(solution)/shard_map/pallas_call | solution.py:349
  96.5 0.0 copy-done.2
  96.5 8.0 %all-to-all-start.3 = ((f32[256,2,128]{2,1,0:T(2,128)}), f32[256,2,128]{2,1,0:T(2,128)S(1)}, u32[]{:S(2)}, u32[]{:S(2)}) async-start(f32[256,2,128]{2,1,0:T(2,128)} %shard_map.120), calls=%async_computation.3 | async-start | bytes 524288 | tf_op jit(solution)/shard_map/all_to_all | solution.py:363
  104.5 3.6 %shard_map.121 = bf16[128,4096]{1,0:T(8,128)(2,1)} custom-call(f32[128,4096]{1,0:T(8,128)} %get-tuple-element.51.refs_0_, f32[128,4096]{1,0:T(8,128)} %get-tuple-element.33.refs_2_.refs_0_.refs_1_, bf16[4096,128]{1,0:T(8,128)(2,1)} %get-tuple-element.42.refs_4_.refs_2_, bf16[1024,128]{1,0:T(8,128)(2,1)} %bitcast.24), custom_call_target="tpu_custom_call" | custom-call | flops 4000000000 | bytes 5505024 | tf_op jit(solution)/shard_map/pallas_call | solution.py:337
  108.1 6.5 %shard_map.119 = bf16[128,4096]{1,0:T(8,128)(2,1)} custom-call(f32[128,4096]{1,0:T(8,128)} %get-tuple-element.33.refs_2_.refs_0_.refs_1_, bf16[128,4096]{1,0:T(8,128)(2,1)} %bitcast.33, f32[128,128]{1,0:T(8,128)} %get-tuple-element.39.refs_2_, f32[32,128]{1,0:T(8,128)} %get-tuple-element.57.refs_4_.refs_3_, f32[32,128]{1,0:T(8,128)} %get-tuple-element.58.refs_5_.refs_4_, ...), custom_call_target="tpu_custom_call" | custom-call | flops 7000000000 | bytes 3506176 | tf_op jit(solution)/shard_map/pallas_call | solution.py:337
  114.6 5.1 %all-to-all-done.3.x_ref = f32[256,2,128]{2,1,0:T(2,128)S(1)} async-done(((f32[256,2,128]{2,1,0:T(2,128)}), f32[256,2,128]{2,1,0:T(2,128)S(1)}, u32[]{:S(2)}, u32[]{:S(2)}) %all-to-all-start.3) | async-done | bytes 262176 | tf_op jit(solution)/shard_map/all_to_all | solution.py:363
  119.7 0.9 shard_map.122
  (1 shorter events, 0.0 us)
Async XLA Ops:
  0.6 7.0 %copy-start.9 = (f32[128,16]{0,1:T(8,128)S(1)}, f32[128,16]{0,1:T(8,128)}, u32[]{:S(2)}) copy-start(f32[128,16]{0,1:T(8,128)} %param.12) | copy-start | bytes 24580
  2.4 21.6 %copy-start.1 = (bf16[128,4096]{1,0:T(8,128)(2,1)}, bf16[128,4096]{1,0:T(8,128)(2,1)S(1)}, u32[]{:S(2)}) copy-start(bf16[128,4096]{1,0:T(8,128)(2,1)S(1)} %fusion.refs_0_.refs_2_) | copy-start | bytes 3145732
  2.5 21.6 %collective-permute-start = (bf16[128,4096]{1,0:T(8,128)(2,1)S(1)}, bf16[128,4096]{1,0:T(8,128)(2,1)S(1)}, u32[]{:S(2)}, u32[]{:S(2)}) collective-permute-start(bf16[128,4096]{1,0:T(8,128)(2,1)S(1)} %fusion.refs_0_.refs_2_), channel_id=1, source_target_pairs={{1,0},{2,1},{3,2},{4,3},{5,4},{6,5},{7,6},{8,7},{9,8},{10,9},{11,1... | collective-permute-start | bytes 3145736 | tf_op jit(solution)/shard_map/ppermute | solution.py:359
  9.1 13.4 %copy-start.11 = (f32[128,16]{0,1:T(8,128)S(1)}, f32[128,16]{0,1:T(8,128)}, u32[]{:S(2)}) copy-start(f32[128,16]{0,1:T(8,128)} %param.11) | copy-start | bytes 24580
  11.6 13.4 %copy-start.4 = (f32[128,128]{1,0:T(8,128)S(1)}, f32[128,128]{1,0:T(8,128)}, u32[]{:S(2)}) copy-start(f32[128,128]{1,0:T(8,128)} %taps_ref) | copy-start | bytes 196612
  11.6 21.6 %all-to-all-start = ((bf16[128,4,128]{2,1,0:T(4,128)(2,1)}), bf16[128,4,128]{2,1,0:T(4,128)(2,1)S(1)}, u32[]{:S(2)}, u32[]{:S(2)}) async-start(bf16[128,4,128]{2,1,0:T(4,128)(2,1)} %bitcast.25), calls=%async_computation | async-start | bytes 262144 | tf_op jit(solution)/shard_map/all_to_all | solution.py:363
  22.5 10.0 %copy-start.10 = (f32[128,16]{0,1:T(8,128)}, f32[128,16]{0,1:T(8,128)S(1)}, u32[]{:S(2)}) copy-start(f32[128,16]{0,1:T(8,128)S(1)} %get-tuple-element.56) | copy-start | bytes 24580
  23.3 9.8 %copy-start.6 = (f32[4,128]{1,0:T(4,128)}, f32[4,128]{1,0:T(4,128)S(1)}, u32[]{:S(2)}) copy-start(f32[4,128]{1,0:T(4,128)S(1)} %get-tuple-element.34.decay_ref) | copy-start | bytes 6148
  24.1 1.0 copy-start.12
  34.2 26.4 %all-to-all-start.1 = ((bf16[128,8,128]{2,1,0:T(8,128)(2,1)}), bf16[128,8,128]{2,1,0:T(8,128)(2,1)S(1)}, u32[]{:S(2)}, u32[]{:S(2)}) async-start(bf16[128,8,128]{2,1,0:T(8,128)(2,1)} %shard_map.113.front_ref), calls=%async_computation.1 | async-start | bytes 524288 | tf_op jit(solution)/shard_map/all_to_all | solution.py:363
  60.6 0.7 copy-start.8
  67.3 14.6 %collective-permute-start.1 = (bf16[128,4096]{1,0:T(8,128)(2,1)}, bf16[128,4096]{1,0:T(8,128)(2,1)S(1)}, u32[]{:S(2)}, u32[]{:S(2)}) collective-permute-start(bf16[128,4096]{1,0:T(8,128)(2,1)} %get-tuple-element.46.refs_0_), channel_id=1, source_target_pairs={{0,1},{1,2},{2,3},{3,4},{4,5},{5,6},{6,7},{7,8},{8,9},{9,10},{10,1... | collective-permute-start | bytes 3145736 | tf_op jit(solution)/shard_map/ppermute | solution.py:359
  70.0 12.0 %copy-start = (bf16[1,128,4096]{2,1,0:T(8,128)(2,1)S(1)}, bf16[1,128,4096]{2,1,0:T(8,128)(2,1)}, u32[]{:S(2)}) copy-start(bf16[1,128,4096]{2,1,0:T(8,128)(2,1)} %param.10) | copy-start | bytes 3145732
  70.0 12.0 %copy-start.3 = (bf16[128,4096]{1,0:T(8,128)(2,1)S(1)}, bf16[128,4096]{1,0:T(8,128)(2,1)}, u32[]{:S(2)}) copy-start(bf16[128,4096]{1,0:T(8,128)(2,1)} %get-tuple-element.46.refs_0_) | copy-start | bytes 3145732
  70.0 12.0 %copy-start.5 = (f32[128,128]{1,0:T(8,128)S(1)}, f32[128,128]{1,0:T(8,128)}, u32[]{:S(2)}) copy-start(f32[128,128]{1,0:T(8,128)} %get-tuple-element.47.refs_2_) | copy-start | bytes 196612
  72.2 22.9 %all-to-all-start.2 = ((bf16[128,8,128]{2,1,0:T(8,128)(2,1)}), bf16[128,8,128]{2,1,0:T(8,128)(2,1)S(1)}, u32[]{:S(2)}, u32[]{:S(2)}) async-start(bf16[128,8,128]{2,1,0:T(8,128)(2,1)} %get-tuple-element.45), calls=%async_computation.2 | async-start | bytes 524288 | tf_op jit(solution)/shard_map/all_to_all | solution.py:363
  82.0 13.2 %copy-start.7 = (f32[4,128]{1,0:T(4,128)S(1)}, f32[4,128]{1,0:T(4,128)}, u32[]{:S(2)}) copy-start(f32[4,128]{1,0:T(4,128)} %get-tuple-element.49.sum_ref) | copy-start | bytes 6148
  95.2 1.3 %copy-start.2 = (bf16[128,8,128]{2,1,0:T(8,128)(2,1)}, bf16[128,8,128]{2,1,0:T(8,128)(2,1)S(1)}, u32[]{:S(2)}) copy-start(bf16[128,8,128]{2,1,0:T(8,128)(2,1)S(1)} %all-to-all-done.2.x_ref) | copy-start | bytes 786436
  96.5 23.2 %all-to-all-start.3 = ((f32[256,2,128]{2,1,0:T(2,128)}), f32[256,2,128]{2,1,0:T(2,128)S(1)}, u32[]{:S(2)}, u32[]{:S(2)}) async-start(f32[256,2,128]{2,1,0:T(2,128)} %shard_map.120), calls=%async_computation.3 | async-start | bytes 524288 | tf_op jit(solution)/shard_map/all_to_all | solution.py:363

commit v8 on v7

--- a/solution.py
+++ b/solution.py
@@ -427,12 +427,12 @@
     mixer_in, lag_taps = call(
         bind(values_kernel, size, modes), width, step, chunk,
         [None, None, None, None, carry_rows, 2 * state_rows], [(None, BF16), (group_rows, F32)],
-        [local, gate, scaled, after, front_table, second.reshape(-1, LANES)], 6,
+        [local, gate, scaled, after, front_table, second.reshape(-1, LANES)], 6, 52,
     )
     before = shifted(mixer_in, 1)
     message, state_sums = whole(
         back_scan_kernel, [(first.shape, BF16), (decay.shape, F32)],
-        [second, decay, first, lag_taps, lag_cot], 60,
+        [second, decay, first, lag_taps, lag_cot], 52,
     )
     third = exchange(message)
     grad_gate_mr = call(

time: 121 us -> 120 us (level)
  transfers between devices with their start and end apart: 6 -> 6, of which waited for: 5 -> 4; matrix products, arithmetic and copies ran while one was open for 2% -> 2% of each run, Pallas kernels for 33% -> 33%
where the time goes in v8:
time: 120 us; the launch traced here: 119 us
  starting transfers between devices  49.4 us (41%)
  Pallas kernels  48.4 us (40%)
  waiting for transfers between devices  15.3 us (13%)
  local copies, waits for them, and re-layouts  2.76 us (2%)
  other arithmetic  2.52 us (2%)
    all_to_all x4, starting transfers between devices, exchange(): return lax.all_to_all(x, axes, split_axis=0, concat_axis=0, tiled=True)  41.6 us
    pallas_call x7, Pallas kernels, call(): pl.pallas_call(kernel, grid=(width // step,), in_specs=[block(rows) for r...  40.1 us
    all_to_all x4, waiting for transfers between devices, exchange(): return lax.all_to_all(x, axes, split_axis=0, concat_axis=0, tiled=True)  15.3 us
    ppermute x2, starting transfers between devices, shifted(): lax.ppermute(x, 'ctx', [(i, i + by) for i in range(count) if 0 <= i + by...  7.78 us
    pallas_call x5, Pallas kernels, whole(): pl.pallas_call(body, out_shape=[jax.ShapeDtypeStruct(shape, kind) for sha...  7.73 us
  transfers between devices with their start and end apart: 6, of which 4 were waited for; matrix products, arithmetic and copies ran while one was open for 2% of the time, Pallas kernels for 33%

profile of v8, /device:TPU:1, one launch (start us, length us, event | category | flops | bytes accessed | tf_op | source)
XLA Modules:
  0.0 119.2 jit_solution(17969566813045826099)
XLA Ops:
  0.6 0.0 copy-start.7
  0.6 1.8 %fusion.refs_0_.refs_2_ = bf16[128,4096]{1,0:T(8,128)(2,1)S(1)} fusion(bf16[1,128,4096]{2,1,0:T(8,128)(2,1)} %param.9, bf16[1,128,4096]{2,1,0:T(8,128)(2,1)} %param.10), kind=kLoop, calls=%fused_computation.1 | loop fusion | flops 2097152 | bytes 3145728 | tf_op jit(solution)/shard_map/convert_element_type | solution.py:382
  2.4 0.0 copy-start.1
  2.5 5.1 %collective-permute-start = (bf16[128,4096]{1,0:T(8,128)(2,1)S(1)}, bf16[128,4096]{1,0:T(8,128)(2,1)S(1)}, u32[]{:S(2)}, u32[]{:S(2)}) collective-permute-start(bf16[128,4096]{1,0:T(8,128)(2,1)S(1)} %fusion.refs_0_.refs_2_), channel_id=1, source_target_pairs={{1,0},{2,1},{3,2},{4,3},{5,4},{6,5},{7,6},{8,7},{9,8},{10,9},{11,1... | collective-permute-start | bytes 3145736 | tf_op jit(solution)/shard_map/ppermute | solution.py:359
  7.6 0.0 copy-done.7
  7.6 0.1 copy.14.rates_ref
  7.7 0.1 broadcast_in_dim.16
  7.8 1.3 %broadcast_in_dim.17.refs_4_.refs_1_ = f32[2048,128]{1,0:T(8,128)} broadcast(f32[2048]{0:T(1024)S(1)} %broadcast_in_dim.16), dimensions={0} | broadcast | bytes 1056768 | tf_op jit(solution)/shard_map/broadcast_in_dim | solution.py:387
  9.1 0.0 copy-start.9
  9.1 2.5 %shard_map.112 = bf16[512,128]{1,0:T(8,128)(2,1)} custom-call(bf16[128,4096]{1,0:T(8,128)(2,1)} %bitcast.28, f32[2048,128]{1,0:T(8,128)} %broadcast_in_dim.17.refs_4_.refs_1_), custom_call_target="tpu_custom_call" | custom-call | flops 3000000000 | bytes 2097152 | tf_op jit(solution)/shard_map/pallas_call | solution.py:337
  11.6 0.0 copy-start.4
  11.6 10.8 %all-to-all-start = ((bf16[128,4,128]{2,1,0:T(4,128)(2,1)}), bf16[128,4,128]{2,1,0:T(4,128)(2,1)S(1)}, u32[]{:S(2)}, u32[]{:S(2)}) async-start(bf16[128,4,128]{2,1,0:T(4,128)(2,1)} %bitcast.25), calls=%async_computation | async-start | bytes 262144 | tf_op jit(solution)/shard_map/all_to_all | solution.py:363
  22.4 0.1 reshape.39
  22.5 0.0 copy-done.9
  22.5 0.0 copy-start.8
  22.6 0.1 copy.17
  22.7 0.1 reshape.40
  22.7 0.6 shard_map.110
  23.3 0.7 pad_maximum_fusion
  24.1 0.0 collective-permute-done.refs_1_.refs_3_
  24.1 0.0 copy-start.10
  24.1 0.0 copy-done.1
  24.1 1.0 copy-done.10
  25.0 0.0 copy-done.4
  25.0 7.5 %shard_map.111 = (f32[128,4096]{1,0:T(8,128)}, f32[512,128]{1,0:T(8,128)S(1)}) custom-call(bf16[128,4096]{1,0:T(8,128)(2,1)S(1)} %fusion.refs_0_.refs_2_, bf16[128,4096]{1,0:T(8,128)(2,1)} %copy-done.10, bf16[128,4096]{1,0:T(8,128)(2,1)} %bitcast.30, f32[128,128]{1,0:T(8,128)S(1)} %copy-done.4, f32[2048,128]{1,0:T(8,128)} %broadcast_in_dim.17.refs_4_.refs_1_), custom_call_target="tpu_custom_call" | custom-call | flops 8000000000 | bytes 4259840 | tf_op jit(solution)/shard_map/pallas_call | solution.py:337
  32.5 0.0 copy-done.8
  32.5 0.7 all-to-all-done.x_ref
  33.2 1.0 shard_map.113.front_ref
  34.2 13.1 %all-to-all-start.1 = ((bf16[128,8,128]{2,1,0:T(8,128)(2,1)}), bf16[128,8,128]{2,1,0:T(8,128)(2,1)S(1)}, u32[]{:S(2)}, u32[]{:S(2)}) async-start(bf16[128,8,128]{2,1,0:T(8,128)(2,1)} %shard_map.113.front_ref), calls=%async_computation.1 | async-start | bytes 524288 | tf_op jit(solution)/shard_map/all_to_all | solution.py:363
  47.3 2.5 %shard_map.114 = (f32[128,128]{1,0:T(8,128)}, f32[128,128]{1,0:T(8,128)}, f32[128,128]{1,0:T(8,128)}) custom-call(f32[16,128]{1,0:T(8,128)} %bitcast.26, f32[16,128]{1,0:T(8,128)} %bitcast.27, f32[128,128]{1,0:T(8,128)} %taps_ref), custom_call_target="tpu_custom_call" | custom-call | flops 2000000000 | bytes 1048576 | tf_op jit(solution)/shard_map/pallas_call | solution.py:349
  49.8 8.5 %shard_map.115 = (f32[128,4096]{1,0:T(8,128)}, bf16[4096,128]{1,0:T(8,128)(2,1)}, f32[128,128]{1,0:T(8,128)}) custom-call(bf16[128,4096]{1,0:T(8,128)(2,1)} %bitcast.29, bf16[128,4096]{1,0:T(8,128)(2,1)} %bitcast.31, f32[128,4096]{1,0:T(8,128)} %get-tuple-element.33.refs_2_.refs_0_.refs_1_, f32[128,128]{1,0:T(8,128)} %get-tuple-element.40.refs_3_, ...), custom_call_target="tpu_custom_call" | custom-call | flops 10000000000 | bytes 4292608 | tf_op jit(solution)/shard_map/pallas_call | solution.py:337
  58.3 2.2 %all-to-all-done.1.x_ref = bf16[128,8,128]{2,1,0:T(8,128)(2,1)S(1)} async-done(((bf16[128,8,128]{2,1,0:T(8,128)(2,1)}), bf16[128,8,128]{2,1,0:T(8,128)(2,1)S(1)}, u32[]{:S(2)}, u32[]{:S(2)}) %all-to-all-start.1) | async-done | bytes 262176 | tf_op jit(solution)/shard_map/all_to_all | solution.py:363
  60.5 0.0 copy-start.2
  60.5 0.0 copy-start.5
  60.5 5.6 %shard_map.116 = (bf16[128,4096]{1,0:T(8,128)(2,1)S(1)}, f32[128,128]{1,0:T(8,128)S(1)}) custom-call(f32[128,4096]{1,0:T(8,128)} %get-tuple-element.51.refs_0_, bf16[128,4096]{1,0:T(8,128)(2,1)} %bitcast.32, bf16[128,4096]{1,0:T(8,128)(2,1)} %copy-done.1, bf16[128,4096]{1,0:T(8,128)(2,1)} %copy-done.10, bf16[4096,128]{1,0:T(8,128)(2,1)} %get-tuple-element.42.refs_4_.refs_2_, ...), custom_call_target="tpu_custom_call" | custom-call | flops 6000000000 | bytes 6553600 | tf_op jit(solution)/shard_map/pallas_call | solution.py:337
  66.1 2.6 %collective-permute-start.1 = (bf16[128,4096]{1,0:T(8,128)(2,1)S(1)}, bf16[128,4096]{1,0:T(8,128)(2,1)S(1)}, u32[]{:S(2)}, u32[]{:S(2)}) collective-permute-start(bf16[128,4096]{1,0:T(8,128)(2,1)S(1)} %get-tuple-element.46.refs_0_), channel_id=1, source_target_pairs={{0,1},{1,2},{2,3},{3,4},{4,5},{5,6},{6,7},{7,8},{8,9},{9,10},{10,1... | collective-permute-start | bytes 3145736 | tf_op jit(solution)/shard_map/ppermute | solution.py:359
  68.8 0.0 copy-done.2
  68.8 0.0 copy-done.5
  68.8 0.0 copy-start
  68.8 0.0 copy-start.6
  68.8 2.0 %shard_map.117 = (bf16[128,8,128]{2,1,0:T(8,128)(2,1)}, f32[4,128]{1,0:T(4,128)S(1)}) custom-call(bf16[128,8,128]{2,1,0:T(8,128)(2,1)S(1)} %all-to-all-done.1.x_ref, f32[4,128]{1,0:T(4,128)S(1)} %get-tuple-element.34.decay_ref, bf16[128,8,128]{2,1,0:T(8,128)(2,1)} %shard_map.113.front_ref, f32[128,128]{1,0:T(8,128)S(1)} %get-tuple-element.43.tap_ref, ...), custom_call_target="tpu_custom_call" | custom-call | flops 2000000000 | bytes 1048576 | tf_op jit(solution)/shard_map/pallas_call | solution.py:349
  70.8 9.7 %all-to-all-start.2 = ((bf16[128,8,128]{2,1,0:T(8,128)(2,1)}), bf16[128,8,128]{2,1,0:T(8,128)(2,1)S(1)}, u32[]{:S(2)}, u32[]{:S(2)}) async-start(bf16[128,8,128]{2,1,0:T(8,128)(2,1)} %get-tuple-element.45), calls=%async_computation.2 | async-start | bytes 524288 | tf_op jit(solution)/shard_map/all_to_all | solution.py:363
  80.6 0.0 collective-permute-done.1.refs_1_
  80.6 0.0 copy-done
  80.6 0.0 copy-done.6
  80.6 5.9 %shard_map.118 = bf16[128,4096]{1,0:T(8,128)(2,1)} custom-call(bf16[128,4096]{1,0:T(8,128)(2,1)S(1)} %get-tuple-element.46.refs_0_, bf16[128,4096]{1,0:T(8,128)(2,1)S(1)} %collective-permute-done.1.refs_1_, f32[128,128]{1,0:T(8,128)S(1)} %copy-done.6, bf16[128,4096]{1,0:T(8,128)(2,1)S(1)} %bitcast.20), custom_call_target="tpu_custom_call" | custom-call | flops 7000000000 | bytes 3211264 | tf_op jit(solution)/shard_map/pallas_call | solution.py:337
  86.5 7.3 %all-to-all-done.2.x_ref = bf16[128,8,128]{2,1,0:T(8,128)(2,1)S(1)} async-done(((bf16[128,8,128]{2,1,0:T(8,128)(2,1)}), bf16[128,8,128]{2,1,0:T(8,128)(2,1)S(1)}, u32[]{:S(2)}, u32[]{:S(2)}) %all-to-all-start.2) | async-done | bytes 262176 | tf_op jit(solution)/shard_map/all_to_all | solution.py:363
  93.8 0.0 copy-start.3
  93.8 1.3 %shard_map.120 = f32[256,2,128]{2,1,0:T(2,128)} custom-call(bf16[128,8,128]{2,1,0:T(8,128)(2,1)S(1)} %all-to-all-done.2.x_ref, f32[4,128]{1,0:T(4,128)S(1)} %get-tuple-element.49.sum_ref, f32[16,128]{1,0:T(8,128)S(1)} %get-tuple-element.50.lam_ref), custom_call_target="tpu_custom_call" | custom-call | flops 2000000000 | bytes 1048576 | tf_op jit(solution)/shard_map/pallas_call | solution.py:349
  95.1 0.0 copy-done.3
  95.1 8.0 %all-to-all-start.3 = ((f32[256,2,128]{2,1,0:T(2,128)}), f32[256,2,128]{2,1,0:T(2,128)S(1)}, u32[]{:S(2)}, u32[]{:S(2)}) async-start(f32[256,2,128]{2,1,0:T(2,128)} %shard_map.120), calls=%async_computation.3 | async-start | bytes 524288 | tf_op jit(solution)/shard_map/all_to_all | solution.py:363
  103.1 3.6 %shard_map.121 = bf16[128,4096]{1,0:T(8,128)(2,1)} custom-call(f32[128,4096]{1,0:T(8,128)} %get-tuple-element.51.refs_0_, f32[128,4096]{1,0:T(8,128)} %get-tuple-element.33.refs_2_.refs_0_.refs_1_, bf16[4096,128]{1,0:T(8,128)(2,1)} %get-tuple-element.42.refs_4_.refs_2_, bf16[1024,128]{1,0:T(8,128)(2,1)} %bitcast.22), custom_call_target="tpu_custom_call" | custom-call | flops 4000000000 | bytes 5505024 | tf_op jit(solution)/shard_map/pallas_call | solution.py:337
  106.7 6.5 %shard_map.119 = bf16[128,4096]{1,0:T(8,128)(2,1)} custom-call(f32[128,4096]{1,0:T(8,128)} %get-tuple-element.33.refs_2_.refs_0_.refs_1_, bf16[128,4096]{1,0:T(8,128)(2,1)} %bitcast.33, f32[128,128]{1,0:T(8,128)} %get-tuple-element.39.refs_2_, f32[32,128]{1,0:T(8,128)} %get-tuple-element.57.refs_4_.refs_3_, f32[32,128]{1,0:T(8,128)} %get-tuple-element.58.refs_5_.refs_4_, ...), custom_call_target="tpu_custom_call" | custom-call | flops 7000000000 | bytes 3506176 | tf_op jit(solution)/shard_map/pallas_call | solution.py:337
  113.2 5.1 %all-to-all-done.3.x_ref = f32[256,2,128]{2,1,0:T(2,128)S(1)} async-done(((f32[256,2,128]{2,1,0:T(2,128)}), f32[256,2,128]{2,1,0:T(2,128)S(1)}, u32[]{:S(2)}, u32[]{:S(2)}) %all-to-all-start.3) | async-done | bytes 262176 | tf_op jit(solution)/shard_map/all_to_all | solution.py:363
  118.3 0.9 shard_map.122
  (1 shorter events, 0.0 us)
Async XLA Ops:
  0.6 7.0 %copy-start.7 = (f32[128,16]{0,1:T(8,128)S(1)}, f32[128,16]{0,1:T(8,128)}, u32[]{:S(2)}) copy-start(f32[128,16]{0,1:T(8,128)} %param.12) | copy-start | bytes 24580
  2.4 21.6 %copy-start.1 = (bf16[128,4096]{1,0:T(8,128)(2,1)}, bf16[128,4096]{1,0:T(8,128)(2,1)S(1)}, u32[]{:S(2)}) copy-start(bf16[128,4096]{1,0:T(8,128)(2,1)S(1)} %fusion.refs_0_.refs_2_) | copy-start | bytes 3145732
  2.5 21.6 %collective-permute-start = (bf16[128,4096]{1,0:T(8,128)(2,1)S(1)}, bf16[128,4096]{1,0:T(8,128)(2,1)S(1)}, u32[]{:S(2)}, u32[]{:S(2)}) collective-permute-start(bf16[128,4096]{1,0:T(8,128)(2,1)S(1)} %fusion.refs_0_.refs_2_), channel_id=1, source_target_pairs={{1,0},{2,1},{3,2},{4,3},{5,4},{6,5},{7,6},{8,7},{9,8},{10,9},{11,1... | collective-permute-start | bytes 3145736 | tf_op jit(solution)/shard_map/ppermute | solution.py:359
  9.1 13.4 %copy-start.9 = (f32[128,16]{0,1:T(8,128)S(1)}, f32[128,16]{0,1:T(8,128)}, u32[]{:S(2)}) copy-start(f32[128,16]{0,1:T(8,128)} %param.11) | copy-start | bytes 24580
  11.6 13.4 %copy-start.4 = (f32[128,128]{1,0:T(8,128)S(1)}, f32[128,128]{1,0:T(8,128)}, u32[]{:S(2)}) copy-start(f32[128,128]{1,0:T(8,128)} %taps_ref) | copy-start | bytes 196612
  11.6 21.6 %all-to-all-start = ((bf16[128,4,128]{2,1,0:T(4,128)(2,1)}), bf16[128,4,128]{2,1,0:T(4,128)(2,1)S(1)}, u32[]{:S(2)}, u32[]{:S(2)}) async-start(bf16[128,4,128]{2,1,0:T(4,128)(2,1)} %bitcast.25), calls=%async_computation | async-start | bytes 262144 | tf_op jit(solution)/shard_map/all_to_all | solution.py:363
  22.5 10.0 %copy-start.8 = (f32[128,16]{0,1:T(8,128)}, f32[128,16]{0,1:T(8,128)S(1)}, u32[]{:S(2)}) copy-start(f32[128,16]{0,1:T(8,128)S(1)} %get-tuple-element.56) | copy-start | bytes 24580
  24.1 1.0 copy-start.10
  34.2 26.3 %all-to-all-start.1 = ((bf16[128,8,128]{2,1,0:T(8,128)(2,1)}), bf16[128,8,128]{2,1,0:T(8,128)(2,1)S(1)}, u32[]{:S(2)}, u32[]{:S(2)}) async-start(bf16[128,8,128]{2,1,0:T(8,128)(2,1)} %shard_map.113.front_ref), calls=%async_computation.1 | async-start | bytes 524288 | tf_op jit(solution)/shard_map/all_to_all | solution.py:363
  60.5 8.3 %copy-start.2 = (bf16[128,8,128]{2,1,0:T(8,128)(2,1)}, bf16[128,8,128]{2,1,0:T(8,128)(2,1)S(1)}, u32[]{:S(2)}) copy-start(bf16[128,8,128]{2,1,0:T(8,128)(2,1)S(1)} %all-to-all-done.1.x_ref) | copy-start | bytes 786436
  60.5 8.3 %copy-start.5 = (f32[128,128]{1,0:T(8,128)S(1)}, f32[128,128]{1,0:T(8,128)}, u32[]{:S(2)}) copy-start(f32[128,128]{1,0:T(8,128)} %get-tuple-element.44.cot_ref) | copy-start | bytes 196612
  66.1 14.4 %collective-permute-start.1 = (bf16[128,4096]{1,0:T(8,128)(2,1)S(1)}, bf16[128,4096]{1,0:T(8,128)(2,1)S(1)}, u32[]{:S(2)}, u32[]{:S(2)}) collective-permute-start(bf16[128,4096]{1,0:T(8,128)(2,1)S(1)} %get-tuple-element.46.refs_0_), channel_id=1, source_target_pairs={{0,1},{1,2},{2,3},{3,4},{4,5},{5,6},{6,7},{7,8},{8,9},{9,10},{10,1... | collective-permute-start | bytes 3145736 | tf_op jit(solution)/shard_map/ppermute | solution.py:359
  68.8 11.8 %copy-start = (bf16[1,128,4096]{2,1,0:T(8,128)(2,1)S(1)}, bf16[1,128,4096]{2,1,0:T(8,128)(2,1)}, u32[]{:S(2)}) copy-start(bf16[1,128,4096]{2,1,0:T(8,128)(2,1)} %param.10) | copy-start | bytes 3145732
  68.8 11.8 %copy-start.6 = (f32[128,128]{1,0:T(8,128)S(1)}, f32[128,128]{1,0:T(8,128)}, u32[]{:S(2)}) copy-start(f32[128,128]{1,0:T(8,128)} %get-tuple-element.47.refs_2_) | copy-start | bytes 196612
  70.8 22.9 %all-to-all-start.2 = ((bf16[128,8,128]{2,1,0:T(8,128)(2,1)}), bf16[128,8,128]{2,1,0:T(8,128)(2,1)S(1)}, u32[]{:S(2)}, u32[]{:S(2)}) async-start(bf16[128,8,128]{2,1,0:T(8,128)(2,1)} %get-tuple-element.45), calls=%async_computation.2 | async-start | bytes 524288 | tf_op jit(solution)/shard_map/all_to_all | solution.py:363
  93.8 1.3 %copy-start.3 = (bf16[128,8,128]{2,1,0:T(8,128)(2,1)}, bf16[128,8,128]{2,1,0:T(8,128)(2,1)S(1)}, u32[]{:S(2)}) copy-start(bf16[128,8,128]{2,1,0:T(8,128)(2,1)S(1)} %all-to-all-done.2.x_ref) | copy-start | bytes 786436
  95.1 23.2 %all-to-all-start.3 = ((f32[256,2,128]{2,1,0:T(2,128)}), f32[256,2,128]{2,1,0:T(2,128)S(1)}, u32[]{:S(2)}, u32[]{:S(2)}) async-start(f32[256,2,128]{2,1,0:T(2,128)} %shard_map.120), calls=%async_computation.3 | async-start | bytes 524288 | tf_op jit(solution)/shard_map/all_to_all | solution.py:363
